TPU v7x, 32 devices: a whole 2x2x4 slice. The times are simulated.
32 devices in a mesh: rows: 4 (over y, x), seq: 8 (over z, core).
Axes of the slice: x: 2, y: 2, z: 4, core: 2. Of those that a mesh axis runs over, the one named last changes fastest.
Arguments:
- tokens: bfloat16 [4, 1024, 768], P('rows', 'seq'), may hold values from -6 to 6
- doc_starts: int32 [4, 5], P('rows'), may hold values from 0 to 1023, as said below
- norm1_gain: bfloat16 [768], replicated, may hold values from 0.25 to 1.75
- norm1_bias: bfloat16 [768], replicated, may hold values from -1.75 to 1.75
- in_weight: bfloat16 [768, 2304], replicated, may hold values from -0.21875 to 0.21875
- in_bias: bfloat16 [2304], replicated, may hold values from -1.75 to 1.75
- short_weight: bfloat16 [3, 2304], replicated, may hold values from -3.5 to 3.5
- short_bias: bfloat16 [2304], replicated, may hold values from -1.75 to 1.75
- filter_first: bfloat16 [33, 64], replicated, may hold values from -1 to 1
- filter_first_bias: bfloat16 [64], replicated, may hold values from -6 to 6
- filter_second: bfloat16 [64, 64], replicated, may hold values from -0.75 to 0.75
- filter_second_bias: bfloat16 [64], replicated, may hold values from -6 to 6
- filter_third: bfloat16 [64, 64], replicated, may hold values from -0.75 to 0.75
- filter_third_bias: bfloat16 [64], replicated, may hold values from -6 to 6
- filter_last: bfloat16 [64, 768], replicated, may hold values from -0.046875 to 0.046875
- sine_freq: bfloat16 [64], replicated, may hold values from 4 to 16
- filter_bias: bfloat16 [768], replicated, may hold values from -6 to 6
- out_weight: bfloat16 [768, 768], replicated, may hold values from -0.21875 to 0.21875
- out_bias: bfloat16 [768], replicated, may hold values from -1.75 to 1.75
- norm2_gain: bfloat16 [768], replicated, may hold values from 0.25 to 1.75
- norm2_bias: bfloat16 [768], replicated, may hold values from -1.75 to 1.75
- up_weight: bfloat16 [768, 3072], replicated, may hold values from -0.21875 to 0.21875
- up_bias: bfloat16 [3072], replicated, may hold values from -1.75 to 1.75
- down_weight: bfloat16 [3072, 768], replicated, may hold values from -0.109375 to 0.109375
- down_bias: bfloat16 [768], replicated, may hold values from -1.75 to 1.75
- cotangent: bfloat16 [4, 1024, 768], P('rows', 'seq'), may hold values from -6 to 6
Outputs:
- output: bfloat16 [4, 1024, 768], P('rows', 'seq')
- grad_tokens: float32 [4, 1024, 768], P('rows', 'seq')
- grad_norm1_gain: float32 [768], replicated
- grad_norm1_bias: float32 [768], replicated
- grad_in_weight: float32 [768, 2304], P('seq')
- grad_in_bias: float32 [2304], replicated
- grad_short_weight: float32 [3, 2304], replicated
- grad_short_bias: float32 [2304], replicated
- grad_filter_first: float32 [33, 64], replicated
- grad_filter_first_bias: float32 [64], replicated
- grad_filter_second: float32 [64, 64], replicated
- grad_filter_second_bias: float32 [64], replicated
- grad_filter_third: float32 [64, 64], replicated
- grad_filter_third_bias: float32 [64], replicated
- grad_filter_last: float32 [64, 768], replicated
- grad_sine_freq: float32 [64], replicated
- grad_filter_bias: float32 [768], replicated
- grad_out_weight: float32 [768, 768], P('seq')
- grad_out_bias: float32 [768], replicated
- grad_norm2_gain: float32 [768], replicated
- grad_norm2_bias: float32 [768], replicated
- grad_up_weight: float32 [768, 3072], P('seq')
- grad_up_bias: float32 [3072], replicated
- grad_down_weight: float32 [3072, 768], P('seq')
- grad_down_bias: float32 [768], replicated
Inputs may be any that keep to these rules, and one draw needn't show every extreme that they name: `doc_starts`: each row's starts rise strictly, the first is 0 and the last is 1023; a document runs from its start to the next start or the end of the row.
All inputs are finite; a program needn't handle non-finite values.
Results may differ from a plain program's by a relative error of at most 0.0098.
The roundings to bfloat16 on the way count: a program that leaves them out, or rounds other values in their place, can miss the bound.
Values may be sent and summed in bfloat16 or wider, within the bound.
No kernel may reach another device: no remote copies, remote signals or barrier semaphores. Data moves between devices by JAX's collectives and lax.ppermute only.
A program may use at most 320 MiB of HBM per device.

v0:
```python
from functools import partial
import math

import jax
import jax.numpy as jnp
from jax import lax
from jax.sharding import PartitionSpec as P

EPSILON = 1e-05
HIGHEST = lax.Precision.HIGHEST
MIN_DECAY = math.log(100.0) / 1.5
MAX_DECAY = math.log(100.0) / 0.3


def passed_along(block, axis, distance):
    devices = range(lax.axis_size(axis))
    route = [(i - distance, i) for i in devices if i - distance in devices]
    return lax.ppermute(block, axis, route)


def layer_norm(values, gain, shift):
    average = jnp.mean(values, axis=-1, keepdims=True)
    centred = values - average
    spread = jnp.mean(centred * centred, axis=-1, keepdims=True)
    return centred * lax.rsqrt(spread + EPSILON) * gain + shift


def filter_taps(first, first_bias, second, second_bias, third, third_bias, last, sine_freq, length):
    lags = jnp.arange(length)
    bands = (first.shape[0] - 1) // 2
    moment = lags.astype(jnp.float32) / (length - 1)
    band_freq = jnp.linspace(0.0001, bands - 1, bands, dtype=jnp.float32)
    phase = 2.0 * math.pi / length * lags.astype(jnp.float32)
    angles = phase[:, None] * band_freq[None, :]
    features = jnp.concatenate([moment[:, None], jnp.cos(angles), -jnp.sin(angles)], axis=1)
    hidden = jnp.sin(sine_freq * (jnp.dot(features, first, precision=HIGHEST) + first_bias))
    hidden = jnp.sin(sine_freq * (jnp.dot(hidden, second, precision=HIGHEST) + second_bias))
    hidden = jnp.sin(sine_freq * (jnp.dot(hidden, third, precision=HIGHEST) + third_bias))
    rates = jnp.linspace(MIN_DECAY, MAX_DECAY, last.shape[1], dtype=jnp.float32)
    window = jnp.exp(-moment[:, None] * rates[None, :])
    return jnp.dot(hidden, last, precision=HIGHEST) * window


def doc_ids_of(starts, positions):
    return jnp.sum((positions[:, None] >= starts[None, :]).astype(jnp.int32), axis=1) - 1


def short_conv_local(proj, rim, weight, bias, ids, rim_ids):
    block_rows = proj.shape[0]
    rim_width = rim.shape[0]
    extended = jnp.concatenate([rim, proj], axis=0)
    extended_ids = jnp.concatenate([rim_ids, ids], axis=0)
    total = bias + jnp.zeros_like(proj)
    for offset in range(weight.shape[0]):
        begin = rim_width - offset
        moved = extended[begin : begin + block_rows]
        same = (extended_ids[begin : begin + block_rows] == ids).astype(jnp.float32)[:, None]
        total = total + weight[offset] * moved * same
    return total


def dft_tables(block_rows):
    period = 2 * block_rows
    packed = jnp.arange(period)
    freq_of = jnp.where(
        packed < block_rows,
        packed,
        jnp.where(packed == block_rows, block_rows, packed - block_rows),
    )
    places = jnp.arange(period)
    phase = freq_of[:, None] * places[None, :] % period
    angle = 2.0 * math.pi / period * phase.astype(jnp.float32)
    forward_table = jnp.where((packed <= block_rows)[:, None], jnp.cos(angle), -jnp.sin(angle))
    later = jnp.arange(block_rows) + block_rows
    phase_back = later[:, None] * freq_of[None, :] % period
    angle_back = 2.0 * math.pi / period * phase_back.astype(jnp.float32)
    scaling = jnp.where((packed == 0) | (packed == block_rows), 1.0, 2.0) / period
    inverse_table = (
        jnp.where((packed <= block_rows)[None, :], jnp.cos(angle_back), -jnp.sin(angle_back))
        * scaling[None, :]
    )
    edge = (jnp.arange(block_rows) >= 1).astype(jnp.float32)[:, None]
    return (forward_table, inverse_table, edge)


def spectral_product(left_spec, right_spec, edge):
    half = left_spec.shape[0] // 2
    left_re, left_im = (left_spec[:half], left_spec[half:])
    right_re, right_im = (right_spec[:half], right_spec[half:])
    real_part = left_re * right_re - edge * left_im * right_im
    imag_part = edge * (left_re * right_im + left_im * right_re) + (1.0 - edge) * left_im * right_im
    return jnp.concatenate([real_part, imag_part], axis=0)


def product_adjoint(left_spec, grad_spec, edge):
    half = left_spec.shape[0] // 2
    left_re, left_im = (left_spec[:half], left_spec[half:])
    grad_re, grad_im = (grad_spec[:half], grad_spec[half:])
    other_re = grad_re * left_re + edge * grad_im * left_im
    other_im = (
        -edge * grad_re * left_im + edge * grad_im * left_re + (1.0 - edge) * grad_im * left_im
    )
    return jnp.concatenate([other_re, other_im], axis=0)


def self_conv(head, signal, ids, ndocs, forward_table, inverse_table, edge):
    block_rows = signal.shape[0]
    head_spec = jnp.dot(forward_table[:, block_rows:], head, precision=HIGHEST)
    total = jnp.zeros_like(signal)
    for document in range(ndocs):
        member = (ids == document).astype(jnp.float32)[:, None]
        signal_spec = jnp.dot(forward_table[:, :block_rows], signal * member, precision=HIGHEST)
        joined = spectral_product(head_spec, signal_spec, edge)
        total = total + member * jnp.dot(inverse_table, joined, precision=HIGHEST)
    return total


def lag_spectra(taps, block_rows, forward_table):
    count = taps.shape[0] // block_rows
    tap_blocks = taps.reshape(count, block_rows, taps.shape[1])
    windows = jnp.concatenate([tap_blocks[:-1], tap_blocks[1:]], axis=1)
    return jnp.einsum("fp,kpc->kfc", forward_table, windows, precision=HIGHEST)


def fold_blocks(block_fn, absorb, piece, block_rows, init):
    count = piece.shape[0] // block_rows
    group = math.gcd(count, 8)
    stacked = piece.reshape(count // group, group, block_rows, piece.shape[1])

    def advance(total, inputs):
        blocks, turn = inputs
        sources = turn * group + jnp.arange(group)
        results = jax.vmap(block_fn)(blocks, sources)
        return (absorb(total, results, sources), None)

    total, unused = lax.scan(advance, init, (stacked, jnp.arange(count // group)))
    return total


def local(
    tokens,
    doc_starts,
    norm1_gain,
    norm1_bias,
    in_weight,
    in_bias,
    short_weight,
    short_bias,
    filter_first,
    filter_first_bias,
    filter_second,
    filter_second_bias,
    filter_third,
    filter_third_bias,
    filter_last,
    sine_freq,
    filter_bias,
    out_weight,
    out_bias,
    norm2_gain,
    norm2_bias,
    up_weight,
    up_bias,
    down_weight,
    down_bias,
    cotangent,
):
    f32 = jnp.float32
    bf16 = jnp.bfloat16
    block_rows = tokens.shape[1]
    width = tokens.shape[2]
    seq_len = block_rows * lax.axis_size("seq")
    index = lax.axis_index("seq")
    anchor = index * block_rows
    starts = doc_starts[0]
    ndocs = starts.shape[0]
    ids = doc_ids_of(starts, anchor + jnp.arange(block_rows))
    rim_width = short_weight.shape[0] - 1
    rim_ids = doc_ids_of(starts, anchor - rim_width + jnp.arange(rim_width))
    first_start = jnp.max(jnp.where(starts <= anchor, starts, 0))
    row_mask = (ids == ids[0]).astype(f32)[:, None]
    forward_table, inverse_table, edge = dft_tables(block_rows)
    inputs = tokens[0].astype(f32)
    normed1, norm1_pull = jax.vjp(
        layer_norm, inputs, norm1_gain.astype(f32), norm1_bias.astype(f32)
    )
    normed1_low = normed1.astype(bf16)
    proj = jnp.dot(normed1_low, in_weight, preferred_element_type=f32) + in_bias.astype(f32)
    rim = passed_along(proj[block_rows - rim_width :], "seq", 1)

    def short_fn(proj_part, rim_part, weight_part, bias_part):
        return short_conv_local(proj_part, rim_part, weight_part, bias_part, ids, rim_ids)

    mixed, short_pull = jax.vjp(
        short_fn, proj, rim, short_weight.astype(f32), short_bias.astype(f32)
    )
    gate_out = mixed[:, :width]
    gate_in = mixed[:, width : 2 * width]
    values = mixed[:, 2 * width :]
    carried = (values * gate_in).astype(bf16)
    carried_wide = carried.astype(f32)
    filter_params = (
        filter_first.astype(f32),
        filter_first_bias.astype(f32),
        filter_second.astype(f32),
        filter_second_bias.astype(f32),
        filter_third.astype(f32),
        filter_third_bias.astype(f32),
        filter_last.astype(f32),
        sine_freq.astype(f32),
    )
    taps, taps_pull = jax.vjp(partial(filter_taps, length=seq_len), *filter_params)

    def pair_setup(source):
        lag_block = index - source
        valid = (lag_block >= 1) & ((source + 1) * block_rows > first_start)
        lag_slot = jnp.maximum(lag_block, 1) - 1
        column = (source * block_rows + jnp.arange(block_rows) >= first_start).astype(f32)[:, None]
        return (valid, lag_slot, column)

    lag_specs = lag_spectra(taps, block_rows, forward_table)

    def self_fn(head, signal):
        return self_conv(head, signal, ids, ndocs, forward_table, inverse_table, edge)

    self_out, self_pull = jax.vjp(self_fn, taps[:block_rows], carried_wide)

    def forward_block(block, source):
        valid, lag_slot, column = pair_setup(source)
        taps_spec = lax.dynamic_index_in_dim(lag_specs, lag_slot, 0, keepdims=False)
        signal_spec = jnp.dot(
            forward_table[:, :block_rows], block.astype(f32) * column, precision=HIGHEST
        )
        return jnp.where(valid, spectral_product(taps_spec, signal_spec, edge), 0.0)

    def add_spectra(total, results, sources):
        return total + jnp.sum(results, axis=0)

    zero_spec = jnp.zeros((2 * block_rows, width), f32)
    cross_spec = fold_blocks(
        forward_block,
        add_spectra,
        lax.all_gather(carried, "seq", axis=0, tiled=True),
        block_rows,
        zero_spec,
    )
    conv_out = row_mask * jnp.dot(inverse_table, cross_spec, precision=HIGHEST) + self_out
    filter_bias_wide = filter_bias.astype(f32)
    long_out = conv_out + filter_bias_wide * carried_wide
    gated_low = (long_out * gate_out).astype(bf16)
    resid = (
        inputs + jnp.dot(gated_low, out_weight, preferred_element_type=f32) + out_bias.astype(f32)
    )
    normed2, norm2_pull = jax.vjp(layer_norm, resid, norm2_gain.astype(f32), norm2_bias.astype(f32))
    normed2_low = normed2.astype(bf16)
    pre = jnp.dot(normed2_low, up_weight, preferred_element_type=f32) + up_bias.astype(f32)
    active, gelu_pull = jax.vjp(partial(jax.nn.gelu, approximate=True), pre)
    active_low = active.astype(bf16)
    output = (
        resid + jnp.dot(active_low, down_weight, preferred_element_type=f32) + down_bias.astype(f32)
    ).astype(bf16)
    grad_top_low = cotangent[0]
    grad_top = grad_top_low.astype(f32)
    grad_down = jnp.dot(active_low.T, grad_top_low, preferred_element_type=f32)
    grad_down_bias = jnp.sum(grad_top, axis=0)
    grad_active = jnp.dot(grad_top_low, down_weight.T, preferred_element_type=f32)
    grad_pre_low = gelu_pull(grad_active)[0].astype(bf16)
    grad_up = jnp.dot(normed2_low.T, grad_pre_low, preferred_element_type=f32)
    grad_up_bias = jnp.sum(grad_pre_low.astype(f32), axis=0)
    grad_normed2 = jnp.dot(grad_pre_low, up_weight.T, preferred_element_type=f32)
    resid_part, grad_gain2, grad_shift2 = norm2_pull(grad_normed2)
    grad_resid = grad_top + resid_part
    grad_mixer_low = grad_resid.astype(bf16)
    grad_out_weight = jnp.dot(gated_low.T, grad_mixer_low, preferred_element_type=f32)
    grad_out_bias = jnp.sum(grad_mixer_low.astype(f32), axis=0)
    grad_gated = jnp.dot(grad_mixer_low, out_weight.T, preferred_element_type=f32)
    grad_long = grad_gated * gate_out
    grad_gate_out = grad_gated * long_out
    grad_filter_bias = jnp.sum(grad_long * carried_wide, axis=0)
    grad_head, grad_signal_self = self_pull(grad_long)
    grad_spec = jnp.dot(inverse_table.T, row_mask * grad_long, precision=HIGHEST)

    def return_block(source):
        valid, lag_slot, column = pair_setup(source)
        taps_spec = lax.dynamic_index_in_dim(lag_specs, lag_slot, 0, keepdims=False)
        signal_grad_spec = product_adjoint(taps_spec, grad_spec, edge)
        signal_grad = jnp.dot(forward_table[:, :block_rows].T, signal_grad_spec, precision=HIGHEST)
        return jnp.where(valid, signal_grad * column, 0.0)

    number = block_rows * lax.axis_size("seq") // block_rows
    group = math.gcd(number, 8)
    sources = jnp.arange(number).reshape(number // group, group)
    stacked = lax.map(jax.vmap(return_block), sources)
    grad_signal_cross = lax.psum_scatter(
        stacked.reshape(block_rows * lax.axis_size("seq"), width),
        "seq",
        scatter_dimension=0,
        tiled=True,
    )

    def tap_block(block, source):
        valid, lag_slot, column = pair_setup(source)
        signal_spec = jnp.dot(
            forward_table[:, :block_rows], block.astype(f32) * column, precision=HIGHEST
        )
        taps_grad_spec = product_adjoint(signal_spec, grad_spec, edge)
        taps_grad = jnp.dot(forward_table.T, taps_grad_spec, precision=HIGHEST)
        return jnp.where(valid, taps_grad, 0.0)

    def add_taps(total, results, sources):
        for member in range(results.shape[0]):
            offset = (jnp.maximum(index - sources[member], 1) - 1) * block_rows
            current = lax.dynamic_slice_in_dim(total, offset, 2 * block_rows, 0)
            total = lax.dynamic_update_slice_in_dim(total, current + results[member], offset, 0)
        return total

    zero_taps = jnp.zeros((seq_len, width), f32)
    taps_grad_all = fold_blocks(
        tap_block,
        add_taps,
        lax.all_gather(carried, "seq", axis=0, tiled=True),
        block_rows,
        zero_taps,
    )
    taps_grad_all = taps_grad_all + jnp.pad(grad_head, ((0, seq_len - block_rows), (0, 0)))
    grad_signal_conv = grad_signal_self + grad_signal_cross
    filter_grads = taps_pull(taps_grad_all)
    grad_carried = grad_signal_conv + filter_bias_wide * grad_long
    grad_mixed = jnp.concatenate(
        [grad_gate_out, grad_carried * values, grad_carried * gate_in], axis=1
    )
    grad_proj, grad_rim, grad_short_weight, grad_short_bias = short_pull(grad_mixed)
    rim_back = passed_along(grad_rim, "seq", -1)
    grad_proj = grad_proj + jnp.pad(rim_back, ((block_rows - rim_width, 0), (0, 0)))
    grad_proj_low = grad_proj.astype(bf16)
    grad_in_weight = jnp.dot(normed1_low.T, grad_proj_low, preferred_element_type=f32)
    grad_in_bias = jnp.sum(grad_proj_low.astype(f32), axis=0)
    grad_normed1 = jnp.dot(grad_proj_low, in_weight.T, preferred_element_type=f32)
    inputs_part, grad_gain1, grad_shift1 = norm1_pull(grad_normed1)
    grad_inputs = grad_resid + inputs_part
    matrix_shards = (
        lax.psum_scatter(grad_in_weight, "seq", scatter_dimension=0, tiled=True),
        lax.psum_scatter(grad_out_weight, "seq", scatter_dimension=0, tiled=True),
        lax.psum_scatter(grad_up, "seq", scatter_dimension=0, tiled=True),
        lax.psum_scatter(grad_down, "seq", scatter_dimension=0, tiled=True),
    )
    matrix_sums = lax.psum(
        (matrix_shards[0], matrix_shards[1], matrix_shards[2], matrix_shards[3]), "rows"
    )
    small_sums = lax.psum(
        (
            grad_gain1,
            grad_shift1,
            grad_in_bias,
            grad_short_weight,
            grad_short_bias,
            filter_grads[0],
            filter_grads[1],
            filter_grads[2],
            filter_grads[3],
            filter_grads[4],
            filter_grads[5],
            filter_grads[6],
            filter_grads[7],
            grad_filter_bias,
            grad_out_bias,
            grad_gain2,
            grad_shift2,
            grad_up_bias,
            grad_down_bias,
        ),
        ("rows", "seq"),
    )
    return (
        output[None],
        grad_inputs[None],
        small_sums[0],
        small_sums[1],
        matrix_sums[0],
        small_sums[2],
        small_sums[3],
        small_sums[4],
        small_sums[5],
        small_sums[6],
        small_sums[7],
        small_sums[8],
        small_sums[9],
        small_sums[10],
        small_sums[11],
        small_sums[12],
        small_sums[13],
        matrix_sums[1],
        small_sums[14],
        small_sums[15],
        small_sums[16],
        matrix_sums[2],
        small_sums[17],
        matrix_sums[3],
        small_sums[18],
    )


def solution(mesh):
    placed = (
        P("rows", "seq", None),
        P("rows", None),
        P(),
        P(),
        P(),
        P(),
        P(),
        P(),
        P(),
        P(),
        P(),
        P(),
        P(),
        P(),
        P(),
        P(),
        P(),
        P(),
        P(),
        P(),
        P(),
        P(),
        P(),
        P(),
        P(),
        P("rows", "seq", None),
    )
    return jax.shard_map(
        local,
        mesh=mesh,
        in_specs=placed,
        out_specs=(
            P("rows", "seq", None),
            P("rows", "seq", None),
            P(),
            P(),
            P("seq", None),
            P(),
            P(),
            P(),
            P(),
            P(),
            P(),
            P(),
            P(),
            P(),
            P(),
            P(),
            P(),
            P("seq", None),
            P(),
            P(),
            P(),
            P("seq", None),
            P(),
            P("seq", None),
            P(),
        ),
        check_vma=False,
    )
```

profile of v0, /device:TPU:0, one launch (start us, length us, event | category | flops | bytes accessed | tf_op | source)
XLA Modules:
  0.0 943.9 jit_solution(5307605170441919123)
XLA Ops:
  14.9 3.0 collective-permute-start
  41.4 3.5 fusion.15
  53.0 3.8 copy.61
  56.8 3.3 copy.62
  62.8 10.6 %fusion.18 = f32[7,256,768]{1,2,0:T(8,128)} fusion(f32[7,128,768]{1,2,0:T(8,128)} %copy.62, f32[7,128,768]{1,2,0:T(8,128)} %copy.61, s32[256]{0:T(256)S(1)} %compare_select_fusion, pred[256]{0:T(512)(128)(4,1)S(1)} %iota_compare_fusion.1), kind=kOutput, calls=%fused_computation.33 | convolution fusion | flops 4230283264 | bytes 11011328 | tf_op jit(solution)/shard_map/fp,kpc->kfc/dot_general | solution.py:122
  74.6 6.3 copy.63
  86.0 6.3 gather_fusion
  92.3 3.0 multiply_add_fusion.5
  114.5 9.7 %all-gather.2.cloned.1.call-done = bf16[1024,768]{1,0:T(8,128)(2,1)} async-done(((bf16[128,768]{1,0:T(8,128)(2,1)}), bf16[1024,768]{1,0:T(8,128)(2,1)}) %all-gather.2.cloned.1.call-update) | async-done | bytes 1572880 | tf_op jit(solution)/shard_map/all_gather | solution.py:243
  124.2 7.3 fusion.13
  131.6 3.5 multiply_subtract_fusion
  140.2 5.6 convert_reduce_fusion
  153.4 3.5 multiply_add_fusion.3
  156.9 5.0 fusion.14
  162.0 2.9 fusion.320
  165.1 6.5 fusion.310
  171.6 6.6 fusion.170
  181.4 2.8 multiply_add_fusion.15
  198.7 3.4 reduce-scatter.6.cloned.1.call-done
  212.7 4.1 fusion.306
  222.8 3.0 fusion.86
  226.0 9.4 select_bitcast_fusion
  237.3 2.9 fusion.54
  248.2 4.0 fusion.21
  255.8 3.1 fusion.312
  261.4 79.4 %reduce-scatter.12.cloned.1.call-done = f32[96,3072]{1,0:T(8,128)} async-done(((f32[768,3072]{1,0:T(8,128)}), f32[96,3072]{1,0:T(8,128)}) %reduce-scatter.12.cloned.1.call-update) | async-done | bytes 1179664 | tf_op jit(solution)/shard_map/reduce_scatter | solution.py:344
  340.8 100.0 %reduce-scatter.14.cloned.1.call-done = f32[384,768]{1,0:T(8,128)} async-done(((f32[3072,768]{1,0:T(8,128)}), f32[384,768]{1,0:T(8,128)}) %reduce-scatter.14.cloned.1.call-update) | async-done | bytes 1179664 | tf_op jit(solution)/shard_map/reduce_scatter | solution.py:345
  440.9 77.8 %reduce-scatter.8.cloned.1.call-done = f32[96,2304]{1,0:T(8,128)} async-done(((f32[768,2304]{1,0:T(8,128)}), f32[96,2304]{1,0:T(8,128)}) %reduce-scatter.8.cloned.1.call-update) | async-done | bytes 884752 | tf_op jit(solution)/shard_map/reduce_scatter | solution.py:342
  518.7 4.6 fusion.55
  523.3 122.9 %all-reduce.35.cloned.1.call-done = f32[64,768]{1,0:T(8,128)} async-done(((f32[64,768]{1,0:T(8,128)}), f32[64,768]{1,0:T(8,128)}) %all-reduce.35.cloned.1.call-update) | async-done | bytes 196624 | tf_op jit(solution)/shard_map/psum | solution.py:350
  646.2 162.4 %all-reduce.37.cloned.1.call-done = (f32[768]{0:T(1024)}, f32[768]{0:T(1024)}, f32[2304]{0:T(1024)}, f32[3,2304]{1,0:T(4,128)}, f32[2304]{0:T(1024)}, /*index=5*...) async-done(((f32[768]{0:T(1024)}, f32[768]{0:T(1024)}, ...) | async-done | bytes 122128 | tf_op jit(solution)/shard_map/psum | solution.py:350
  808.6 99.4 %all-reduce.39.cloned.1.call-done = (f32[96,2304]{1,0:T(8,128)}, f32[96,768]{1,0:T(8,128)}, f32[96,3072]{1,0:T(8,128)}, f32[384,768]{1,0:T(8,128)}) async-done(((f32[96,2304]{1,0:T(8,128)}, f32[96,768]{1,0:T(8,128)}, f32[96,3072]{1,0:T(8,128)}, f32[384,768]{1,0:T(8,128)}), (f32[96,2304]{1,0:T(8,128)}, f32[96,768]{1,0:T(8,128)}, f32[96,3072]{1,0:T(8,128)}, ...) | async-done | bytes 3538960 | tf_op jit(solution)/shard_map/psum | solution.py:347
  (432 shorter events, 153.0 us)
Async XLA Ops:
  7.2 117.0 %all-gather.2.cloned.1.call-start = ((), (), s32[]{:S(2)}) async-start(), calls=%async_computation.5 | async-start | bytes 1769472 | tf_op jit(solution)/shard_map/all_gather | solution.py:243
  8.5 9.5 %copy-start.86 = (f32[128]{0:T(128)}, f32[128]{0:T(128)S(1)}, u32[]{:S(2)}) copy-start(f32[128]{0:T(128)S(1)} %broadcast_multiply_fusion.5) | copy-start | bytes 1540
  9.6 8.3 copy-start.102
  14.9 77.3 %collective-permute-start = (f32[2,2304]{1,0:T(2,128)}, f32[2,2304]{1,0:T(2,128)}, u32[]{:S(2)}, u32[]{:S(2)}) collective-permute-start(f32[2,2304]{1,0:T(2,128)} %slice.297), channel_id=1, source_target_pairs={{0,1},{1,2},{2,3},{3,4},{4,5},{5,6},{6,7},{8,9},{9,10},{10,11},{11... | collective-permute-start | bytes 55304 | tf_op jit(solution)/shard_map/ppermute | solution.py:18
  17.9 44.9 %copy-start.62 = (pred[256]{0:T(512)(128)(4,1)}, pred[256]{0:T(512)(128)(4,1)S(1)}, u32[]{:S(2)}) copy-start(pred[256]{0:T(512)(128)(4,1)S(1)} %iota_compare_fusion.1) | copy-start | bytes 772
  30.5 10.1 %copy-start.79 = (f32[64]{0:T(128)}, f32[64]{0:T(128)S(1)}, u32[]{:S(2)}) copy-start(f32[64]{0:T(128)S(1)} %convert_element_type.340) | copy-start | bytes 772
  62.8 11.1 %copy-start.108 = (bf16[2304]{0:T(1024)(128)(2,1)S(1)}, bf16[2304]{0:T(1024)(128)(2,1)}, u32[]{:S(2)}) copy-start(bf16[2304]{0:T(1024)(128)(2,1)} %param.33) | copy-start | bytes 13828
  97.0 105.0 %reduce-scatter.6.cloned.1.call-start = ((), (), s32[]{:S(2)}) async-start(), calls=%async_computation.6 | async-start | bytes 3538944 | tf_op jit(solution)/shard_map/reduce_scatter | solution.py:294
  124.2 7.3 copy-start.77
  138.9 9.1 copy-start.11
  138.9 9.1 copy-start.89
  139.2 8.9 copy-start.105
  140.2 13.2 %slice-start = ((s8[6291456]{0:T(1024)(128)(4,1)}), s8[4194304]{0:T(1024)(128)(4,1)S(1)}, s32[]{:S(2)}) async-start(s8[6291456]{0:T(1024)(128)(4,1)} %bitcast.182), calls=%async_computation.14 | async-start | bytes 8388608
  145.7 7.7 slice-start.1
  162.0 99.4 %reduce-scatter.10.cloned.1.call-start = ((), (), s32[]{:S(2)}) async-start(), calls=%async_computation.9 | async-start | bytes 2654208 | tf_op jit(solution)/shard_map/reduce_scatter | solution.py:343
  165.0 175.8 %reduce-scatter.12.cloned.1.call-start = ((), (), s32[]{:S(2)}) async-start(), calls=%async_computation.10 | async-start | bytes 10616832 | tf_op jit(solution)/shard_map/reduce_scatter | solution.py:344
  171.5 269.3 %reduce-scatter.14.cloned.1.call-start = ((), (), s32[]{:S(2)}) async-start(), calls=%async_computation.11 | async-start | bytes 10616832 | tf_op jit(solution)/shard_map/reduce_scatter | solution.py:345
  178.2 340.5 %reduce-scatter.8.cloned.1.call-start = ((), (), s32[]{:S(2)}) async-start(), calls=%async_computation.7 | async-start | bytes 7962624 | tf_op jit(solution)/shard_map/reduce_scatter | solution.py:342
  207.9 3.2 collective-permute-start.1
  216.9 9.0 copy-start.66
  216.9 9.0 copy-start.113
  216.9 429.3 %all-reduce.35.cloned.1.call-start = ((), (), s32[]{:S(2)}) async-start(), calls=%async_computation.8 | async-start | bytes 393216 | tf_op jit(solution)/shard_map/psum | solution.py:350
  243.4 11.8 %copy-start.82 = (f32[2304]{0:T(1024)S(1)}, f32[2304]{0:T(1024)}, u32[]{:S(2)}) copy-start(f32[2304]{0:T(1024)} %get-tuple-element.105) | copy-start | bytes 27652
  252.3 556.3 %all-reduce.37.cloned.1.call-start = ((), (), s32[]{:S(2)}) async-start(), calls=%async_computation.12 | async-start | bytes 380928 | tf_op jit(solution)/shard_map/psum | solution.py:350
  252.4 7.4 copy-start.38
  252.4 7.3 copy-start.43
  258.9 259.8 %copy-start.116 = (bf16[768]{0:T(1024)(128)(2,1)S(1)}, bf16[768]{0:T(1024)(128)(2,1)}, u32[]{:S(2)}) copy-start(bf16[768]{0:T(1024)(128)(2,1)} %param.50) | copy-start | bytes 4612
  261.4 646.7 %all-reduce.39.cloned.1.call-start = ((), (), s32[]{:S(2)}) async-start(), calls=%async_computation.13 | async-start | bytes 7077888 | tf_op jit(solution)/shard_map/psum | solution.py:347
  808.6 126.3 %copy-start.106 = (f32[3072]{0:T(1024)S(1)}, f32[3072]{0:T(1024)}, u32[]{:S(2)}) copy-start(f32[3072]{0:T(1024)} %get-tuple-element.275) | copy-start | bytes 36868
  908.0 25.9 %copy-start.50 = (f32[96,3072]{1,0:T(8,128)S(1)}, f32[96,3072]{1,0:T(8,128)}, u32[]{:S(2)}) copy-start(f32[96,3072]{1,0:T(8,128)} %get-tuple-element.274) | copy-start | bytes 3538948
  908.0 27.5 %copy-start.49 = (f32[384,768]{1,0:T(8,128)S(1)}, f32[384,768]{1,0:T(8,128)}, u32[]{:S(2)}) copy-start(f32[384,768]{1,0:T(8,128)} %get-tuple-element.276) | copy-start | bytes 3538948
  912.9 23.7 %copy-start.114 = (f32[768]{0:T(1024)S(1)}, f32[768]{0:T(1024)}, u32[]{:S(2)}) copy-start(f32[768]{0:T(1024)} %get-tuple-element.277) | copy-start | bytes 9220
  (107 other events, 400.4 us)
Sparse Core Ops, SparseCore 0:
  97.1 27.0 all-gather.1
  162.1 39.9 reduce-scatter.5
  204.4 35.3 reduce-scatter.9
  241.9 98.8 reduce-scatter.11
  343.0 97.8 reduce-scatter.13
  443.1 75.5 reduce-scatter.7
  524.8 121.3 all-reduce.34
  654.9 153.6 all-reduce.36
  812.1 95.9 all-reduce.38
where the time goes:
time: 953 us; the launch traced here: 944 us
  waiting for transfers between devices  657 us (69%)
  matrix products  131 us (14%)
  other arithmetic  66.5 us (7%)
  local copies, waits for them, and re-layouts  63.2 us (7%)
  between operations  21.2 us (2%)
    psum x2, waiting for transfers between devices, local(): lax.psum((grad_gain1, grad_shift1, grad_in_bias, grad_short_weight, grad_...  285 us
    reduce_scatter x1, waiting for transfers between devices, local(): lax.psum_scatter(grad_down, 'seq', scatter_dimension=0, tiled=True)  100 us
    psum x1, waiting for transfers between devices, local(): lax.psum((matrix_shards[0], matrix_shards[1], matrix_shards[2], matrix_sh...  99.4 us
    reduce_scatter x1, waiting for transfers between devices, local(): lax.psum_scatter(grad_up, 'seq', scatter_dimension=0, tiled=True)  79.4 us
    reduce_scatter x1, waiting for transfers between devices, local(): lax.psum_scatter(grad_in_weight, 'seq', scatter_dimension=0, tiled=True)  77.8 us
    unnamed x279, local copies, waits for them, and re-layouts  37.1 us
  transfers between devices with their start and end apart: 11, of which 9 were waited for; matrix products, arithmetic and copies ran while one was open for 19% of the time, Pallas kernels for 0%

commit v1 on v0

v1 whole, which is shorter than its diff:
```python
from functools import partial
import math

import jax
import jax.numpy as jnp
import numpy as np
from jax import lax
from jax.experimental import pallas as pl
from jax.experimental.pallas import tpu as pltpu
from jax.sharding import PartitionSpec as P

EPSILON = 1e-05
HIGHEST = lax.Precision.HIGHEST
MIN_DECAY = math.log(100.0) / 1.5
MAX_DECAY = math.log(100.0) / 0.3
F32 = jnp.float32
BF16 = jnp.bfloat16
RIM = 16
VMEM_LIMIT = 58 * 1024 * 1024
GELU_C = math.sqrt(2.0 / math.pi)
GELU_A = 0.044715


def params():
    return pltpu.CompilerParams(vmem_limit_bytes=VMEM_LIMIT)


def smem():
    return pl.BlockSpec(memory_space=pltpu.SMEM)


def whole(shape):
    return pl.BlockSpec(shape, lambda *_: (0,) * len(shape))


def dot(left, right):
    return jnp.dot(left, right, preferred_element_type=F32)


def dot_t(left, right):
    return lax.dot_general(left, right, (((1,), (1,)), ((), ())), preferred_element_type=F32)


def high_low(values):
    high = values.astype(BF16)
    return high, (values - high.astype(F32)).astype(BF16)


def doc_at(meta, ndocs, position):
    total = jnp.int32(-1)
    for d in range(ndocs):
        total = total + (position >= meta[4 + d]).astype(jnp.int32)
    return total


def doc_start(meta, ndocs, position):
    found = jnp.int32(0)
    for d in range(ndocs):
        found = jnp.where(position >= meta[4 + d], meta[4 + d], found)
    return found


def doc_end(meta, ndocs, position, length):
    found = jnp.int32(length)
    for d in reversed(range(ndocs)):
        found = jnp.where(position < meta[4 + d], meta[4 + d], found)
    return found


def doc_column(meta, ndocs, first, rows):
    position = first + lax.broadcasted_iota(jnp.int32, (rows, 1), 0)
    total = jnp.full((rows, 1), -1, jnp.int32)
    for d in range(ndocs):
        total = total + (position >= meta[4 + d]).astype(jnp.int32)
    return position, total


def block_tables(block):
    period = 2 * block
    packed = np.arange(period)
    freq = np.where(packed <= block, packed, packed - block)
    places = np.arange(period)
    angle = 2.0 * np.pi / period * (freq[:, None] * places[None, :] % period)
    real = (packed <= block)[:, None]
    forward = np.where(real, np.cos(angle), -np.sin(angle))
    scaling = np.where((packed == 0) | (packed == block), 1.0, 2.0) / period
    inverse = (forward * scaling[:, None]).T[block:]
    left = forward[:, :block]

    def split(table):
        table = table.astype(np.float32)
        high = table.astype(BF16)
        return high, (table - high.astype(np.float32)).astype(BF16)

    lh, ll = split(left)
    ih, il = split(inverse)
    return dict(
        left2=np.concatenate([lh, ll], 1),
        left3=np.concatenate([lh, lh, ll], 1),
        inv3=np.concatenate([ih, ih, il], 1),
        invt2=np.concatenate([ih.T, il.T], 1),
        leftt3=np.concatenate([lh.T, lh.T, ll.T], 1),
    )


def spectrum2(table, signal):
    return dot(table, jnp.concatenate([signal, signal], axis=0))


def spectrum3(table, values):
    high, low = high_low(values)
    return dot(table, jnp.concatenate([high, low, high], axis=0))


def masked(signal, mask):
    return jnp.where(mask, signal.astype(F32), 0.0).astype(BF16)


def first_row(shape):
    return lax.broadcasted_iota(jnp.int32, shape, 0) == 0


def times(left, right):
    half = left.shape[0] // 2
    lre, lim = left[:half], left[half:]
    rre, rim = right[:half], right[half:]
    row = first_row(lre.shape)
    edge = jnp.where(row, 0.0, lim)
    return lre * rre - edge * rim, edge * rre + jnp.where(row, lim, lre) * rim


def times_back(left, grad):
    half = left.shape[0] // 2
    lre, lim = left[:half], left[half:]
    gre, gim = grad[:half], grad[half:]
    row = first_row(lre.shape)
    edge = jnp.where(row, 0.0, lim)
    return lre * gre + edge * gim, jnp.where(row, lim, lre) * gim - edge * gre


def add_spec(acc, pair):
    half = acc.shape[0] // 2
    acc[:half, :] += pair[0]
    acc[half:, :] += pair[1]


def set_spec(acc, pair):
    half = acc.shape[0] // 2
    acc[:half, :] = pair[0]
    acc[half:, :] = pair[1]


def normalise(values):
    average = jnp.mean(values, axis=-1, keepdims=True)
    centred = values - average
    spread = jnp.mean(centred * centred, axis=-1, keepdims=True)
    rstd = lax.rsqrt(spread + EPSILON)
    return centred * rstd, rstd


def front_kernel(ndocs, meta, tokens, rim, gain, bias, weight, wbias, taps, tbias,
                 proj_ref, normt_ref, mixed_ref, carried_ref):
    block, width = tokens.shape
    taps_n = taps.shape[0]
    ext = jnp.concatenate([rim[...], tokens[...]], axis=0).astype(F32)
    hat, _ = normalise(ext)
    normed = hat * gain[...].astype(F32) + bias[...].astype(F32)
    normt_ref[...] = normed[RIM:].T.astype(BF16)
    low = normed.astype(BF16)
    base = meta[0] * block
    position, ids = doc_column(meta, ndocs, base, block)
    masks = []
    for k in range(taps_n):
        _, back = doc_column(meta, ndocs, base - k, block)
        masks.append(((back == ids) & (position >= k)).astype(F32))
    for third in range(3):
        cols = slice(third * width, (third + 1) * width)
        proj_ref[:, cols] = dot(low, weight[:, cols]) + wbias[:, cols].astype(F32)
        total = tbias[:, cols].astype(F32)
        for k in range(taps_n):
            moved = proj_ref[pl.ds(RIM - k, block), cols]
            total = total + taps[k : k + 1, cols].astype(F32) * moved * masks[k]
        mixed_ref[:, cols] = total
    carried_ref[...] = (mixed_ref[:, 2 * width :] * mixed_ref[:, width : 2 * width]).astype(BF16)


def lag_kernel(taps, left3, out):
    blocks = taps.shape[0]
    sign = 1.0 - 2.0 * (lax.broadcasted_iota(jnp.int32, (out.shape[1], 1), 0) % 2).astype(F32)

    def step(j, carry):
        spec = spectrum3(left3[...], taps[j])
        out[j] = out[j] + sign * spec

        @pl.when(j + 1 < blocks)
        def _():
            out[j + 1] = spec

        return carry

    out[0] = jnp.zeros(out.shape[1:], F32)
    lax.fori_loop(0, blocks, step, 0)


def conv_kernel(ndocs, length, meta, signal, lags, left2, inv3, out, acc):
    block = signal.shape[1]
    me = meta[0]
    base = me * block
    start = doc_start(meta, ndocs, base)
    low_block = start // block
    _, ids = doc_column(meta, ndocs, base, block)
    first_doc = doc_at(meta, ndocs, base)
    last_doc = doc_at(meta, ndocs, base + block - 1)
    own = signal[me]
    spec = spectrum2(left2[...], masked(own, ids == first_doc))
    set_spec(acc, times(lags[0], spec))

    def cross(s, carry):
        position = s * block + lax.broadcasted_iota(jnp.int32, (block, 1), 0)
        spec = spectrum2(left2[...], masked(signal[s], position >= start))
        add_spec(acc, times(lags[me - s], spec))
        return carry

    lax.fori_loop(low_block, me, cross, 0)
    out[...] = jnp.where(ids == first_doc, spectrum3(inv3[...], acc[...]), 0.0)

    def inner(d, carry):
        spec = spectrum2(left2[...], masked(own, ids == d))
        set_spec(acc, times(lags[0], spec))
        out[...] += jnp.where(ids == d, spectrum3(inv3[...], acc[...]), 0.0)
        return carry

    lax.fori_loop(first_doc + 1, last_doc + 1, inner, 0)


def mlp_kernel(tokens, cot, conv, carried, gate_out, fbias, w_out, b_out, gain, shift,
               up, up_bias, down, down_bias,
               output, actt, gpre_ref, ubias_grad, n2t, gatedt, gmix, gresid, glong, glong16,
               ggate, smalls,
               resid, n2, hat2, rstd2, oacc, gacc):
    j = pl.program_id(0)

    @pl.when(j == 0)
    def _():
        long_out = conv[...] + fbias[...].astype(F32) * carried[...].astype(F32)
        gated = long_out * gate_out[...]
        gatedt[...] = gated.T.astype(BF16)
        r = tokens[...].astype(F32) + dot(gated.astype(BF16), w_out[...]) + b_out[...].astype(F32)
        resid[...] = r
        hat, rstd = normalise(r)
        hat2[...] = hat
        rstd2[...] = rstd
        normed = hat * gain[...].astype(F32) + shift[...].astype(F32)
        n2t[...] = normed.T.astype(BF16)
        n2[...] = normed.astype(BF16)
        oacc[...] = jnp.zeros_like(oacc)
        gacc[...] = jnp.zeros_like(gacc)

    pre = dot(n2[...], up[...]) + up_bias[...].astype(F32)
    sq = pre * pre
    th = jnp.tanh(GELU_C * (pre * (1.0 + GELU_A * sq)))
    act = 0.5 * pre * (1.0 + th)
    slope = 0.5 * (1.0 + th) + 0.5 * pre * (1.0 - th * th) * (
        GELU_C * (1.0 + 3.0 * GELU_A * sq)
    )
    actt[...] = act.T.astype(BF16)
    oacc[...] += dot(act.astype(BF16), down[...])
    gpre = (dot_t(cot[...], down[...]) * slope).astype(BF16)
    gpre_ref[...] = gpre
    ubias_grad[...] = jnp.sum(gpre.astype(F32), axis=0, keepdims=True)
    gacc[...] += dot_t(gpre, up[...])

    @pl.when(j == pl.num_programs(0) - 1)
    def _():
        output[...] = (resid[...] + oacc[...] + down_bias[...].astype(F32)).astype(BF16)
        top = cot[...].astype(F32)
        gn = gacc[...]
        hat = hat2[...]
        q = gn * gain[...].astype(F32)
        mean_q = jnp.mean(q, axis=-1, keepdims=True)
        mean_qh = jnp.mean(q * hat, axis=-1, keepdims=True)
        gr = top + (q - mean_q - hat * mean_qh) * rstd2[...]
        gresid[...] = gr
        gm = gr.astype(BF16)
        gmix[...] = gm
        gg = dot_t(gm, w_out[...])
        c = carried[...].astype(F32)
        long_out = conv[...] + fbias[...].astype(F32) * c
        gl = gg * gate_out[...]
        glong[...] = gl
        glong16[...] = gl.astype(BF16)
        ggate[...] = gg * long_out
        rows = [
            jnp.sum(top, axis=0, keepdims=True),
            jnp.sum(gn * hat, axis=0, keepdims=True),
            jnp.sum(gn, axis=0, keepdims=True),
            jnp.sum(gm.astype(F32), axis=0, keepdims=True),
            jnp.sum(gl * c, axis=0, keepdims=True),
        ]
        rows.append(jnp.zeros((8 - len(rows), gn.shape[1]), F32))
        smalls[...] = jnp.concatenate(rows, axis=0)


def conv_back_kernel(ndocs, length, meta, grads, own_grad, lags, invt2, leftt3, fbias,
                     gate_in, values, for_in, for_values, acc):
    block = grads.shape[1]
    me = meta[0]
    base = me * block
    _, ids = doc_column(meta, ndocs, base, block)
    first_doc = doc_at(meta, ndocs, base)
    last_doc = doc_at(meta, ndocs, base + block - 1)
    last_block = (doc_end(meta, ndocs, base + block - 1, length) - 1) // block
    own = grads[me]
    spec = spectrum2(invt2[...], masked(own, ids == last_doc))
    set_spec(acc, times_back(lags[0], spec))

    def cross(t, carry):
        _, far = doc_column(meta, ndocs, t * block, block)
        spec = spectrum2(invt2[...], masked(grads[t], far == last_doc))
        add_spec(acc, times_back(lags[t - me], spec))
        return carry

    lax.fori_loop(me + 1, last_block + 1, cross, 0)
    for_in[...] = jnp.where(ids == last_doc, spectrum3(leftt3[...], acc[...]), 0.0)

    def inner(d, carry):
        spec = spectrum2(invt2[...], masked(own, ids == d))
        set_spec(acc, times_back(lags[0], spec))
        for_in[...] += jnp.where(ids == d, spectrum3(leftt3[...], acc[...]), 0.0)
        return carry

    lax.fori_loop(first_doc, last_doc, inner, 0)
    total = for_in[...] + fbias[...].astype(F32) * own_grad[...]
    for_in[...] = total * values[...]
    for_values[...] = total * gate_in[...]


def taps_grad_kernel(ndocs, length, meta, signal, own_grad, left2, invt2, leftt3, out, win, gspec):
    blocks, block = signal.shape[0], signal.shape[1]
    me = meta[0]
    base = me * block
    start = doc_start(meta, ndocs, base)
    low_block = start // block
    _, ids = doc_column(meta, ndocs, base, block)
    first_doc = doc_at(meta, ndocs, base)
    last_doc = doc_at(meta, ndocs, base + block - 1)
    sign = 1.0 - 2.0 * (lax.broadcasted_iota(jnp.int32, (2 * block, 1), 0) % 2).astype(F32)
    own = signal[me]
    grad = own_grad[...]
    out[...] = jnp.zeros_like(out)
    win[me - low_block + 1] = jnp.zeros(win.shape[1:], F32)
    gspec[...] = spectrum2(invt2[...], masked(grad, ids == first_doc))
    spec = spectrum2(left2[...], masked(own, ids == first_doc))
    set_spec(win.at[0], times_back(spec, gspec[...]))

    def inner(d, carry):
        spec = spectrum2(left2[...], masked(own, ids == d))
        back = spectrum2(invt2[...], masked(grad, ids == d))
        add_spec(win.at[0], times_back(spec, back))
        return carry

    lax.fori_loop(first_doc + 1, last_doc + 1, inner, 0)

    def cross(s, carry):
        position = s * block + lax.broadcasted_iota(jnp.int32, (block, 1), 0)
        spec = spectrum2(left2[...], masked(signal[s], position >= start))
        set_spec(win.at[me - s], times_back(spec, gspec[...]))
        return carry

    lax.fori_loop(low_block, me, cross, 0)

    def emit(k, carry):
        out[k] = spectrum3(leftt3[...], win[k + 1] + sign * win[k])
        return carry

    lax.fori_loop(0, me - low_block + 1, emit, 0)


def short_back_kernel(ndocs, meta, ggate, for_in, for_values, rim, proj, taps,
                      gproj_ref, smalls):
    block, width = ggate.shape
    taps_n = taps.shape[0]
    base = meta[0] * block
    position, ids = doc_column(meta, ndocs, base, block)
    masks = []
    for k in range(taps_n):
        _, back = doc_column(meta, ndocs, base - k, block)
        masks.append(((back == ids) & (position >= k)).astype(F32))
    row = lax.broadcasted_iota(jnp.int32, (block, 1), 0)
    ahead = []
    for k in range(1, taps_n):
        _, later = doc_column(meta, ndocs, base + k, block)
        ahead.append(((later == ids) & (row < block - k)).astype(F32))
    bias_rows, weight_rows, short_rows = [], [], []
    for third, grad_ref in enumerate((ggate, for_in, for_values)):
        cols = slice(third * width, (third + 1) * width)
        grad = grad_ref[...]
        total = taps[0:1, cols].astype(F32) * grad
        weights = [jnp.sum(grad * proj[pl.ds(RIM, block), cols], axis=0, keepdims=True)]
        for k in range(1, taps_n):
            moved = pltpu.roll(grad, block - k, 0) * ahead[k - 1]
            total = total + taps[k : k + 1, cols].astype(F32) * moved
            weights.append(
                jnp.sum(grad * masks[k] * proj[pl.ds(RIM - k, block), cols], axis=0, keepdims=True)
            )
        tail = jnp.concatenate([jnp.zeros((block - 8, width), F32), rim[:, cols]], axis=0)
        low = (total + tail).astype(BF16)
        gproj_ref[:, cols] = low
        bias_rows.append(jnp.sum(low.astype(F32), axis=0, keepdims=True))
        short_rows.append(jnp.sum(grad, axis=0, keepdims=True))
        weight_rows.append(weights)
    rows = bias_rows + [weight_rows[t][k] for k in range(taps_n) for t in range(3)] + short_rows
    pad = smalls.shape[0] - len(rows)
    smalls[...] = jnp.concatenate(rows + [jnp.zeros((pad, width), F32)], axis=0)


def tail_kernel(gproj, weight, tokens, gain, gresid, out, smalls):
    gn = dot_t(gproj[...], weight[...])
    hat, rstd = normalise(tokens[...].astype(F32))
    q = gn * gain[...].astype(F32)
    mean_q = jnp.mean(q, axis=-1, keepdims=True)
    mean_qh = jnp.mean(q * hat, axis=-1, keepdims=True)
    out[...] = gresid[...] + (q - mean_q - hat * mean_qh) * rstd
    rows = [
        jnp.sum(gn * hat, axis=0, keepdims=True),
        jnp.sum(gn, axis=0, keepdims=True),
        jnp.zeros((6, gn.shape[1]), F32),
    ]
    smalls[...] = jnp.concatenate(rows, axis=0)


def filter_taps(first, first_bias, second, second_bias, third, third_bias, last, sine_freq, length):
    lags = jnp.arange(length)
    bands = (first.shape[0] - 1) // 2
    moment = lags.astype(F32) / (length - 1)
    band_freq = jnp.linspace(0.0001, bands - 1, bands, dtype=F32)
    phase = 2.0 * math.pi / length * lags.astype(F32)
    angles = phase[:, None] * band_freq[None, :]
    features = jnp.concatenate([moment[:, None], jnp.cos(angles), -jnp.sin(angles)], axis=1)
    hidden = jnp.sin(sine_freq * (jnp.dot(features, first, precision=HIGHEST) + first_bias))
    hidden = jnp.sin(sine_freq * (jnp.dot(hidden, second, precision=HIGHEST) + second_bias))
    hidden = jnp.sin(sine_freq * (jnp.dot(hidden, third, precision=HIGHEST) + third_bias))
    rates = jnp.linspace(MIN_DECAY, MAX_DECAY, last.shape[1], dtype=F32)
    window = jnp.exp(-moment[:, None] * rates[None, :])
    return jnp.dot(hidden, last, precision=HIGHEST) * window


def shift(block, axis, distance):
    devices = range(lax.axis_size(axis))
    return lax.ppermute(block, axis, [(i - distance, i) for i in devices if i - distance in devices])


def swap(block, axis, mask):
    return lax.ppermute(block, axis, [(i, i ^ mask) for i in range(lax.axis_size(axis))])


def butterfly(values):
    for axis in ("seq", "rows"):
        mask = 1
        while mask < lax.axis_size(axis):
            values = values + swap(values, axis, mask)
            mask *= 2
    return values


def strips(ref, chips, rows, core, first, take):
    return [
        ref[pl.ds(pl.multiple_of((2 * z + core) * rows + first, 16), take), :] for z in range(chips)
    ]


def early_grad_kernel(chips, meta, actt, act_sib, cot, cot_sib, n2t, n2_sib, gpre, gpre_sib,
                      gatedt, gated_sib, n1t, n1_sib, gmix, gmix_sib, gproj, gproj_sib, out):
    core, chip, row = meta[1], meta[2], meta[3]
    part = pl.program_id(0) ^ row
    rows = n2t.shape[0] // (2 * chips)
    width = cot.shape[1]

    def emit(left, left_sib, right, right_sib, first):
        lhs = jnp.concatenate([left, left_sib], axis=1)
        rhs = jnp.concatenate([right, right_sib], axis=0)
        made = dot(lhs, rhs).astype(BF16)
        for z in range(chips):
            out[0, z ^ chip, :, first : first + made.shape[1]] = made[z * rows : (z + 1) * rows]

    big = actt.shape[0] // (2 * chips)
    offset = pl.multiple_of(part * rows, 16)
    emit(
        jnp.concatenate(strips(actt, chips, big, core, offset, rows), axis=0),
        jnp.concatenate([act_sib[z, pl.ds(offset, rows), :] for z in range(chips)], axis=0),
        cot[...], cot_sib[...], 0,
    )
    cols = pl.ds(pl.multiple_of(part * width, 128), width)
    emit(
        jnp.concatenate(strips(n2t, chips, rows, core, 0, rows), axis=0),
        n2_sib[...].reshape(chips * rows, -1),
        gpre[:, cols], gpre_sib[:, cols], width,
    )
    half = pl.ds(pl.multiple_of((part % 2) * (width // 2), 128), width // 2)

    @pl.when(part < 2)
    def _():
        emit(
            jnp.concatenate(strips(gatedt, chips, rows, core, 0, rows), axis=0),
            gated_sib[...].reshape(chips * rows, -1),
            gmix[:, half], gmix_sib[:, half], 2 * width,
        )

    @pl.when(part >= 2)
    def _():
        emit(
            jnp.concatenate(strips(n1t, chips, rows, core, 0, rows), axis=0),
            n1_sib[...].reshape(chips * rows, -1),
            gproj[:, half], gproj_sib[:, half], 2 * width,
        )


def late_grad_kernel(chips, meta, n1t, n1_sib, gproj, gproj_sib, out):
    core, chip, row = meta[1], meta[2], meta[3]
    part = pl.program_id(0) ^ row
    rows = n1t.shape[0] // (2 * chips)
    take = out.shape[3]
    cols = pl.ds(pl.multiple_of(part * take, 128), take)
    left = jnp.concatenate(strips(n1t, chips, rows, core, 0, rows), axis=0)
    lhs = jnp.concatenate([left, n1_sib[...].reshape(chips * rows, -1)], axis=1)
    rhs = jnp.concatenate([gproj[:, cols], gproj_sib[:, cols]], axis=0)
    made = dot(lhs, rhs).astype(BF16)
    for z in range(chips):
        out[0, z ^ chip, :, :] = made[z * rows : (z + 1) * rows]


def sum_over_mesh(parts):
    chips = parts.shape[1]
    total = parts[0].astype(F32)
    for j in range(1, parts.shape[0]):
        total = total + swap(parts[j], "rows", j).astype(F32)
    low = total.astype(BF16)
    own = total[0]
    for j in range(1, chips):
        own = own + swap(low[j], "seq", 2 * j).astype(F32)
    own = own.astype(BF16)
    return [own] + [swap(own, "rows", j) for j in range(1, parts.shape[0])]


def place_early_kernel(meta, *refs):
    pieces, (down, up, out_w, in_w) = refs[:-4], refs[-4:]
    row = meta[3]
    rows = pieces[0].shape[0]
    width = out_w.shape[1]
    for j, piece in enumerate(pieces):
        part = row ^ j
        down[pl.ds(pl.multiple_of(part * rows, 8), rows), :] = piece[:, :width].astype(F32)
        up[:, pl.ds(pl.multiple_of(part * width, 128), width)] = piece[:, width : 2 * width].astype(F32)
        half = pl.ds(pl.multiple_of((part % 2) * (width // 2), 128), width // 2)

        @pl.when(part < 2)
        def _():
            out_w[:, half] = piece[:, 2 * width :].astype(F32)

        @pl.when(part >= 2)
        def _():
            in_w[:, half] = piece[:, 2 * width :].astype(F32)


def place_late_kernel(meta, early, *refs):
    pieces, in_w = refs[:-1], refs[-1]
    row = meta[3]
    width = early.shape[1]
    take = pieces[0].shape[1]
    in_w[:, :width] = early[...]
    for j, piece in enumerate(pieces):
        part = row ^ j
        in_w[:, pl.ds(pl.multiple_of(width + part * take, 128), take)] = piece[...].astype(F32)


def local(
    tokens, doc_starts, norm1_gain, norm1_bias, in_weight, in_bias, short_weight, short_bias,
    filter_first, filter_first_bias, filter_second, filter_second_bias, filter_third,
    filter_third_bias, filter_last, sine_freq, filter_bias, out_weight, out_bias, norm2_gain,
    norm2_bias, up_weight, up_bias, down_weight, down_bias, cotangent,
):
    block, width = tokens.shape[1:]
    blocks = lax.axis_size("seq")
    chips = blocks // 2
    nrows = lax.axis_size("rows")
    length = block * blocks
    hidden = up_weight.shape[1]
    index = lax.axis_index("seq")
    row = lax.axis_index("rows")
    starts = doc_starts[0]
    ndocs = starts.shape[0]
    taps_n = short_weight.shape[0]
    meta = jnp.concatenate(
        [jnp.stack([index, index % 2, index // 2, row]).astype(jnp.int32), starts]
    )
    tables = {k: jnp.asarray(v) for k, v in block_tables(block).items()}
    chunk = width if blocks <= 8 else 128
    steps = width // chunk
    tok, cot = tokens[0], cotangent[0]
    line = lambda v: v.reshape(1, -1)

    rim = shift(tok[block - RIM :], "seq", 1)
    proj, n1t, mixed, carried = pl.pallas_call(
        partial(front_kernel, ndocs),
        out_shape=(
            jax.ShapeDtypeStruct((block + RIM, 3 * width), F32),
            jax.ShapeDtypeStruct((width, block), BF16),
            jax.ShapeDtypeStruct((block, 3 * width), F32),
            jax.ShapeDtypeStruct((block, width), BF16),
        ),
        in_specs=[smem()] + [pl.BlockSpec(memory_space=pltpu.VMEM)] * 8,
        compiler_params=params(),
        name="front",
    )(meta, tok, rim, line(norm1_gain), line(norm1_bias), in_weight, line(in_bias), short_weight,
      line(short_bias))

    filter_params = tuple(
        v.astype(F32)
        for v in (filter_first, filter_first_bias, filter_second, filter_second_bias, filter_third,
                  filter_third_bias, filter_last, sine_freq)
    )
    taps, taps_pull = jax.vjp(partial(filter_taps, length=length), *filter_params)
    by_chunk = lambda lead: pl.BlockSpec(lead + (chunk,), lambda i: (0,) * len(lead) + (i,))
    lags = pl.pallas_call(
        lag_kernel,
        grid=(steps,),
        out_shape=jax.ShapeDtypeStruct((blocks, 2 * block, width), F32),
        in_specs=[by_chunk((blocks, block)), whole(tables["left3"].shape)],
        out_specs=by_chunk((blocks, 2 * block)),
        compiler_params=params(),
        name="lags",
    )(taps.reshape(blocks, block, width), tables["left3"])

    signal = lax.all_gather(carried, "seq", axis=0, tiled=False)
    conv = pl.pallas_call(
        partial(conv_kernel, ndocs, length),
        grid=(steps,),
        out_shape=jax.ShapeDtypeStruct((block, width), F32),
        in_specs=[smem(), by_chunk((blocks, block)), by_chunk((blocks, 2 * block)),
                  whole(tables["left2"].shape), whole(tables["inv3"].shape)],
        out_specs=by_chunk((block,)),
        scratch_shapes=[pltpu.VMEM((2 * block, chunk), F32)],
        compiler_params=params(),
        name="conv",
    )(meta, signal, lags, tables["left2"], tables["inv3"])

    ff = width
    fsteps = hidden // ff
    row_spec = whole((1, width))
    mat = whole((block, width))
    (output, actt, gpre, up_bias_grad, n2t, gatedt, gmix, gresid, glong, glong16, ggate,
     smalls_mlp) = pl.pallas_call(
        mlp_kernel,
        grid=(fsteps,),
        out_shape=(
            jax.ShapeDtypeStruct((block, width), BF16),
            jax.ShapeDtypeStruct((hidden, block), BF16),
            jax.ShapeDtypeStruct((block, hidden), BF16),
            jax.ShapeDtypeStruct((1, hidden), F32),
            jax.ShapeDtypeStruct((width, block), BF16),
            jax.ShapeDtypeStruct((width, block), BF16),
            jax.ShapeDtypeStruct((block, width), BF16),
            jax.ShapeDtypeStruct((block, width), F32),
            jax.ShapeDtypeStruct((block, width), F32),
            jax.ShapeDtypeStruct((block, width), BF16),
            jax.ShapeDtypeStruct((block, width), F32),
            jax.ShapeDtypeStruct((8, width), F32),
        ),
        in_specs=[
            mat, mat, mat, mat, mat, row_spec, whole((width, width)), row_spec, row_spec, row_spec,
            pl.BlockSpec((width, ff), lambda i: (0, i)), pl.BlockSpec((1, ff), lambda i: (0, i)),
            pl.BlockSpec((ff, width), lambda i: (i, 0)), row_spec,
        ],
        out_specs=(
            mat, pl.BlockSpec((ff, block), lambda i: (i, 0)), pl.BlockSpec((block, ff), lambda i: (0, i)),
            pl.BlockSpec((1, ff), lambda i: (0, i)), whole((width, block)), whole((width, block)),
            mat, mat, mat, mat, mat, whole((8, width)),
        ),
        scratch_shapes=[
            pltpu.VMEM((block, width), F32), pltpu.VMEM((block, width), BF16),
            pltpu.VMEM((block, width), F32), pltpu.VMEM((block, 1), F32),
            pltpu.VMEM((block, width), F32), pltpu.VMEM((block, width), F32),
        ],
        compiler_params=params(),
        name="mlp",
    )(tok, cot, conv, carried, mixed, line(filter_bias), out_weight, line(out_bias),
      line(norm2_gain), line(norm2_bias), up_weight, line(up_bias), down_weight, line(down_bias))

    grads = lax.all_gather(glong16, "seq", axis=0, tiled=False)
    third = lambda n: pl.BlockSpec((block, chunk), lambda i: (0, n * steps + i))
    for_in, for_values = pl.pallas_call(
        partial(conv_back_kernel, ndocs, length),
        grid=(steps,),
        out_shape=(jax.ShapeDtypeStruct((block, width), F32),) * 2,
        in_specs=[smem(), by_chunk((blocks, block)), by_chunk((block,)), by_chunk((blocks, 2 * block)),
                  whole(tables["invt2"].shape), whole(tables["leftt3"].shape), by_chunk((1,)),
                  third(1), third(2)],
        out_specs=(by_chunk((block,)),) * 2,
        scratch_shapes=[pltpu.VMEM((2 * block, chunk), F32)],
        compiler_params=params(),
        name="conv_back",
    )(meta, grads, glong, lags, tables["invt2"], tables["leftt3"], line(filter_bias), mixed, mixed)

    base = index * block
    head = jnp.concatenate([ggate[: taps_n - 1], for_in[: taps_n - 1], for_values[: taps_n - 1]], axis=1)
    places = base - (taps_n - 1) + jnp.arange(2 * (taps_n - 1))
    ids = jnp.sum((places[:, None] >= starts[None, :]).astype(jnp.int32), axis=1) - 1
    rim_out = []
    for p in range(taps_n - 1):
        total = jnp.zeros((3 * width,), F32)
        for k in range(1, taps_n):
            t = p - (taps_n - 1) + k
            if 0 <= t < taps_n - 1:
                same = ((ids[p] == ids[t + taps_n - 1]) & (base > 0)).astype(F32)
                total = total + short_weight[k].astype(F32) * head[t] * same
        rim_out.append(total)
    rim_out = jnp.concatenate([jnp.zeros((8 - (taps_n - 1), 3 * width), F32), jnp.stack(rim_out)], axis=0)
    rim_back = shift(rim_out, "seq", -1)

    vm = pl.BlockSpec(memory_space=pltpu.VMEM)
    gproj, smalls_short = pl.pallas_call(
        partial(short_back_kernel, ndocs),
        out_shape=(
            jax.ShapeDtypeStruct((block, 3 * width), BF16),
            jax.ShapeDtypeStruct((24, width), F32),
        ),
        in_specs=[smem()] + [vm] * 6,
        compiler_params=params(),
        name="short_back",
    )(meta, ggate, for_in, for_values, rim_back, proj, short_weight)

    grad_tokens, smalls_norm = pl.pallas_call(
        tail_kernel,
        out_shape=(
            jax.ShapeDtypeStruct((block, width), F32),
            jax.ShapeDtypeStruct((8, width), F32),
        ),
        in_specs=[vm] * 5,
        compiler_params=params(),
        name="tail",
    )(gproj, in_weight, tok, line(norm1_gain), gresid)

    taps_grad = pl.pallas_call(
        partial(taps_grad_kernel, ndocs, length),
        grid=(steps,),
        out_shape=jax.ShapeDtypeStruct((blocks, block, width), F32),
        in_specs=[smem(), by_chunk((blocks, block)), by_chunk((block,)), whole(tables["left2"].shape),
                  whole(tables["invt2"].shape), whole(tables["leftt3"].shape)],
        out_specs=by_chunk((blocks, block)),
        scratch_shapes=[pltpu.VMEM((blocks + 1, 2 * block, chunk), F32), pltpu.VMEM((2 * block, chunk), F32)],
        compiler_params=params(),
        name="taps_grad",
    )(meta, signal, glong, tables["left2"], tables["invt2"], tables["leftt3"])
    filter_grads = taps_pull(taps_grad.reshape(length, width))

    share = width // blocks
    if share % 16 == 0 and nrows == 4 and width % (2 * 128) == 0 and taps_n == 3:
        other = 1 - index % 2

        def for_sibling(features):
            parted = features.reshape(chips, 2, features.shape[0] // blocks, block)
            return lax.dynamic_index_in_dim(parted, other, 1, keepdims=False)

        cot_sib = swap(cot, "seq", 1)
        n1_sib = swap(for_sibling(n1t), "seq", 1)
        gproj_sib = swap(gproj, "seq", 1)
        early_cols = 2 * width + width // 2
        early = pl.pallas_call(
            partial(early_grad_kernel, chips),
            grid=(nrows,),
            out_shape=jax.ShapeDtypeStruct((nrows, chips, share, early_cols), BF16),
            in_specs=[smem()] + [
                whole(s) for s in (
                    (hidden, block), (chips, hidden // blocks, block), (block, width), (block, width),
                    (width, block), (chips, share, block), (block, hidden), (block, hidden),
                    (width, block), (chips, share, block), (width, block), (chips, share, block),
                    (block, width), (block, width), (block, width), (block, width),
                )
            ],
            out_specs=pl.BlockSpec((1, chips, share, early_cols), lambda i: (i, 0, 0, 0)),
            compiler_params=params(),
            name="early_grad",
        )(meta, actt, swap(for_sibling(actt), "seq", 1), cot, cot_sib, n2t,
          swap(for_sibling(n2t), "seq", 1), gpre, swap(gpre, "seq", 1), gatedt,
          swap(for_sibling(gatedt), "seq", 1), n1t, n1_sib, gmix, swap(gmix, "seq", 1),
          gproj, gproj_sib)
        pieces = sum_over_mesh(early)
        grad_down, grad_up, grad_out, grad_in_early = pl.pallas_call(
            place_early_kernel,
            out_shape=(
                jax.ShapeDtypeStruct((hidden // blocks, width), F32),
                jax.ShapeDtypeStruct((share, hidden), F32),
                jax.ShapeDtypeStruct((share, width), F32),
                jax.ShapeDtypeStruct((share, width), F32),
            ),
            in_specs=[smem()] + [vm] * 4,
            compiler_params=params(),
            name="place_early",
        )(meta, *pieces)
        late_cols = width // 2
        late = pl.pallas_call(
            partial(late_grad_kernel, chips),
            grid=(nrows,),
            out_shape=jax.ShapeDtypeStruct((nrows, chips, share, late_cols), BF16),
            in_specs=[smem(), whole((width, block)), whole((chips, share, block)),
                      whole((block, 2 * width)), whole((block, 2 * width))],
            out_specs=pl.BlockSpec((1, chips, share, late_cols), lambda i: (i, 0, 0, 0)),
            compiler_params=params(),
            name="late_grad",
        )(meta, n1t, n1_sib, gproj[:, width:], gproj_sib[:, width:])
        grad_in = pl.pallas_call(
            place_late_kernel,
            out_shape=jax.ShapeDtypeStruct((share, 3 * width), F32),
            in_specs=[smem()] + [vm] * 5,
            compiler_params=params(),
            name="place_late",
        )(meta, grad_in_early, *sum_over_mesh(late))
    else:
        def spread(left, right):
            part = lax.psum_scatter(dot(left, right), "seq", scatter_dimension=0, tiled=True)
            return lax.psum(part, "rows")

        grad_in = spread(n1t, gproj)
        grad_out = spread(gatedt, gmix)
        grad_up = spread(n2t, gpre)
        grad_down = spread(actt, cot)

    flat_filter = jnp.concatenate([filter_grads[i].reshape(-1) for i in (0, 1, 2, 3, 4, 5, 7)])
    used = flat_filter.shape[0]
    fill = -used % width
    smalls = jnp.concatenate(
        [
            up_bias_grad.reshape(-1, width),
            smalls_mlp,
            smalls_short,
            smalls_norm,
            filter_grads[6],
            jnp.pad(flat_filter, (0, fill)).reshape(-1, width),
        ],
        axis=0,
    )
    smalls = butterfly(smalls)
    at = hidden // width
    grad_up_bias = smalls[:at].reshape(-1)
    grad_down_bias, grad_gain2, grad_shift2, grad_out_bias, grad_filter_bias = (
        smalls[at + i] for i in range(5)
    )
    at += 8
    grad_in_bias = smalls[at : at + 3].reshape(-1)
    grad_short_weight = smalls[at + 3 : at + 3 + 3 * taps_n].reshape(taps_n, 3 * width)
    grad_short_bias = smalls[at + 3 + 3 * taps_n : at + 6 + 3 * taps_n].reshape(-1)
    at += 24
    grad_gain1, grad_shift1 = smalls[at], smalls[at + 1]
    at += 8
    grad_last = smalls[at : at + filter_last.shape[0]]
    at += filter_last.shape[0]
    flat = smalls[at:].reshape(-1)
    pieces, place = {}, 0
    for i in (0, 1, 2, 3, 4, 5, 7):
        size = math.prod(filter_grads[i].shape)
        pieces[i] = flat[place : place + size].reshape(filter_grads[i].shape)
        place += size
    return (
        output[None], grad_tokens[None], grad_gain1, grad_shift1, grad_in, grad_in_bias,
        grad_short_weight, grad_short_bias, pieces[0], pieces[1], pieces[2], pieces[3], pieces[4],
        pieces[5], grad_last, pieces[7], grad_filter_bias, grad_out, grad_out_bias, grad_gain2,
        grad_shift2, grad_up, grad_up_bias, grad_down, grad_down_bias,
    )


def solution(mesh):
    sharded = P("rows", "seq", None)
    placed = (sharded, P("rows", None)) + (P(),) * 23 + (sharded,)
    outs = [P()] * 25
    outs[0] = outs[1] = sharded
    for i in (4, 17, 21, 23):
        outs[i] = P("seq", None)
    return jax.shard_map(local, mesh=mesh, in_specs=placed, out_specs=tuple(outs), check_vma=False)
```

time: 953 us -> 310 us (0.33)
  waiting for transfers between devices: 657 us -> 106 us
  matrix products: 131 us -> 17.6 us
  Pallas kernels: 0 us -> 69.2 us
  other arithmetic: 66.5 us -> 10.4 us
  starting transfers between devices: 4.93 us -> 40.5 us
  local copies, waits for them, and re-layouts: 63.2 us -> 46.5 us
    psum x3 -> x0, waiting for transfers between devices: 385 us -> none  [the longest x2 285 us: local(): lax.psum((grad_gain1, grad_shift1, grad_in_bias, grad_short_weight, grad_...]
    reduce_scatter x5 -> x0, waiting for transfers between devices: 261 us -> none  [the longest x1 100 us: local(): lax.psum_scatter(grad_down, 'seq', scatter_dimension=0, tiled=True)]
    dot_general x40 -> x0, matrix products: 108 us -> none  [the longest x10 15.7 us: self_conv(): total = total + member * jnp.dot(inverse_table, joined, precision=HIGHEST)]
    ppermute x2 -> x33, waiting for transfers between devices: 1.53 us -> 94.7 us  [the longest x31 93.5 us: swap(): lax.ppermute(block, axis, [(i, i ^ mask) for i in range(lax.axis_size(axi...]
    pallas_call x0 -> x12, Pallas kernels: none -> 69.2 us  [the longest x1 11.6 us: local(): pl.pallas_call(mlp_kernel, grid=(fsteps,), out_shape=(jax.ShapeDtypeStruc...]
    ppermute x2 -> x33, starting transfers between devices: 4.38 us -> 40.4 us  [the longest x31 36.5 us: swap(): lax.ppermute(block, axis, [(i, i ^ mask) for i in range(lax.axis_size(axi...]
    unnamed x279 -> x84, local copies, waits for them, and re-layouts: 37.1 us -> 5.35 us
    reshape x3 -> x20, local copies, waits for them, and re-layouts: 1.43 us -> 13.4 us  [the longest x10 8.63 us: local(): line = lambda v: v.reshape(1, -1)]
  transfers between devices with their start and end apart: 11 -> 35, of which waited for: 9 -> 11; matrix products, arithmetic and copies ran while one was open for 19% -> 22% of each run, Pallas kernels for 0% -> 14%
where the time goes in v1:
time: 310 us; the launch traced here: 308 us
  waiting for transfers between devices  106 us (34%)
  Pallas kernels  69.2 us (22%)
  local copies, waits for them, and re-layouts  46.5 us (15%)
  starting transfers between devices  40.5 us (13%)
  between operations  18.7 us (6%)
  matrix products  17.6 us (6%)
  other arithmetic  10.4 us (3%)
    ppermute x31, waiting for transfers between devices, swap(): lax.ppermute(block, axis, [(i, i ^ mask) for i in range(lax.axis_size(axi...  93.5 us
    ppermute x31, starting transfers between devices, swap(): lax.ppermute(block, axis, [(i, i ^ mask) for i in range(lax.axis_size(axi...  36.5 us
    pallas_call x1, Pallas kernels, local(): pl.pallas_call(mlp_kernel, grid=(fsteps,), out_shape=(jax.ShapeDtypeStruc...  11.6 us
    dot_general x3, matrix products, filter_taps(): return jnp.dot(hidden, last, precision=HIGHEST) * window  9.5 us
    pallas_call x1, Pallas kernels, local(): pl.pallas_call(partial(conv_back_kernel, ndocs, length), grid=(steps,), o...  9.07 us
    all_gather x1, waiting for transfers between devices, local(): signal = lax.all_gather(carried, 'seq', axis=0, tiled=False)  8.75 us
    reshape x10, local copies, waits for them, and re-layouts, local(): line = lambda v: v.reshape(1, -1)  8.63 us
    pallas_call x1, Pallas kernels, local(): pl.pallas_call(lag_kernel, grid=(steps,), out_shape=jax.ShapeDtypeStruct(...  7.9 us
  transfers between devices with their start and end apart: 35, of which 11 were waited for; matrix products, arithmetic and copies ran while one was open for 22% of the time, Pallas kernels for 14%

profile of v1, /device:TPU:0, one launch (start us, length us, event | category | flops | bytes accessed | tf_op | source)
XLA Modules:
  0.0 308.5 jit_solution(1918113175988152446)
XLA Ops:
  8.2 2.3 collective-permute-start
  17.6 5.0 %front.1 = (f32[144,2304]{1,0:T(8,128)}, bf16[768,128]{1,0:T(8,128)(2,1)}, f32[128,2304]{1,0:T(8,128)}, bf16[128,768]{1,0:T(8,128)(2,1)}) custom-call(s32[9]{0:T(128)} %concatenate.26.meta, bf16[128,768]{1,0:T(8,128)(2,1)} %bitcast.107, bf16[16,768]{1,0:T(8,128)(2,1)} %copy-done.28, bf16[1,768]{1,0:T(2,128)(2,1)} %reshape.204.gain, ...), custom_call_target="tpu_custom_call" | custom-call | tf_op jit(solution)/shard_map/front/pallas_call | solution.py:603
  29.5 4.2 %fusion = f32[1024,768]{1,0:T(8,128)} fusion(bf16[64,768]{1,0:T(8,128)(2,1)S(1)} %copy-done, f32[768]{0:T(1024)S(1)} %pad_maximum_fusion.5, f32[1024]{0:T(1024)S(1)} %multiply_negate_fusion, f32[1024,64]{0,1:T(8,128)S(1)} %convolution_add_fusion, f32[64]{0:T(128)S(1)} %convert_element_type.123), kind=kOutput, calls=%fused_computation.2 | convolution fusion | flops 605618176 | bytes 3513600 | tf_op jit(solution)/shard_map/jvp()/dot_general | solution.py:445
  33.7 7.9 %lags.1 = f32[8,256,768]{2,1,0:T(8,128)} custom-call(f32[8,128,768]{2,1,0:T(8,128)} %bitcast.104, bf16[256,384]{1,0:T(8,128)(2,1)} %constant.103.clone.left3), custom_call_target="tpu_custom_call" | custom-call | tf_op jit(solution)/shard_map/lags/pallas_call | solution.py:624
  41.6 8.7 %all-gather.5.cloned.1.call-done = bf16[1024,768]{1,0:T(8,128)(2,1)} async-done(((bf16[128,768]{1,0:T(8,128)(2,1)}), bf16[1024,768]{1,0:T(8,128)(2,1)}) %all-gather.5.cloned.1.call-update) | async-done | bytes 1572880 | tf_op jit(solution)/shard_map/all_gather | solution.py:634
  50.4 6.2 %conv.1 = f32[128,768]{1,0:T(8,128)} custom-call(s32[9]{0:T(128)} %concatenate.26.meta, bf16[8,128,768]{2,1,0:T(8,128)(2,1)} %bitcast.105, f32[8,256,768]{2,1,0:T(8,128)} %lags.1, bf16[256,256]{1,0:T(8,128)(2,1)} %constant.102.clone.left2, bf16[128,768]{1,0:T(8,128)(2,1)} %constant.104.clone.inv3), custom_call_target="tpu_custom_call" | custom-call | tf_op jit(solution)/shard_map/conv/pallas_call | solution.py:635
  56.6 11.6 %mlp.1 = (bf16[128,768]{1,0:T(8,128)(2,1)}, bf16[3072,128]{1,0:T(8,128)(2,1)}, bf16[128,3072]{1,0:T(8,128)(2,1)}, f32[1,3072]{1,0:T(1,128)}, bf16[768,128]{1,0:T...) custom-call(bf16[128,768]{1,0:T(8,128)(2,1)} %bitcast.108, ...), custom_call_target="tpu_custom_call" | custom-call | tf_op jit(solution)/shard_map/mlp/pallas_call | solution.py:652
  75.0 5.2 %taps_grad.1 = f32[8,128,768]{2,1,0:T(8,128)} custom-call(s32[9]{0:T(128)} %concatenate.26.meta, bf16[8,128,768]{2,1,0:T(8,128)(2,1)} %bitcast.106, f32[128,768]{1,0:T(8,128)} %get-tuple-element.56.own_grad, bf16[256,256]{1,0:T(8,128)(2,1)} %constant.102.clone.left2, bf16[256,256]{1,0:T(8,128)(2,1)} %constant.105.clone.invt2, ...), custom_call_target="tpu_custom_call" | custom-call | tf_op jit(solution)/shard_map/taps_grad/pallas_call | solution.py:743
  80.2 2.4 bitcast_multiply_fusion
  82.6 2.4 convolution_multiply_fusion.2
  90.0 2.9 fusion.13
  92.9 2.2 all-gather.7.cloned.1.call-done
  95.1 9.1 %conv_back.1 = (f32[128,768]{1,0:T(8,128)}, f32[128,768]{1,0:T(8,128)}) custom-call(s32[9]{0:T(128)} %concatenate.26.meta, bf16[8,128,768]{2,1,0:T(8,128)(2,1)} %bitcast.111, f32[128,768]{1,0:T(8,128)} %get-tuple-element.56.own_grad, f32[8,256,768]{2,1,0:T(8,128)} %lags.1, bf16[256,256]{1,0:T(8,128)(2,1)} %constant.105.clone.invt2, ...), custom_call_target="tpu_custom_call" | custom-call | tf_op jit(solution)/shard_map/conv_back/pallas_call | solution.py:691
  109.6 3.8 %short_back.1 = (bf16[128,2304]{1,0:T(8,128)(2,1)}, f32[24,768]{1,0:T(8,128)}) custom-call(s32[9]{0:T(128)} %concatenate.26.meta, f32[128,768]{1,0:T(8,128)} %get-tuple-element.54.ggate, f32[128,768]{1,0:T(8,128)} %get-tuple-element.57.for_in, f32[128,768]{1,0:T(8,128)} %get-tuple-element.58.for_values, f32[8,2304]{1,0:T(8,128)} %copy-done.24, ...), custom_call_target="tpu_custom_call" | custom-call | tf_op jit(solution)/shard_map/short_back/pallas_call | solution.py:721
  116.0 4.5 %tail.1 = (f32[128,768]{1,0:T(8,128)}, f32[8,768]{1,0:T(8,128)}) custom-call(bf16[128,2304]{1,0:T(8,128)(2,1)} %get-tuple-element.60.gproj, bf16[768,2304]{1,0:T(8,128)(2,1)} %weight.3, bf16[128,768]{1,0:T(8,128)(2,1)} %bitcast.109, bf16[1,768]{1,0:T(2,128)(2,1)} %reshape.204.gain, f32[128,768]{1,0:T(8,128)} %get-tuple-element.61.gresid), custom_call_target="tpu_custom_call" | custom-call | tf_op jit(solution)/shard_map/tail/pallas_call | solution.py:732
  120.6 3.0 concatenate.33
  130.3 7.0 %early_grad.1 = bf16[4,4,96,1920]{3,2,1,0:T(8,128)(2,1)} custom-call(s32[9]{0:T(128)} %concatenate.26.meta, bf16[3072,128]{1,0:T(8,128)(2,1)} %get-tuple-element.67.actt, bf16[4,384,128]{2,1,0:T(8,128)(2,1)} %copy-done.14, bf16[128,768]{1,0:T(8,128)(2,1)} %bitcast.114, bf16[128,768]{1,0:T(8,128)(2,1)} %collective-permute-done.8.cot_sib, ...), custom_call_target="tpu_custom_call" | custom-call | tf_op jit(solution)/shard_map/early_grad/pallas_call | solution.py:768
  137.3 4.4 %slice_bitcast_fusion.2 = (bf16[4,96,1920]{2,1,0:T(8,128)(2,1)S(1)}, bf16[4,96,1920]{2,1,0:T(8,128)(2,1)}, bf16[4,96,1920]{2,1,0:T(8,128)(2,1)}) fusion(bf16[4,4,96,1920]{3,2,1,0:T(8,128)(2,1)} %early_grad.1), kind=kLoop, calls=%fused_computation.8 | loop fusion | bytes 8847360 | tf_op jit(solution)/shard_map/squeeze | solution.py:536
  141.6 2.4 collective-permute-start.17
  146.7 3.5 %late_grad.1 = bf16[4,4,96,384]{3,2,1,0:T(8,128)(2,1)} custom-call(s32[9]{0:T(128)} %concatenate.26.meta, bf16[768,128]{1,0:T(8,128)(2,1)} %get-tuple-element.71.n1t, bf16[4,96,128]{2,1,0:T(8,128)(2,1)} %copy-done.13, bf16[128,1536]{1,0:T(8,128)(2,1)} %slice.185.gproj, bf16[128,1536]{1,0:T(8,128)(2,1)} %slice.226.gproj_sib), custom_call_target="tpu_custom_call" | custom-call | tf_op jit(solution)/shard_map/late_grad/pallas_call | solution.py:801
  150.3 2.5 collective-permute-start.4
  154.0 2.4 collective-permute-start.26
  156.4 58.6 %collective-permute-done.26 = bf16[4,96,384]{2,1,0:T(8,128)(2,1)S(1)} collective-permute-done((bf16[4,96,384]{2,1,0:T(8,128)(2,1)S(1)}, bf16[4,96,384]{2,1,0:T(8,128)(2,1)S(1)}, u32[]{:S(2)}, u32[]{:S(2)}) %collective-permute-start.26) | collective-permute-done | bytes 294944 | tf_op jit(solution)/shard_map/ppermute | solution.py:454
  217.9 5.2 %collective-permute-done.25 = bf16[4,96,384]{2,1,0:T(8,128)(2,1)S(1)} collective-permute-done((bf16[4,96,384]{2,1,0:T(8,128)(2,1)S(1)}, bf16[4,96,384]{2,1,0:T(8,128)(2,1)S(1)}, u32[]{:S(2)}, u32[]{:S(2)}) %collective-permute-start.25) | collective-permute-done | bytes 294944 | tf_op jit(solution)/shard_map/ppermute | solution.py:454
  225.7 3.1 %collective-permute-start.29 = (bf16[96,384]{1,0:T(8,128)(2,1)S(1)}, bf16[96,384]{1,0:T(8,128)(2,1)S(1)}, u32[]{:S(2)}, u32[]{:S(2)}) collective-permute-start(bf16[96,384]{1,0:T(8,128)(2,1)S(1)} %get-tuple-element.106), channel_id=1, source_target_pairs={{0,6},{1,7},{2,4},{3,5},{4,2},{5,3},{6,0},{7,1},{8,14},{9,15},{10,... | collective-permute-start | bytes 221192 | tf_op jit(solution)/shard_map/ppermute | solution.py:454
  228.8 3.8 %collective-permute-done.5 = f32[122,768]{1,0:T(8,128)S(1)} collective-permute-done((f32[122,768]{1,0:T(8,128)S(1)}, f32[122,768]{1,0:T(8,128)S(1)}, u32[]{:S(2)}, u32[]{:S(2)}) %collective-permute-start.5) | collective-permute-done | bytes 374816 | tf_op jit(solution)/shard_map/ppermute | solution.py:454
  237.6 3.0 fusion.43
  243.7 2.3 collective-permute-start.18
  252.4 2.8 collective-permute-done.20
  255.2 18.0 %collective-permute-done.19 = bf16[96,1920]{1,0:T(8,128)(2,1)} collective-permute-done((bf16[96,1920]{1,0:T(8,128)(2,1)}, bf16[96,1920]{1,0:T(8,128)(2,1)}, u32[]{:S(2)}, u32[]{:S(2)}) %collective-permute-start.19) | collective-permute-done | bytes 368672 | tf_op jit(solution)/shard_map/ppermute | solution.py:454
  291.8 2.4 collective-permute-done.22.refs_2_
  295.7 3.2 %place_early.1 = (f32[384,768]{1,0:T(8,128)}, f32[96,3072]{1,0:T(8,128)}, f32[96,768]{1,0:T(8,128)}, f32[96,768]{1,0:T(8,128)}) custom-call(s32[9]{0:T(128)} %concatenate.26.meta, bf16[96,1920]{1,0:T(8,128)(2,1)} %copy-done.7, bf16[96,1920]{1,0:T(8,128)(2,1)} %copy-done.16, bf16[96,1920]{1,0:T(8,128)(2,1)} %copy-done.17, bf16[96,1920]{1,0:T(8,128)(2,1)} %copy-done.18), custom_call_target="tpu_custom_call" | custom-call | tf_op jit(solution)/shard_map/place_early/pallas_call | solution.py:788
  (229 shorter events, 83.6 us)
Async XLA Ops:
  7.4 43.0 %all-gather.5.cloned.1.call-start = ((), (), s32[]{:S(2)}) async-start(), calls=%async_computation | async-start | bytes 1769472 | tf_op jit(solution)/shard_map/all_gather | solution.py:634
  8.2 8.8 %collective-permute-start = (bf16[16,768]{1,0:T(8,128)(2,1)S(1)}, bf16[16,768]{1,0:T(8,128)(2,1)S(1)}, u32[]{:S(2)}, u32[]{:S(2)}) collective-permute-start(bf16[16,768]{1,0:T(8,128)(2,1)S(1)} %slice_bitcast_fusion.16), channel_id=1, source_target_pairs={{0,1},{1,2},{2,3},{3,4},{4,5},{5,6},{6,7},{8,9},{9,10},{10,11},{11... | collective-permute-start | bytes 73736 | tf_op jit(solution)/shard_map/ppermute | solution.py:450
  22.6 72.5 %all-gather.7.cloned.1.call-start = ((), (), s32[]{:S(2)}) async-start(), calls=%async_computation.1 | async-start | bytes 1769472 | tf_op jit(solution)/shard_map/all_gather | solution.py:689
  68.2 56.0 %collective-permute-start.8 = (bf16[128,768]{1,0:T(8,128)(2,1)S(1)}, bf16[128,768]{1,0:T(8,128)(2,1)}, u32[]{:S(2)}, u32[]{:S(2)}) collective-permute-start(bf16[128,768]{1,0:T(8,128)(2,1)S(1)} %bitcast.115), channel_id=1, source_target_pairs={{0,1},{1,0},{2,3},{3,2},{4,5},{5,4},{6,7},{7,6},{8,9},{9,8},{10,11... | collective-permute-start | bytes 589832 | tf_op jit(solution)/shard_map/ppermute | solution.py:454
  73.7 49.9 %collective-permute-start.12 = (bf16[4,96,128]{2,1,0:T(8,128)(2,1)}, bf16[4,96,128]{2,1,0:T(8,128)(2,1)S(1)}, u32[]{:S(2)}, u32[]{:S(2)}) collective-permute-start(bf16[4,96,128]{2,1,0:T(8,128)(2,1)} %dynamic-slice_bitcast_fusion.1), channel_id=1, source_target_pairs={{0,1},{1,0},{2,3},{3,2},{4,5},{5,4},{6,7},{7,6},{8,9},{9,8},{10,11... | collective-permute-start | bytes 294920 | tf_op jit(solution)/shard_map/ppermute | solution.py:454
  75.0 53.4 %collective-permute-start.10 = (bf16[128,3072]{1,0:T(8,128)(2,1)}, bf16[128,3072]{1,0:T(8,128)(2,1)S(1)}, u32[]{:S(2)}, u32[]{:S(2)}) collective-permute-start(bf16[128,3072]{1,0:T(8,128)(2,1)} %get-tuple-element.69.gpre), channel_id=1, source_target_pairs={{0,1},{1,0},{2,3},{3,2},{4,5},{5,4},{6,7},{7,6},{8,9},{9,8},{10,11... | collective-permute-start | bytes 2359304 | tf_op jit(solution)/shard_map/ppermute | solution.py:454
  105.8 3.1 %collective-permute-start.1 = (f32[8,2304]{1,0:T(8,128)S(1)}, f32[8,2304]{1,0:T(8,128)S(1)}, u32[]{:S(2)}, u32[]{:S(2)}) collective-permute-start(f32[8,2304]{1,0:T(8,128)S(1)} %pad_maximum_fusion.3), channel_id=1, source_target_pairs={{1,0},{2,1},{3,2},{4,3},{5,4},{6,5},{7,6},{9,8},{10,9},{11,10},{12... | collective-permute-start | bytes 221192 | tf_op jit(solution)/shard_map/ppermute | solution.py:450
  113.4 15.0 %collective-permute-start.14 = (bf16[128,2304]{1,0:T(8,128)(2,1)}, bf16[128,2304]{1,0:T(8,128)(2,1)S(1)}, u32[]{:S(2)}, u32[]{:S(2)}) collective-permute-start(bf16[128,2304]{1,0:T(8,128)(2,1)} %get-tuple-element.60.gproj), channel_id=1, source_target_pairs={{0,1},{1,0},{2,3},{3,2},{4,5},{5,4},{6,7},{7,6},{8,9},{9,8},{10,11... | collective-permute-start | bytes 1769480 | tf_op jit(solution)/shard_map/ppermute | solution.py:454
  123.5 2.6 collective-permute-start.2
  123.7 4.7 %collective-permute-start.7 = (bf16[4,384,128]{2,1,0:T(8,128)(2,1)S(1)}, bf16[4,384,128]{2,1,0:T(8,128)(2,1)S(1)}, u32[]{:S(2)}, u32[]{:S(2)}) collective-permute-start(bf16[4,384,128]{2,1,0:T(8,128)(2,1)S(1)} %dynamic-slice_bitcast_fusion), channel_id=1, source_target_pairs={{0,1},{1,0},{2,3},{3,2},{4,5},{5,4},{6,7},{7,6},{8,9},{9,8},{10,11... | collective-permute-start | bytes 1179656 | tf_op jit(solution)/shard_map/ppermute | solution.py:454
  127.6 22.6 %collective-permute-start.3 = (f32[122,768]{1,0:T(8,128)S(1)}, f32[122,768]{1,0:T(8,128)S(1)}, u32[]{:S(2)}, u32[]{:S(2)}) collective-permute-start(f32[122,768]{1,0:T(8,128)S(1)} %add.128), channel_id=1, source_target_pairs={{0,2},{1,3},{2,0},{3,1},{4,6},{5,7},{6,4},{7,5},{8,10},{9,11},{10,... | collective-permute-start | bytes 1124360 | tf_op jit(solution)/shard_map/ppermute | solution.py:454
  141.6 93.2 %collective-permute-start.17 = (bf16[4,96,1920]{2,1,0:T(8,128)(2,1)}, bf16[4,96,1920]{2,1,0:T(8,128)(2,1)S(1)}, u32[]{:S(2)}, u32[]{:S(2)}) collective-permute-start(bf16[4,96,1920]{2,1,0:T(8,128)(2,1)} %get-tuple-element.95), channel_id=1, source_target_pairs={{0,24},{8,16},{16,8},{24,0},{1,25},{9,17},{17,9},{25,1},{2,26},{10... | collective-permute-start | bytes 4423688 | tf_op jit(solution)/shard_map/ppermute | solution.py:454
  144.0 92.4 %collective-permute-start.16 = (bf16[4,96,1920]{2,1,0:T(8,128)(2,1)}, bf16[4,96,1920]{2,1,0:T(8,128)(2,1)S(1)}, u32[]{:S(2)}, u32[]{:S(2)}) collective-permute-start(bf16[4,96,1920]{2,1,0:T(8,128)(2,1)} %get-tuple-element.96), channel_id=1, source_target_pairs={{0,16},{8,24},{16,0},{24,8},{1,17},{9,25},{17,1},{25,9},{2,18},{10... | collective-permute-start | bytes 4423688 | tf_op jit(solution)/shard_map/ppermute | solution.py:454
  144.6 93.1 %collective-permute-start.15 = (bf16[4,96,1920]{2,1,0:T(8,128)(2,1)S(1)}, bf16[4,96,1920]{2,1,0:T(8,128)(2,1)}, u32[]{:S(2)}, u32[]{:S(2)}) collective-permute-start(bf16[4,96,1920]{2,1,0:T(8,128)(2,1)S(1)} %get-tuple-element.94), channel_id=1, source_target_pairs={{0,8},{8,0},{16,24},{24,16},{1,9},{9,1},{17,25},{25,17},{2,10},{10... | collective-permute-start | bytes 4423688 | tf_op jit(solution)/shard_map/ppermute | solution.py:454
  150.3 66.1 %collective-permute-start.4 = (f32[122,768]{1,0:T(8,128)S(1)}, f32[122,768]{1,0:T(8,128)S(1)}, u32[]{:S(2)}, u32[]{:S(2)}) collective-permute-start(f32[122,768]{1,0:T(8,128)S(1)} %add.129), channel_id=1, source_target_pairs={{0,4},{1,5},{2,6},{3,7},{4,0},{5,1},{6,2},{7,3},{8,12},{9,13},{10,... | collective-permute-start | bytes 1124360 | tf_op jit(solution)/shard_map/ppermute | solution.py:454
  154.0 61.0 %collective-permute-start.26 = (bf16[4,96,384]{2,1,0:T(8,128)(2,1)S(1)}, bf16[4,96,384]{2,1,0:T(8,128)(2,1)S(1)}, u32[]{:S(2)}, u32[]{:S(2)}) collective-permute-start(bf16[4,96,384]{2,1,0:T(8,128)(2,1)S(1)} %get-tuple-element.101), channel_id=1, source_target_pairs={{0,24},{8,16},{16,8},{24,0},{1,25},{9,17},{17,9},{25,1},{2,26},{10... | collective-permute-start | bytes 884744 | tf_op jit(solution)/shard_map/ppermute | solution.py:454
  215.0 8.1 %collective-permute-start.25 = (bf16[4,96,384]{2,1,0:T(8,128)(2,1)S(1)}, bf16[4,96,384]{2,1,0:T(8,128)(2,1)S(1)}, u32[]{:S(2)}, u32[]{:S(2)}) collective-permute-start(bf16[4,96,384]{2,1,0:T(8,128)(2,1)S(1)} %get-tuple-element.102), channel_id=1, source_target_pairs={{0,16},{8,24},{16,0},{24,8},{1,17},{9,25},{17,1},{25,9},{2,18},{10... | collective-permute-start | bytes 884744 | tf_op jit(solution)/shard_map/ppermute | solution.py:454
  216.4 8.2 %collective-permute-start.24 = (bf16[4,96,384]{2,1,0:T(8,128)(2,1)S(1)}, bf16[4,96,384]{2,1,0:T(8,128)(2,1)S(1)}, u32[]{:S(2)}, u32[]{:S(2)}) collective-permute-start(bf16[4,96,384]{2,1,0:T(8,128)(2,1)S(1)} %get-tuple-element.100), channel_id=1, source_target_pairs={{0,8},{8,0},{16,24},{24,16},{1,9},{9,1},{17,25},{25,17},{2,10},{10... | collective-permute-start | bytes 884744 | tf_op jit(solution)/shard_map/ppermute | solution.py:454
  223.1 9.6 %collective-permute-start.5 = (f32[122,768]{1,0:T(8,128)S(1)}, f32[122,768]{1,0:T(8,128)S(1)}, u32[]{:S(2)}, u32[]{:S(2)}) collective-permute-start(f32[122,768]{1,0:T(8,128)S(1)} %add.130), channel_id=1, source_target_pairs={{0,8},{8,0},{16,24},{24,16},{1,9},{9,1},{17,25},{25,17},{2,10},{10... | collective-permute-start | bytes 1124360 | tf_op jit(solution)/shard_map/ppermute | solution.py:454
  225.7 16.7 %collective-permute-start.29 = (bf16[96,384]{1,0:T(8,128)(2,1)S(1)}, bf16[96,384]{1,0:T(8,128)(2,1)S(1)}, u32[]{:S(2)}, u32[]{:S(2)}) collective-permute-start(bf16[96,384]{1,0:T(8,128)(2,1)S(1)} %get-tuple-element.106), channel_id=1, source_target_pairs={{0,6},{1,7},{2,4},{3,5},{4,2},{5,3},{6,0},{7,1},{8,14},{9,15},{10,... | collective-permute-start | bytes 221192 | tf_op jit(solution)/shard_map/ppermute | solution.py:454
  232.7 11.0 %collective-permute-start.28 = (bf16[96,384]{1,0:T(8,128)(2,1)S(1)}, bf16[96,384]{1,0:T(8,128)(2,1)S(1)}, u32[]{:S(2)}, u32[]{:S(2)}) collective-permute-start(bf16[96,384]{1,0:T(8,128)(2,1)S(1)} %get-tuple-element.107), channel_id=1, source_target_pairs={{0,4},{1,5},{2,6},{3,7},{4,0},{5,1},{6,2},{7,3},{8,12},{9,13},{10,... | collective-permute-start | bytes 221192 | tf_op jit(solution)/shard_map/ppermute | solution.py:454
  234.9 11.2 %collective-permute-start.27 = (bf16[96,384]{1,0:T(8,128)(2,1)S(1)}, bf16[96,384]{1,0:T(8,128)(2,1)S(1)}, u32[]{:S(2)}, u32[]{:S(2)}) collective-permute-start(bf16[96,384]{1,0:T(8,128)(2,1)S(1)} %get-tuple-element.105), channel_id=1, source_target_pairs={{0,2},{1,3},{2,0},{3,1},{4,6},{5,7},{6,4},{7,5},{8,10},{9,11},{10,... | collective-permute-start | bytes 221192 | tf_op jit(solution)/shard_map/ppermute | solution.py:454
  236.4 11.2 %collective-permute-start.6 = (f32[122,768]{1,0:T(8,128)S(1)}, f32[122,768]{1,0:T(8,128)S(1)}, u32[]{:S(2)}, u32[]{:S(2)}) collective-permute-start(f32[122,768]{1,0:T(8,128)S(1)} %add.131), channel_id=1, source_target_pairs={{0,16},{8,24},{16,0},{24,8},{1,17},{9,25},{17,1},{25,9},{2,18},{10... | collective-permute-start | bytes 1124360 | tf_op jit(solution)/shard_map/ppermute | solution.py:454
  241.6 13.6 %collective-permute-start.20 = (bf16[96,1920]{1,0:T(8,128)(2,1)}, bf16[96,1920]{1,0:T(8,128)(2,1)S(1)}, u32[]{:S(2)}, u32[]{:S(2)}) collective-permute-start(bf16[96,1920]{1,0:T(8,128)(2,1)} %get-tuple-element.98), channel_id=1, source_target_pairs={{0,6},{1,7},{2,4},{3,5},{4,2},{5,3},{6,0},{7,1},{8,14},{9,15},{10,... | collective-permute-start | bytes 1105928 | tf_op jit(solution)/shard_map/ppermute | solution.py:454
  242.4 30.8 %collective-permute-start.19 = (bf16[96,1920]{1,0:T(8,128)(2,1)}, bf16[96,1920]{1,0:T(8,128)(2,1)}, u32[]{:S(2)}, u32[]{:S(2)}) collective-permute-start(bf16[96,1920]{1,0:T(8,128)(2,1)} %get-tuple-element.99), channel_id=1, source_target_pairs={{0,4},{1,5},{2,6},{3,7},{4,0},{5,1},{6,2},{7,3},{8,12},{9,13},{10,... | collective-permute-start | bytes 1105928 | tf_op jit(solution)/shard_map/ppermute | solution.py:454
  243.7 29.6 %collective-permute-start.18 = (bf16[96,1920]{1,0:T(8,128)(2,1)}, bf16[96,1920]{1,0:T(8,128)(2,1)}, u32[]{:S(2)}, u32[]{:S(2)}) collective-permute-start(bf16[96,1920]{1,0:T(8,128)(2,1)} %get-tuple-element.97), channel_id=1, source_target_pairs={{0,2},{1,3},{2,0},{3,1},{4,6},{5,7},{6,4},{7,5},{8,10},{9,11},{10,... | collective-permute-start | bytes 1105928 | tf_op jit(solution)/shard_map/ppermute | solution.py:454
  246.1 52.8 %collective-permute-start.30 = (bf16[96,384]{1,0:T(8,128)(2,1)S(1)}, bf16[96,384]{1,0:T(8,128)(2,1)}, u32[]{:S(2)}, u32[]{:S(2)}) collective-permute-start(bf16[96,384]{1,0:T(8,128)(2,1)S(1)} %fusion.21.refs_0_), channel_id=1, source_target_pairs={{0,8},{8,0},{16,24},{24,16},{1,9},{9,1},{17,25},{25,17},{2,10},{10... | collective-permute-start | bytes 221192 | tf_op jit(solution)/shard_map/ppermute | solution.py:454
  247.6 51.3 %collective-permute-start.31 = (bf16[96,384]{1,0:T(8,128)(2,1)S(1)}, bf16[96,384]{1,0:T(8,128)(2,1)}, u32[]{:S(2)}, u32[]{:S(2)}) collective-permute-start(bf16[96,384]{1,0:T(8,128)(2,1)S(1)} %fusion.21.refs_0_), channel_id=1, source_target_pairs={{0,16},{8,24},{16,0},{24,8},{1,17},{9,25},{17,1},{25,9},{2,18},{10... | collective-permute-start | bytes 221192 | tf_op jit(solution)/shard_map/ppermute | solution.py:454
  274.7 14.0 %collective-permute-start.21 = (bf16[96,1920]{1,0:T(8,128)(2,1)S(1)}, bf16[96,1920]{1,0:T(8,128)(2,1)S(1)}, u32[]{:S(2)}, u32[]{:S(2)}) collective-permute-start(bf16[96,1920]{1,0:T(8,128)(2,1)S(1)} %fusion.6.refs_0_), channel_id=1, source_target_pairs={{0,8},{8,0},{16,24},{24,16},{1,9},{9,1},{17,25},{25,17},{2,10},{10... | collective-permute-start | bytes 1105928 | tf_op jit(solution)/shard_map/ppermute | solution.py:454
  276.3 17.9 %collective-permute-start.22 = (bf16[96,1920]{1,0:T(8,128)(2,1)S(1)}, bf16[96,1920]{1,0:T(8,128)(2,1)S(1)}, u32[]{:S(2)}, u32[]{:S(2)}) collective-permute-start(bf16[96,1920]{1,0:T(8,128)(2,1)S(1)} %fusion.6.refs_0_), channel_id=1, source_target_pairs={{0,16},{8,24},{16,0},{24,8},{1,17},{9,25},{17,1},{25,9},{2,18},{10... | collective-permute-start | bytes 1105928 | tf_op jit(solution)/shard_map/ppermute | solution.py:454
  276.9 17.4 %collective-permute-start.23 = (bf16[96,1920]{1,0:T(8,128)(2,1)S(1)}, bf16[96,1920]{1,0:T(8,128)(2,1)S(1)}, u32[]{:S(2)}, u32[]{:S(2)}) collective-permute-start(bf16[96,1920]{1,0:T(8,128)(2,1)S(1)} %fusion.6.refs_0_), channel_id=1, source_target_pairs={{0,24},{8,16},{16,8},{24,0},{1,25},{9,17},{17,9},{25,1},{2,26},{10... | collective-permute-start | bytes 1105928 | tf_op jit(solution)/shard_map/ppermute | solution.py:454
  288.6 10.3 %collective-permute-start.32 = (bf16[96,384]{1,0:T(8,128)(2,1)S(1)}, bf16[96,384]{1,0:T(8,128)(2,1)S(1)}, u32[]{:S(2)}, u32[]{:S(2)}) collective-permute-start(bf16[96,384]{1,0:T(8,128)(2,1)S(1)} %fusion.21.refs_0_), channel_id=1, source_target_pairs={{0,24},{8,16},{16,8},{24,0},{1,25},{9,17},{17,9},{25,1},{2,26},{10... | collective-permute-start | bytes 221192 | tf_op jit(solution)/shard_map/ppermute | solution.py:454
  (45 other events, 495.5 us)
Sparse Core Ops, SparseCore 0:
  22.7 27.6 all-gather.4
  68.4 26.6 all-gather.6

commit v2 on v1

v2 whole, which is shorter than its diff:
```python
from functools import partial
import math

import jax
import jax.numpy as jnp
import numpy as np
from jax import lax
from jax.experimental import pallas as pl
from jax.experimental.pallas import tpu as pltpu
from jax.sharding import PartitionSpec as P

EPSILON = 1e-05
HIGHEST = lax.Precision.HIGHEST
MIN_DECAY = math.log(100.0) / 1.5
MAX_DECAY = math.log(100.0) / 0.3
F32 = jnp.float32
BF16 = jnp.bfloat16
RIM = 16
VMEM_LIMIT = 26 * 1024 * 1024
GELU_C = math.sqrt(2.0 / math.pi)
GELU_A = 0.044715


def params():
    return pltpu.CompilerParams(vmem_limit_bytes=VMEM_LIMIT)


def cost(micros):
    return pl.CostEstimate(flops=0, bytes_accessed=int(micros * 3.0e6), transcendentals=0)


def single(kernel, name, micros, outs, scalars, arrays, after=(), scratch=()):
    count, skip = 1 + len(arrays), len(after)

    def body(*refs):
        kernel(*refs[:count], *refs[count + skip :])

    made = pl.pallas_call(
        body,
        grid=(1,),
        out_shape=tuple(outs),
        in_specs=[smem()] + [whole(v.shape) for v in arrays]
        + [pl.BlockSpec(memory_space=pl.ANY)] * skip,
        out_specs=tuple(whole(v.shape) for v in outs),
        scratch_shapes=list(scratch),
        compiler_params=params(),
        cost_estimate=cost(micros),
        name=name,
    )(scalars, *arrays, *after)
    return made


def smem():
    return pl.BlockSpec(memory_space=pltpu.SMEM)


def whole(shape):
    return pl.BlockSpec(shape, lambda *_: (0,) * len(shape))


def dot(left, right):
    return jnp.dot(left, right, preferred_element_type=F32)


def dot_t(left, right):
    return lax.dot_general(left, right, (((1,), (1,)), ((), ())), preferred_element_type=F32)


def high_low(values):
    high = values.astype(BF16)
    return high, (values - high.astype(F32)).astype(BF16)


def doc_at(meta, ndocs, position):
    total = jnp.int32(-1)
    for d in range(ndocs):
        total = total + (position >= meta[4 + d]).astype(jnp.int32)
    return total


def doc_start(meta, ndocs, position):
    found = jnp.int32(0)
    for d in range(ndocs):
        found = jnp.where(position >= meta[4 + d], meta[4 + d], found)
    return found


def doc_end(meta, ndocs, position, length):
    found = jnp.int32(length)
    for d in reversed(range(ndocs)):
        found = jnp.where(position < meta[4 + d], meta[4 + d], found)
    return found


def doc_column(meta, ndocs, first, rows):
    position = first + lax.broadcasted_iota(jnp.int32, (rows, 1), 0)
    total = jnp.full((rows, 1), -1, jnp.int32)
    for d in range(ndocs):
        total = total + (position >= meta[4 + d]).astype(jnp.int32)
    return position, total


def block_tables(block):
    period = 2 * block
    packed = np.arange(period)
    freq = np.where(packed <= block, packed, packed - block)
    places = np.arange(period)
    angle = 2.0 * np.pi / period * (freq[:, None] * places[None, :] % period)
    real = (packed <= block)[:, None]
    forward = np.where(real, np.cos(angle), -np.sin(angle))
    scaling = np.where((packed == 0) | (packed == block), 1.0, 2.0) / period
    inverse = (forward * scaling[:, None]).T[block:]
    left = forward[:, :block]

    def split(table):
        table = table.astype(np.float32)
        high = table.astype(BF16)
        return high, (table - high.astype(np.float32)).astype(BF16)

    lh, ll = split(left)
    ih, il = split(inverse)
    return dict(
        left2=np.concatenate([lh, ll], 1),
        left3=np.concatenate([lh, lh, ll], 1),
        inv3=np.concatenate([ih, ih, il], 1),
        invt2=np.concatenate([ih.T, il.T], 1),
        leftt3=np.concatenate([lh.T, lh.T, ll.T], 1),
    )


def spectrum2(table, signal):
    return dot(table, jnp.concatenate([signal, signal], axis=0))


def spectrum3(table, values):
    high, low = high_low(values)
    return dot(table, jnp.concatenate([high, low, high], axis=0))


def masked(signal, mask):
    return jnp.where(mask, signal.astype(F32), 0.0).astype(BF16)


def first_row(shape):
    return lax.broadcasted_iota(jnp.int32, shape, 0) == 0


def times(left, right):
    half = left.shape[0] // 2
    lre, lim = left[:half], left[half:]
    rre, rim = right[:half], right[half:]
    row = first_row(lre.shape)
    edge = jnp.where(row, 0.0, lim)
    return lre * rre - edge * rim, edge * rre + jnp.where(row, lim, lre) * rim


def times_back(left, grad):
    half = left.shape[0] // 2
    lre, lim = left[:half], left[half:]
    gre, gim = grad[:half], grad[half:]
    row = first_row(lre.shape)
    edge = jnp.where(row, 0.0, lim)
    return lre * gre + edge * gim, jnp.where(row, lim, lre) * gim - edge * gre


def add_spec(acc, pair):
    half = acc.shape[0] // 2
    acc[:half, :] += pair[0]
    acc[half:, :] += pair[1]


def set_spec(acc, pair):
    half = acc.shape[0] // 2
    acc[:half, :] = pair[0]
    acc[half:, :] = pair[1]


def normalise(values):
    average = jnp.mean(values, axis=-1, keepdims=True)
    centred = values - average
    spread = jnp.mean(centred * centred, axis=-1, keepdims=True)
    rstd = lax.rsqrt(spread + EPSILON)
    return centred * rstd, rstd


def row_of(ref):
    return ref[...].astype(F32).reshape(1, -1)


def part_of(ref, first, size):
    return ref[pl.ds(first, size)].astype(F32).reshape(1, -1)


def write_strips(out, first, source, count, rows, core):
    for p in range(2):
        for z in range(count):
            out[pl.ds(first + (p * count + z) * rows, rows), :] = source[
                pl.ds(pl.multiple_of((2 * z + (core ^ p)) * rows, 16), rows), :
            ]


def write_tiles(out, first, source, start, count):
    tokens = source.shape[0]
    for t in range(count):
        out[pl.ds(first + t * tokens, tokens), :] = source[
            :, pl.ds(pl.multiple_of(start + t * 128, 128), 128)
        ]


def front_kernel(ndocs, packed, meta, tokens, rim, cot, gain, bias, weight, wbias, taps, tbias,
                 proj_ref, normt_ref, mixed_ref, carried_ref, turned):
    block, width = tokens.shape
    taps_n = taps.shape[0]
    ext = jnp.concatenate([rim[...], tokens[...]], axis=0).astype(F32)
    hat, _ = normalise(ext)
    normed = hat * row_of(gain) + row_of(bias)
    turned[...] = normed[RIM:].T.astype(BF16)
    if packed:
        chips = packed
        write_strips(normt_ref, 0, turned, chips, width // (2 * chips), meta[1])
        write_tiles(normt_ref, width, cot, 0, width // 128)
    else:
        normt_ref[...] = turned[...]
    low = normed.astype(BF16)
    base = meta[0] * block
    position, ids = doc_column(meta, ndocs, base, block)
    masks = []
    for k in range(taps_n):
        _, back = doc_column(meta, ndocs, base - k, block)
        masks.append(((back == ids) & (position >= k)).astype(F32))
    for third in range(3):
        cols = slice(third * width, (third + 1) * width)
        proj_ref[:, cols] = dot(low, weight[:, cols]) + part_of(wbias, third * width, width)
        total = part_of(tbias, third * width, width)
        for k in range(taps_n):
            moved = proj_ref[pl.ds(RIM - k, block), cols]
            total = total + taps[k : k + 1, cols].astype(F32) * moved * masks[k]
        mixed_ref[:, cols] = total
    carried_ref[...] = (mixed_ref[:, 2 * width :] * mixed_ref[:, width : 2 * width]).astype(BF16)


def lag_kernel(taps, left3, out):
    blocks = taps.shape[0]
    sign = 1.0 - 2.0 * (lax.broadcasted_iota(jnp.int32, (out.shape[1], 1), 0) % 2).astype(F32)

    def step(j, carry):
        spec = spectrum3(left3[...], taps[j])
        out[j] = out[j] + sign * spec

        @pl.when(j + 1 < blocks)
        def _():
            out[j + 1] = spec

        return carry

    out[0] = jnp.zeros(out.shape[1:], F32)
    lax.fori_loop(0, blocks, step, 0)


def fill(meta, parts, held, ahead):
    own, sibling = parts
    chips = own.shape[0]
    for k in range(chips):
        z = meta[2] + k if ahead else meta[2] - k

        @pl.when((z >= 0) & (z < chips))
        def _():
            held[2 * z + meta[1]] = own[k]
            held[2 * z + 1 - meta[1]] = sibling[k]


def conv_kernel(ndocs, nparts, meta, *refs):
    parts, (lags, left2, inv3, out, acc), rest = refs[:nparts], refs[nparts : nparts + 5], refs[nparts + 5 :]
    signal = parts[0]
    if nparts > 1:
        (signal,) = rest
        fill(meta, parts, signal, False)
    block = signal.shape[1]
    me = meta[0]
    base = me * block
    start = doc_start(meta, ndocs, base)
    low_block = start // block
    _, ids = doc_column(meta, ndocs, base, block)
    first_doc = doc_at(meta, ndocs, base)
    last_doc = doc_at(meta, ndocs, base + block - 1)
    own = signal[me]
    spec = spectrum2(left2[...], masked(own, ids == first_doc))
    set_spec(acc, times(lags[0], spec))

    def cross(s, carry):
        position = s * block + lax.broadcasted_iota(jnp.int32, (block, 1), 0)
        spec = spectrum2(left2[...], masked(signal[s], position >= start))
        add_spec(acc, times(lags[me - s], spec))
        return carry

    lax.fori_loop(low_block, me, cross, 0)
    out[...] = jnp.where(ids == first_doc, spectrum3(inv3[...], acc[...]), 0.0)

    def inner(d, carry):
        spec = spectrum2(left2[...], masked(own, ids == d))
        set_spec(acc, times(lags[0], spec))
        out[...] += jnp.where(ids == d, spectrum3(inv3[...], acc[...]), 0.0)
        return carry

    lax.fori_loop(first_doc + 1, last_doc + 1, inner, 0)


def mlp_kernel(packed, meta, tokens, cot, conv, carried, gate_out, fbias, w_out, b_out, gain, shift,
               up, up_bias, down, down_bias, *refs):
    (output, gresid, glong, glong16, ggate, smalls), refs = refs[:6], refs[6:]
    (e1, e1_send, e2, e2_send) = refs[:4]
    if packed:
        refs = refs[4:]
    else:
        actt, gpre_out, n2t_out, gatedt_out, gmix_out = refs[:5]
        refs = refs[5:]
    resid, n2, hat2, rstd2, oacc, gacc, ubias, ubias_grad, turned, rows_held = refs
    j = pl.program_id(0)
    block, width = tokens.shape
    ff = up.shape[1]
    core, x, y = meta[1], meta[3] % 2, meta[3] // 2
    chips = packed
    if packed:
        share, big = width // (2 * chips), ff // 2
        half = big // 2
        slot = chips * (half + share)

    @pl.when(j == 0)
    def _():
        ubias[...] = row_of(up_bias)
        long_out = conv[...] + row_of(fbias) * carried[...].astype(F32)
        gated = long_out * gate_out[...]
        gated_t = gated.T.astype(BF16)
        r = tokens[...].astype(F32) + dot(gated.astype(BF16), w_out[...]) + row_of(b_out)
        resid[...] = r
        hat, rstd = normalise(r)
        hat2[...] = hat
        rstd2[...] = rstd
        normed = hat * row_of(gain) + row_of(shift)
        n2[...] = normed.astype(BF16)
        oacc[...] = jnp.zeros_like(oacc)
        gacc[...] = jnp.zeros_like(gacc)
        if packed:
            turned[...] = gated_t
            for dest in (e1, e1_send):
                for p in range(2):
                    for z in range(chips):
                        dest[pl.ds(p * slot + chips * half + z * share, share), :] = turned[
                            pl.ds(pl.multiple_of((2 * z + (core ^ p)) * share, 16), share), :
                        ]
            turned[...] = normed.T.astype(BF16)
            for dest in (e2, e2_send):
                write_strips(dest, 0, turned, chips, share, core)
        else:
            gatedt_out[...] = gated_t
            n2t_out[...] = normed.T.astype(BF16)

    bias = ubias[:, pl.ds(pl.multiple_of(j * ff, 128), ff)]
    pre = dot(n2[...], up[...]) + bias
    sq = pre * pre
    th = jnp.tanh(GELU_C * (pre * (1.0 + GELU_A * sq)))
    act = 0.5 * pre * (1.0 + th)
    slope = 0.5 * (1.0 + th) + 0.5 * pre * (1.0 - th * th) * (
        GELU_C * (1.0 + 3.0 * GELU_A * sq)
    )
    if packed:
        turned[...] = act.T.astype(BF16)
        for p in range(2):
            for dest, side in ((e1, x), (e1_send, 1 - x)):
                dest[pl.ds(pl.multiple_of(p * slot + j * half, 16), half), :] = turned[
                    pl.ds(pl.multiple_of((core ^ p) * big + side * half, 16), half), :
                ]
    else:
        actt[...] = act.T.astype(BF16)
    oacc[...] += dot(act.astype(BF16), down[...])
    gpre = (dot_t(cot[...], down[...]) * slope).astype(BF16)
    if packed:
        rows_held[...] = gpre
        per = chips // 2
        for t in range(ff // 128):
            place = pl.ds(pl.multiple_of(width + ((j % per) * (ff // 128) + t) * block, 16), block)
            tile = gpre[:, t * 128 : (t + 1) * 128]

            @pl.when(j // per == y)
            def _():
                e2[place, :] = tile

            @pl.when(j // per != y)
            def _():
                e2_send[place, :] = tile
    else:
        gpre_out[...] = gpre
    ubias_grad[:, pl.ds(pl.multiple_of(j * ff, 128), ff)] = jnp.sum(
        gpre.astype(F32), axis=0, keepdims=True
    )
    gacc[...] += dot_t(gpre, up[...])

    @pl.when(j == pl.num_programs(0) - 1)
    def _():
        output[...] = (resid[...] + oacc[...] + row_of(down_bias)).astype(BF16)
        top = cot[...].astype(F32)
        gn = gacc[...]
        hat = hat2[...]
        q = gn * row_of(gain)
        mean_q = jnp.mean(q, axis=-1, keepdims=True)
        mean_qh = jnp.mean(q * hat, axis=-1, keepdims=True)
        gr = top + (q - mean_q - hat * mean_qh) * rstd2[...]
        gresid[...] = gr
        gm = gr.astype(BF16)
        if packed:
            rows_held[...] = gm
            for dest, side in ((e1, x), (e1_send, 1 - x)):
                write_tiles(dest, 2 * slot, rows_held, side * (width // 2), width // 256)
        else:
            gmix_out[...] = gm
        gg = dot_t(gm, w_out[...])
        c = carried[...].astype(F32)
        long_out = conv[...] + row_of(fbias) * c
        gl = gg * gate_out[...]
        glong[...] = gl
        glong16[...] = gl.astype(BF16)
        ggate[...] = gg * long_out
        rows = [
            jnp.sum(top, axis=0, keepdims=True),
            jnp.sum(gn * hat, axis=0, keepdims=True),
            jnp.sum(gn, axis=0, keepdims=True),
            jnp.sum(gm.astype(F32), axis=0, keepdims=True),
            jnp.sum(gl * c, axis=0, keepdims=True),
        ]
        lanes = smalls.shape[1]
        for i, made in enumerate(rows):
            smalls[i : i + 1, :width] = made
            smalls[i : i + 1, width:] = jnp.zeros((1, lanes - width), F32)
        for i in range(ubias_grad.shape[1] // lanes):
            smalls[len(rows) + i : len(rows) + i + 1, :] = ubias_grad[:, i * lanes : (i + 1) * lanes]


def conv_back_kernel(ndocs, length, nparts, meta, *refs):
    parts, refs = refs[:nparts], refs[nparts:]
    (own_grad, lags, invt2, leftt3, fbias, gate_in, values, ggate, short_gate, short_in,
     short_values, for_in, for_values, rim, acc) = refs[:15]
    grads = parts[0]
    if nparts > 1:
        grads = refs[15]
        fill(meta, parts, grads, True)
    block = grads.shape[1]
    me = meta[0]
    base = me * block
    _, ids = doc_column(meta, ndocs, base, block)
    first_doc = doc_at(meta, ndocs, base)
    last_doc = doc_at(meta, ndocs, base + block - 1)
    last_block = (doc_end(meta, ndocs, base + block - 1, length) - 1) // block
    own = grads[me]
    spec = spectrum2(invt2[...], masked(own, ids == last_doc))
    set_spec(acc, times_back(lags[0], spec))

    def cross(t, carry):
        _, far = doc_column(meta, ndocs, t * block, block)
        spec = spectrum2(invt2[...], masked(grads[t], far == last_doc))
        add_spec(acc, times_back(lags[t - me], spec))
        return carry

    lax.fori_loop(me + 1, last_block + 1, cross, 0)
    for_in[...] = jnp.where(ids == last_doc, spectrum3(leftt3[...], acc[...]), 0.0)

    def inner(d, carry):
        spec = spectrum2(invt2[...], masked(own, ids == d))
        set_spec(acc, times_back(lags[0], spec))
        for_in[...] += jnp.where(ids == d, spectrum3(leftt3[...], acc[...]), 0.0)
        return carry

    lax.fori_loop(first_doc, last_doc, inner, 0)
    total = for_in[...] + row_of(fbias) * own_grad[...]
    for_in[...] = total * values[...]
    for_values[...] = total * gate_in[...]
    reach = short_gate.shape[0] - 1
    for third, (grad, taps) in enumerate(
        ((ggate, short_gate), (for_in, short_in), (for_values, short_values))
    ):
        rows = [jnp.zeros((8 - reach, grad.shape[1]), F32)]
        for p in range(reach):
            made = jnp.zeros((1, grad.shape[1]), F32)
            for k in range(1, reach + 1):
                t = p - reach + k
                if 0 <= t < reach:
                    same = doc_at(meta, ndocs, base - reach + p) == doc_at(meta, ndocs, base + t)
                    keep = (same & (base > 0)).astype(F32)
                    made = made + taps[k : k + 1, :].astype(F32) * grad[t : t + 1, :] * keep
            rows.append(made)
        rim[third] = jnp.concatenate(rows, axis=0)


def taps_grad_kernel(ndocs, nparts, meta, *refs):
    parts, refs = refs[:nparts], refs[nparts:]
    own_grad, left2, invt2, leftt3, out, win, gspec = refs[:7]
    signal = parts[0]
    if nparts > 1:
        signal = refs[7]
        fill(meta, parts, signal, False)
    blocks, block = signal.shape[0], signal.shape[1]
    me = meta[0]
    base = me * block
    start = doc_start(meta, ndocs, base)
    low_block = start // block
    _, ids = doc_column(meta, ndocs, base, block)
    first_doc = doc_at(meta, ndocs, base)
    last_doc = doc_at(meta, ndocs, base + block - 1)
    sign = 1.0 - 2.0 * (lax.broadcasted_iota(jnp.int32, (2 * block, 1), 0) % 2).astype(F32)
    own = signal[me]
    grad = own_grad[...]
    out[...] = jnp.zeros_like(out)
    win[me - low_block + 1] = jnp.zeros(win.shape[1:], F32)
    gspec[...] = spectrum2(invt2[...], masked(grad, ids == first_doc))
    spec = spectrum2(left2[...], masked(own, ids == first_doc))
    set_spec(win.at[0], times_back(spec, gspec[...]))

    def inner(d, carry):
        spec = spectrum2(left2[...], masked(own, ids == d))
        back = spectrum2(invt2[...], masked(grad, ids == d))
        add_spec(win.at[0], times_back(spec, back))
        return carry

    lax.fori_loop(first_doc + 1, last_doc + 1, inner, 0)

    def cross(s, carry):
        position = s * block + lax.broadcasted_iota(jnp.int32, (block, 1), 0)
        spec = spectrum2(left2[...], masked(signal[s], position >= start))
        set_spec(win.at[me - s], times_back(spec, gspec[...]))
        return carry

    lax.fori_loop(low_block, me, cross, 0)

    def emit(k, carry):
        out[k] = spectrum3(leftt3[...], win[k + 1] + sign * win[k])
        return carry

    lax.fori_loop(0, me - low_block + 1, emit, 0)


def short_back_kernel(ndocs, packed, meta, ggate, for_in, for_values, rim, proj, taps,
                      gproj_ref, smalls, *sends):
    block, width = ggate.shape
    taps_n = taps.shape[0]
    base = meta[0] * block
    position, ids = doc_column(meta, ndocs, base, block)
    masks = []
    for k in range(taps_n):
        _, back = doc_column(meta, ndocs, base - k, block)
        masks.append(((back == ids) & (position >= k)).astype(F32))
    row = lax.broadcasted_iota(jnp.int32, (block, 1), 0)
    ahead = []
    for k in range(1, taps_n):
        _, later = doc_column(meta, ndocs, base + k, block)
        ahead.append(((later == ids) & (row < block - k)).astype(F32))
    bias_rows, weight_rows, short_rows = [], [], []
    for third, grad_ref in enumerate((ggate, for_in, for_values)):
        cols = slice(third * width, (third + 1) * width)
        grad = grad_ref[...]
        total = taps[0:1, cols].astype(F32) * grad
        weights = [jnp.sum(grad * proj[pl.ds(RIM, block), cols], axis=0, keepdims=True)]
        for k in range(1, taps_n):
            moved = pltpu.roll(grad, block - k, 0) * ahead[k - 1]
            total = total + taps[k : k + 1, cols].astype(F32) * moved
            weights.append(
                jnp.sum(grad * masks[k] * proj[pl.ds(RIM - k, block), cols], axis=0, keepdims=True)
            )
        tail = jnp.concatenate([jnp.zeros((block - 8, width), F32), rim[third]], axis=0)
        low = (total + tail).astype(BF16)
        gproj_ref[:, cols] = low
        bias_rows.append(jnp.sum(low.astype(F32), axis=0, keepdims=True))
        short_rows.append(jnp.sum(grad, axis=0, keepdims=True))
        weight_rows.append(weights)
    rows = bias_rows + [weight_rows[t][k] for k in range(taps_n) for t in range(3)] + short_rows
    pad = smalls.shape[0] - len(rows)
    smalls[...] = jnp.concatenate(rows + [jnp.zeros((pad, width), F32)], axis=0)
    if packed:
        x = meta[3] % 2
        half = 3 * width // 2
        for dest, side in zip(sends, (x, 1 - x)):
            write_tiles(dest, 0, gproj_ref, side * half, half // 128)


def tail_kernel(meta, gproj, weight, tokens, gain, gresid, others, out, smalls):
    gn = dot_t(gproj[...], weight[...])
    hat, rstd = normalise(tokens[...].astype(F32))
    q = gn * row_of(gain)
    mean_q = jnp.mean(q, axis=-1, keepdims=True)
    mean_qh = jnp.mean(q * hat, axis=-1, keepdims=True)
    out[...] = gresid[...] + (q - mean_q - hat * mean_qh) * rstd
    smalls[...] = others[...]
    count = smalls.shape[0]
    smalls[count - 2 : count - 1, :] = jnp.sum(gn * hat, axis=0, keepdims=True)
    smalls[count - 1 :, :] = jnp.sum(gn, axis=0, keepdims=True)


def filter_taps(first, first_bias, second, second_bias, third, third_bias, last, sine_freq, length):
    lags = jnp.arange(length)
    bands = (first.shape[0] - 1) // 2
    moment = lags.astype(F32) / (length - 1)
    band_freq = jnp.linspace(0.0001, bands - 1, bands, dtype=F32)
    phase = 2.0 * math.pi / length * lags.astype(F32)
    angles = phase[:, None] * band_freq[None, :]
    features = jnp.concatenate([moment[:, None], jnp.cos(angles), -jnp.sin(angles)], axis=1)
    hidden = jnp.sin(sine_freq * (jnp.dot(features, first, precision=HIGHEST) + first_bias))
    hidden = jnp.sin(sine_freq * (jnp.dot(hidden, second, precision=HIGHEST) + second_bias))
    hidden = jnp.sin(sine_freq * (jnp.dot(hidden, third, precision=HIGHEST) + third_bias))
    rates = jnp.linspace(MIN_DECAY, MAX_DECAY, last.shape[1], dtype=F32)
    window = jnp.exp(-moment[:, None] * rates[None, :])
    return jnp.dot(hidden, last, precision=HIGHEST) * window


def sine_pair(values):
    turns = jnp.floor(values * (2.0 / math.pi) + 0.5)
    rest = values - turns * 1.5703125
    rest = rest - turns * 4.837512969970703125e-4
    rest = rest - turns * 7.549789948768648e-8
    sq = rest * rest
    s = ((-1.9515295891e-4 * sq + 8.3321608736e-3) * sq - 1.6666654611e-1) * sq * rest + rest
    c = ((2.443315711809948e-5 * sq - 1.388731625493765e-3) * sq + 4.166664568298827e-2) * sq * sq
    c = c - 0.5 * sq + 1.0
    quarter = turns.astype(jnp.int32)
    odd = (quarter & 1) == 1
    half = (quarter & 2) == 2
    first = jnp.where(odd, c, s)
    second = jnp.where(odd, s, c)
    return jnp.where(half, -first, first), jnp.where(half ^ odd, -second, second)


def exact_dot(weights, values):
    high = values.astype(BF16)
    rest = values - high.astype(F32)
    middle = rest.astype(BF16)
    low = (rest - middle.astype(F32)).astype(BF16)
    return dot(weights, high) + (dot(weights, middle) + dot(weights, low))


def feature_table(length, bands):
    lags = np.arange(length).astype(np.float32)
    moment = lags / np.float32(length - 1)
    freq = np.linspace(0.0001, bands - 1, bands).astype(np.float32)
    phase = np.float32(2.0 * math.pi / length) * lags
    angles = (phase[:, None] * freq[None, :]).astype(np.float64)
    table = np.concatenate(
        [moment[:, None].astype(np.float64), np.cos(angles), -np.sin(angles)], axis=1
    )
    return np.pad(table.astype(np.float32), ((0, 0), (0, -table.shape[1] % 8))).T


def decay_window(width, length):
    moment = lax.broadcasted_iota(jnp.int32, (length, 1), 0).astype(F32) / (length - 1)
    step = (MAX_DECAY - MIN_DECAY) / (width - 1)
    rates = MIN_DECAY + step * lax.broadcasted_iota(jnp.int32, (1, width), 1).astype(F32)
    return jnp.exp(-moment * rates)


def turned_column(ref):
    return jnp.broadcast_to(row_of(ref), (8, ref.shape[0])).T[:, :1]


def filter_kernel(meta, table, first, b1, second, b2, third, b3, last, freq, left3,
                  lags, window, act, slope, pre, a3):
    blocks, period, width = lags.shape
    block = period // 2
    length = blocks * block
    fwidth = freq.shape[0]
    scale = turned_column(freq)
    hidden = table[...]
    pad = table.shape[0] - first.shape[0]
    firsts = jnp.concatenate([first[...].astype(F32), jnp.zeros((pad, fwidth), F32)], axis=0)
    for i, (weight, bias) in enumerate(
        ((firsts, b1), (second[...].astype(F32), b2), (third[...].astype(F32), b3))
    ):
        u = exact_dot(weight.T.astype(BF16), hidden) + turned_column(bias)
        hidden, cosine = sine_pair(scale * u)
        rows = slice(i * fwidth, (i + 1) * fwidth)
        act[rows, :] = hidden
        slope[rows, :] = cosine
        pre[rows, :] = u
    a3[...] = hidden.T
    window[...] = decay_window(width, length)
    sign = 1.0 - 2.0 * (lax.broadcasted_iota(jnp.int32, (period, 1), 0) % 2).astype(F32)
    before = None
    for j in range(blocks):
        part = a3[j * block : (j + 1) * block, :]
        high = part.astype(BF16)
        rest = part - high.astype(F32)
        middle = rest.astype(BF16)
        low = (rest - middle.astype(F32)).astype(BF16)
        lhs = jnp.concatenate([high, middle, low], axis=1)
        rhs = jnp.concatenate([last[...]] * 3, axis=0)
        taps = dot(lhs, rhs) * window[j * block : (j + 1) * block, :]
        spec = spectrum3(left3[...], taps)
        lags[j] = sign * spec if before is None else before + sign * spec
        before = spec


def filter_back_kernel(meta, grads, window, act, slope, pre, table, first, second, third, last,
                       freq, others, mine, send, packed):
    blocks, block, width = grads.shape
    length = blocks * block
    fwidth = freq.shape[0]
    scale = turned_column(freq)
    core = meta[1]
    weighted = grads[...].reshape(length, width) * window[...]
    wh, wl = high_low(weighted)
    ah, al = high_low(act[2 * fwidth :, :])
    packed[...] = jnp.zeros_like(packed)
    packed[:fwidth, :width] = dot(ah, wh) + (dot(ah, wl) + dot(al, wh))
    packed[fwidth : fwidth + others.shape[0], :] = others[...]
    back = dot_t(last[...], wh) + dot_t(last[...], wl)
    ones = jnp.ones((8, length), BF16)

    def wide_t(left, right):
        lh, ll = high_low(left)
        rh, rl = high_low(right)
        return dot_t(lh, rh) + (dot_t(lh, rl) + dot_t(ll, rh))

    def sums(values):
        high, low = high_low(values)
        return (dot_t(ones, high) + dot_t(ones, low))[:1]

    freq_total = jnp.zeros((1, fwidth), F32)
    place = width
    for i, weight in ((2, third), (1, second), (0, first)):
        rows = slice(i * fwidth, (i + 1) * fwidth)
        step = back * slope[rows, :]
        freq_total = freq_total + sums(step * pre[rows, :])
        step = step * scale
        below = act[(i - 1) * fwidth : i * fwidth, :] if i else table[...]
        made = wide_t(below, step)
        packed[: made.shape[0], place : place + fwidth] = made
        packed[fwidth + others.shape[0] + i : fwidth + others.shape[0] + i + 1, :fwidth] = sums(step)
        place += fwidth
        if i:
            high, low = high_low(step)
            back = dot(weight[...], high) + dot(weight[...], low)
    at = fwidth + others.shape[0] + 3
    packed[at : at + 1, :fwidth] = freq_total
    half = packed.shape[0] // 2
    for side in range(2):

        def store(dest):
            dest[...] = packed[side * half : (side + 1) * half, :]

        pick(core == side, mine, send, store)


def shift(block, axis, distance):
    devices = range(lax.axis_size(axis))
    return lax.ppermute(block, axis, [(i - distance, i) for i in devices if i - distance in devices])


def swap(block, axis, mask):
    return lax.ppermute(block, axis, [(i, i ^ mask) for i in range(lax.axis_size(axis))])


def butterfly(values):
    for axis in ("seq", "rows"):
        mask = 1
        while mask < lax.axis_size(axis):
            values = values + swap(values, axis, mask)
            mask *= 2
    return values


def collect_kernel(meta, *refs):
    out = refs[-1]
    for k, ref in enumerate(refs[:-1]):
        out[k] = ref[...]


def along_row(meta, block, blocks, ahead, after):
    if blocks > 8:
        return (lax.all_gather(block, "seq", axis=0, tiled=False),)
    step = -2 if ahead else 2
    near = [block] + [shift(block, "seq", step * k) for k in range(1, blocks // 2)]
    (own,) = single(
        collect_kernel, "collect", 0.5, [jax.ShapeDtypeStruct((len(near),) + block.shape, block.dtype)],
        meta, near, after,
    )
    return own, swap(own, "seq", 1)


def joined_left(sources, first, slot, rows):
    return jnp.concatenate(
        [ref[pl.ds(first + (i % 2) * slot, rows), :] for i, ref in enumerate(sources)], axis=1
    )


def joined_right(sources, first, block, count):
    return jnp.concatenate(
        [
            jnp.concatenate([ref[pl.ds(first + t * block, block), :] for t in range(count)], axis=1)
            for ref in sources
        ],
        axis=0,
    )


def pick(flag, keep, send, store):
    @pl.when(flag)
    def _():
        store(keep)

    @pl.when(jnp.logical_not(flag))
    def _():
        store(send)


def down_out_kernel(chips, meta, *refs):
    acts, early, (keep, send) = refs[:4], refs[4:8], refs[8:]
    block = acts[0].shape[1]
    share = keep.shape[1]
    width = early[0].shape[0] // 2
    half = 2 * share
    slot = chips * (half + share)
    y, chip = meta[3] // 2, meta[2]
    made = dot(
        joined_left(acts, 0, slot, chips * half), joined_right(early, width, block, width // 128)
    ).astype(BF16)
    out = dot(
        joined_left(acts, chips * half, slot, chips * share),
        joined_right(acts, 2 * slot, block, width // 256),
    ).astype(BF16)
    part = share // 2
    for side in range(2):

        def store(dest):
            for z in range(chips):
                at = z ^ chip
                first = z * half + side * share
                dest[at, :, :width] = made[first : first + share]
                rows = out[z * share + side * part : z * share + (side + 1) * part]
                dest[at, :part, width : width + 128] = rows[:, :128]
                dest[at, part:, width : width + 128] = rows[:, 128:256]
                dest[at, :part, width + 128 :] = rows[:, 256:]
                dest[at, part:, width + 128 :] = jnp.zeros((part, 128), BF16)

        pick(y == side, keep, send, store)


def up_kernel(chips, meta, *refs):
    acts, (keep, send) = refs[:4], refs[4:]
    block = acts[0].shape[1]
    share, width = keep.shape[1:]
    x, chip = meta[3] % 2, meta[2]
    left = joined_left(acts, 0, width // 2, width // 2)
    for side in range(2):
        right = joined_right(acts, width + side * width, block, width // 128)
        made = dot(left, right).astype(BF16)

        def store(dest):
            for z in range(chips):
                dest[z ^ chip] = made[z * share : (z + 1) * share]

        pick(x == side, keep, send, store)


def in_kernel(chips, meta, *refs):
    acts, early, (keep, send) = refs[:4], refs[4:8], refs[8:]
    block = acts[0].shape[1]
    part, cols = keep.shape[1:]
    width = early[0].shape[0] // 2
    y, chip = meta[3] // 2, meta[2]
    made = dot(
        joined_left(early, 0, width // 2, width // 2), joined_right(acts, 0, block, cols // 128)
    ).astype(BF16)
    for side in range(2):

        def store(dest):
            for z in range(chips):
                first = (2 * z + side) * part
                dest[z ^ chip] = made[first : first + part]

        pick(y == side, keep, send, store)


def merge_kernel(meta, keep, got, own, *sends):
    own[...] = keep[0].astype(F32) + got[0].astype(F32)
    for j, dest in enumerate(sends):
        dest[...] = (keep[j + 1].astype(F32) + got[j + 1].astype(F32)).astype(BF16)


def spread_out(meta, keep, send, mask):
    chips, rows, cols = keep.shape
    outs = [jax.ShapeDtypeStruct((rows, cols), F32)]
    outs += [jax.ShapeDtypeStruct((rows, cols), BF16)] * (chips - 1)
    own, *sends = single(merge_kernel, "merge", 1.0, outs, meta, [keep, swap(send, "rows", mask)])
    for j, block in enumerate(sends):
        own = own + swap(block, "seq", 2 * (j + 1)).astype(F32)
    own = own.astype(BF16)
    return [own] + [swap(own, "rows", j) for j in (1, 2, 3)]


def unpack_kernel(taps_n, fwidth, feats, meta, first_half, second_half, late, *outs):
    (gain1, shift1, in_bias, short_weight, short_bias, f1, f1b, f2, f2b, f3, f3b, flast, freq,
     fbias, obias, gain2, shift2, ubias, dbias) = outs
    width = gain1.shape[0]
    half = first_half.shape[0]

    def rows(first, count):
        if first >= half:
            return second_half[first - half : first - half + count, :]
        return first_half[first : first + count, :]

    def flat(ref, piece, start=0):
        ref[pl.ds(start, piece.shape[1])] = piece.reshape(-1)

    for g in range(0, fwidth, 8):
        eight = rows(g, 8)
        flast[g : g + 8, :] = eight[:, :width]
        f3[g : g + 8, :] = eight[:, width : width + fwidth]
        f2[g : g + 8, :] = eight[:, width + fwidth : width + 2 * fwidth]
        take = min(8, feats - g)
        if take > 0:
            f1[g : g + take, :] = eight[:take, width + 2 * fwidth : width + 3 * fwidth]
    for i, ref in enumerate((dbias, gain2, shift2, obias, fbias)):
        flat(ref, rows(fwidth + i, 1)[:, :width])
    ubias[...] = jnp.concatenate([rows(fwidth + 5 + i, 1) for i in range(3)], axis=1).reshape(-1)
    for i, ref in enumerate((f1b, f2b, f3b, freq)):
        flat(ref, rows(fwidth + 8 + i, 1)[:, :fwidth])
    wide = lambda first: jnp.concatenate([late[first + i : first + i + 1, :] for i in range(3)], axis=1)
    in_bias[...] = wide(0).reshape(-1)
    for k in range(taps_n):
        short_weight[k : k + 1, :] = wide(3 + 3 * k)
    short_bias[...] = wide(3 + 3 * taps_n).reshape(-1)
    count = late.shape[0]
    flat(gain1, late[count - 2 : count - 1, :])
    flat(shift1, late[count - 1 : count, :])


def place_down_out_kernel(meta, *refs):
    pieces, (down, out) = refs[:4], refs[4:]
    row = meta[3]
    share = pieces[0].shape[0]
    width = out.shape[1]
    part = share // 2
    for j, piece in enumerate(pieces):
        x, y = (row ^ j) % 2, (row ^ j) // 2
        down[pl.ds(pl.multiple_of((2 * x + y) * share, 8), share), :] = piece[:, :width].astype(F32)
        tiles = (
            piece[:part, width : width + 128],
            piece[part:, width : width + 128],
            piece[:part, width + 128 :],
        )
        for t, tile in enumerate(tiles):
            cols = pl.ds(pl.multiple_of(x * (width // 2) + t * 128, 128), 128)
            out[pl.ds(pl.multiple_of(y * part, 8), part), cols] = tile.astype(F32)


def place_up_kernel(meta, *refs):
    pieces, up = refs[:4], refs[4]
    width = pieces[0].shape[1]
    for j, piece in enumerate(pieces):
        x, y = (meta[3] ^ j) % 2, (meta[3] ^ j) // 2
        up[:, pl.ds(pl.multiple_of((2 * y + x) * width, 128), width)] = piece[...].astype(F32)


def place_in_kernel(meta, *refs):
    pieces, full = refs[:4], refs[4]
    part, cols = pieces[0].shape
    for j, piece in enumerate(pieces):
        x, y = (meta[3] ^ j) % 2, (meta[3] ^ j) // 2
        full[pl.ds(pl.multiple_of(y * part, 8), part), pl.ds(pl.multiple_of(x * cols, 128), cols)] = (
            piece[...].astype(F32)
        )


def local(
    tokens, doc_starts, norm1_gain, norm1_bias, in_weight, in_bias, short_weight, short_bias,
    filter_first, filter_first_bias, filter_second, filter_second_bias, filter_third,
    filter_third_bias, filter_last, sine_freq, filter_bias, out_weight, out_bias, norm2_gain,
    norm2_bias, up_weight, up_bias, down_weight, down_bias, cotangent,
):
    block, width = tokens.shape[1:]
    blocks = lax.axis_size("seq")
    chips = blocks // 2
    nrows = lax.axis_size("rows")
    length = block * blocks
    hidden = up_weight.shape[1]
    index = lax.axis_index("seq")
    row = lax.axis_index("rows")
    starts = doc_starts[0]
    ndocs = starts.shape[0]
    taps_n = short_weight.shape[0]
    ff = width
    fsteps = hidden // ff
    share = width // blocks
    fits = blocks == 8 and nrows == 4 and fsteps == chips and share % 32 == 0 and block == 128
    packed = chips if fits and width == 768 else 0
    meta = jnp.concatenate(
        [jnp.stack([index, index % 2, index // 2, row]).astype(jnp.int32), starts]
    )
    tables = {k: jnp.asarray(v) for k, v in block_tables(block).items()}
    chunk = width if blocks <= 8 else 128
    steps = width // chunk
    tok, cot = tokens[0], cotangent[0]
    mat = whole((block, width))
    vec = whole((width,))
    sds = jax.ShapeDtypeStruct

    rim = shift(tok[block - RIM :], "seq", 1)
    proj, early, mixed, carried = single(
        partial(front_kernel, ndocs, packed), "front", 3.0,
        [sds((block + RIM, 3 * width), F32), sds((2 * width if packed else width, block), BF16),
         sds((block, 3 * width), F32), sds((block, width), BF16)],
        meta,
        [tok, rim, cot, norm1_gain, norm1_bias, in_weight, in_bias, short_weight, short_bias],
        scratch=[pltpu.VMEM((width, block), BF16)],
    )

    by_chunk = lambda lead: pl.BlockSpec(lead + (chunk,), lambda i: (0,) * len(lead) + (i,))
    fwidth, feats = sine_freq.shape[0], filter_first.shape[0]
    if packed:
        table = jnp.asarray(feature_table(length, (feats - 1) // 2))
        lags, window, *net = single(
            filter_kernel, "filter", 8.0,
            [sds((blocks, 2 * block, width), F32), sds((length, width), F32)]
            + [sds((3 * fwidth, length), F32)] * 3,
            meta,
            [table, filter_first, filter_first_bias, filter_second, filter_second_bias, filter_third,
             filter_third_bias, filter_last, sine_freq, tables["left3"]],
            after=[carried], scratch=[pltpu.VMEM((length, fwidth), F32)],
        )
    else:
        filter_params = tuple(
            v.astype(F32)
            for v in (filter_first, filter_first_bias, filter_second, filter_second_bias, filter_third,
                      filter_third_bias, filter_last, sine_freq)
        )
        taps, taps_pull = jax.vjp(partial(filter_taps, length=length), *filter_params)
        lags = pl.pallas_call(
            lag_kernel,
            grid=(steps,),
            out_shape=sds((blocks, 2 * block, width), F32),
            in_specs=[by_chunk((blocks, block)), whole(tables["left3"].shape)],
            out_specs=by_chunk((blocks, 2 * block)),
            compiler_params=params(),
            name="lags",
        )(taps.reshape(blocks, block, width), tables["left3"])

    signal = along_row(meta, carried, blocks, False, [lags])
    nparts = len(signal)
    part_specs = [by_chunk((v.shape[0], block)) for v in signal]
    held = [pltpu.VMEM((blocks, block, chunk), BF16)] if nparts > 1 else []
    spec_scratch = pltpu.VMEM((2 * block, chunk), F32)
    conv = pl.pallas_call(
        partial(conv_kernel, ndocs, nparts),
        grid=(steps,),
        out_shape=sds((block, width), F32),
        in_specs=[smem()] + part_specs + [by_chunk((blocks, 2 * block)),
                  whole(tables["left2"].shape), whole(tables["inv3"].shape)],
        out_specs=by_chunk((block,)),
        scratch_shapes=[spec_scratch] + held,
        compiler_params=params(),
        cost_estimate=cost(3.0),
        name="conv",
    )(meta, *signal, lags, tables["left2"], tables["inv3"])

    if packed:
        e1_rows = 2 * chips * 3 * share + width // 2
        e2_rows = width + hidden // 2
        extra = (sds((e1_rows, block), BF16),) * 2 + (sds((e2_rows, block), BF16),) * 2
        extra_specs = (whole((e1_rows, block)),) * 2 + (whole((e2_rows, block)),) * 2
    else:
        extra = (sds((hidden, block), BF16), sds((block, hidden), BF16), sds((width, block), BF16),
                 sds((width, block), BF16), sds((block, width), BF16))
        extra_specs = (pl.BlockSpec((ff, block), lambda i: (i, 0)),
                       pl.BlockSpec((block, ff), lambda i: (0, i)),
                       whole((width, block)), whole((width, block)), mat)
    lanes = hidden // 3
    output, gresid, glong, glong16, ggate, smalls_mlp, *acts = pl.pallas_call(
        partial(mlp_kernel, packed),
        grid=(fsteps,),
        out_shape=(
            sds((block, width), BF16), sds((block, width), F32),
            sds((block, width), F32), sds((block, width), BF16), sds((block, width), F32),
            sds((8, lanes), F32),
        ) + extra,
        in_specs=[
            smem(), mat, mat, mat, mat, mat, vec, whole((width, width)), vec, vec, vec,
            pl.BlockSpec((width, ff), lambda i: (0, i)), whole((hidden,)),
            pl.BlockSpec((ff, width), lambda i: (i, 0)), vec,
        ],
        out_specs=(mat, mat, mat, mat, mat, whole((8, lanes))) + extra_specs,
        scratch_shapes=[
            pltpu.VMEM((block, width), F32), pltpu.VMEM((block, width), BF16),
            pltpu.VMEM((block, width), F32), pltpu.VMEM((block, 1), F32),
            pltpu.VMEM((block, width), F32), pltpu.VMEM((block, width), F32),
            pltpu.VMEM((1, hidden), F32), pltpu.VMEM((1, hidden), F32),
            pltpu.VMEM((width, block), BF16), pltpu.VMEM((block, width), BF16),
        ],
        compiler_params=params(),
        cost_estimate=cost(10.0),
        name="mlp",
    )(meta, tok, cot, conv, carried, mixed, filter_bias, out_weight, out_bias, norm2_gain,
      norm2_bias, up_weight, up_bias, down_weight, down_bias)

    taps_grad = pl.pallas_call(
        partial(taps_grad_kernel, ndocs, nparts),
        grid=(steps,),
        out_shape=sds((blocks, block, width), F32),
        in_specs=[smem()] + part_specs + [
            by_chunk((block,)), whole(tables["left2"].shape), whole(tables["invt2"].shape),
            whole(tables["leftt3"].shape)],
        out_specs=by_chunk((blocks, block)),
        scratch_shapes=[pltpu.VMEM((blocks + 1, 2 * block, chunk), F32), spec_scratch] + held,
        compiler_params=params(),
        cost_estimate=cost(4.0),
        name="taps_grad",
    )(meta, *signal, glong, tables["left2"], tables["invt2"], tables["leftt3"])
    if packed:
        half_rows = (fwidth + 16) // 2
        mine, send = single(
            filter_back_kernel, "filter_back", 5.0, [sds((half_rows, lanes), F32)] * 2, meta,
            [taps_grad, window, *net, table, filter_first, filter_second, filter_third, filter_last,
             sine_freq, smalls_mlp],
            scratch=[pltpu.VMEM((2 * half_rows, lanes), F32)],
        )
        wait_for = [mine]
    else:
        filter_grads = taps_pull(taps_grad.reshape(length, width))
        wait_for = []

    grads = along_row(meta, glong16, blocks, True, wait_for)
    third = lambda n: pl.BlockSpec((block, chunk), lambda i: (0, n * steps + i))
    tap_third = lambda n: pl.BlockSpec((taps_n, chunk), lambda i: (0, n * steps + i))
    for_in, for_values, rim_out = pl.pallas_call(
        partial(conv_back_kernel, ndocs, length, nparts),
        grid=(steps,),
        out_shape=(sds((block, width), F32), sds((block, width), F32), sds((3, 8, width), F32)),
        in_specs=[smem()] + part_specs + [
            by_chunk((block,)), by_chunk((blocks, 2 * block)), whole(tables["invt2"].shape),
            whole(tables["leftt3"].shape), vec if steps == 1 else by_chunk((1,)), third(1), third(2),
            by_chunk((block,)), tap_third(0), tap_third(1), tap_third(2)],
        out_specs=(by_chunk((block,)), by_chunk((block,)), by_chunk((3, 8))),
        scratch_shapes=[spec_scratch] + held,
        compiler_params=params(),
        cost_estimate=cost(4.0),
        name="conv_back",
    )(meta, *grads, glong, lags, tables["invt2"], tables["leftt3"],
      filter_bias if steps == 1 else filter_bias.reshape(1, -1),
      mixed, mixed, ggate, short_weight, short_weight, short_weight)
    rim_back = shift(rim_out, "seq", -1)

    parts1 = parts2 = ()
    if packed:
        def gathered(mine, send, mask):
            got = swap(send, "rows", mask)
            return mine, swap(mine, "seq", 1), got, swap(got, "seq", 1)

        def partials(kernel, name, piece, arrays, after=()):
            return single(
                partial(kernel, chips), name, 3.0, [sds((chips,) + piece, BF16)] * 2, meta, arrays, after
            )

        e1, e1_send, e2, e2_send = acts
        early_all = gathered(early, early, 1)
        e1_all = gathered(e1, e1_send, 1)
        e2_all = gathered(e2, e2_send, 2)
        parts2 = partials(up_kernel, "up_grad", (share, width), e2_all, [rim_out])
        parts1 = partials(
            down_out_kernel, "down_out", (share, width + 256), (*e1_all, *early_all), [rim_out]
        )

    gproj, smalls_short, *late = single(
        partial(short_back_kernel, ndocs, packed), "short_back", 3.0,
        [sds((block, 3 * width), BF16), sds((24, width), F32)]
        + ([sds((3 * width // 2, block), BF16)] * 2 if packed else []),
        meta, [ggate, for_in, for_values, rim_back, proj, short_weight],
        after=[v[0] for v in (parts1, parts2) if v],
    )
    grad_tokens, smalls_late = single(
        tail_kernel, "tail", 2.5, [sds((block, width), F32), sds((24, width), F32)],
        meta, [gproj, in_weight, tok, norm1_gain, gresid, smalls_short],
    )

    if packed:
        def placed(kernel, name, shapes, pieces):
            return single(kernel, name, 1.5, [sds(v, F32) for v in shapes], meta, pieces)

        pieces1 = spread_out(meta, *parts1, 2)
        pieces2 = spread_out(meta, *parts2, 1)
        late_all = gathered(*late, 1)
        parts3 = partials(in_kernel, "in_grad", (share // 2, 3 * width // 2), (*late_all, *early_all))
        pieces3 = spread_out(meta, *parts3, 2)
        grad_down, grad_out = placed(
            place_down_out_kernel, "place_down_out", ((hidden // blocks, width), (share, width)), pieces1
        )
        (grad_up,) = placed(place_up_kernel, "place_up", ((share, hidden),), pieces2)
        (grad_in,) = placed(place_in_kernel, "place_in", ((share, 3 * width),), pieces3)

        small = mine + swap(send, "seq", 1)
        for axis, mask in (("rows", 1), ("rows", 2), ("seq", 2), ("seq", 4)):
            small = small + swap(small, axis, mask)
        other = swap(small, "seq", 1)
        first_half = jnp.where(index % 2 == 0, small, other)
        second_half = jnp.where(index % 2 == 0, other, small)
        shapes = [
            (width,), (width,), (3 * width,), (taps_n, 3 * width), (3 * width,), (feats, fwidth),
            (fwidth,), (fwidth, fwidth), (fwidth,), (fwidth, fwidth), (fwidth,), (fwidth, width),
            (fwidth,), (width,), (width,), (width,), (width,), (hidden,), (width,),
        ]
        smalls = single(
            partial(unpack_kernel, taps_n, fwidth, feats), "unpack", 1.5, [sds(v, F32) for v in shapes],
            meta, [first_half, second_half, butterfly(smalls_late)],
        )
    else:
        def summed(left, right):
            part = lax.psum_scatter(dot(left, right), "seq", scatter_dimension=0, tiled=True)
            return lax.psum(part, "rows")

        actt, gpre, n2t, gatedt, gmix = acts
        grad_in = summed(early, gproj)
        grad_out = summed(gatedt, gmix)
        grad_up = summed(n2t, gpre)
        grad_down = summed(actt, cot)
        small, late_sum, *fg = lax.psum((smalls_mlp, smalls_late, *filter_grads), ("rows", "seq"))
        wide = lambda first: late_sum[first : first + 3].reshape(-1)
        smalls = [
            late_sum[22], late_sum[23], wide(0), late_sum[3 : 3 + 3 * taps_n].reshape(taps_n, -1),
            wide(3 + 3 * taps_n), *fg, small[4, :width], small[3, :width], small[1, :width],
            small[2, :width], small[5:8].reshape(-1), small[0, :width],
        ]
    (grad_gain1, grad_shift1, grad_in_bias, grad_short_weight, grad_short_bias, f1, f1b, f2, f2b, f3,
     f3b, flast, freq, grad_filter_bias, grad_out_bias, grad_gain2, grad_shift2, grad_up_bias,
     grad_down_bias) = smalls
    return (
        output[None], grad_tokens[None], grad_gain1, grad_shift1, grad_in, grad_in_bias,
        grad_short_weight, grad_short_bias, f1, f1b, f2, f2b, f3, f3b, flast, freq,
        grad_filter_bias, grad_out, grad_out_bias, grad_gain2, grad_shift2, grad_up, grad_up_bias,
        grad_down, grad_down_bias,
    )


def solution(mesh):
    sharded = P("rows", "seq", None)
    placed = (sharded, P("rows", None)) + (P(),) * 23 + (sharded,)
    outs = [P()] * 25
    outs[0] = outs[1] = sharded
    for i in (4, 17, 21, 23):
        outs[i] = P("seq", None)
    return jax.shard_map(local, mesh=mesh, in_specs=placed, out_specs=tuple(outs), check_vma=False)
```

time: 310 us -> 203 us (0.65)
  waiting for transfers between devices: 106 us -> 58 us
  starting transfers between devices: 40.5 us -> 72.5 us
  local copies, waits for them, and re-layouts: 46.5 us -> 14.8 us
  matrix products: 17.6 us -> 0 us
  between operations: 18.7 us -> 1.46 us
  Pallas kernels: 69.2 us -> 53.6 us
  other arithmetic: 10.4 us -> 1.48 us
    ppermute x31 -> x46, waiting for transfers between devices: 93.5 us -> 43.8 us  [swap(): lax.ppermute(block, axis, [(i, i ^ mask) for i in range(lax.axis_size(axi...]
    dot_general x11 -> x0, matrix products: 17.6 us -> none  [the longest x3 9.5 us: filter_taps(): return jnp.dot(hidden, last, precision=HIGHEST) * window]
    ppermute x2 -> x8, starting transfers between devices: 3.85 us -> 20.2 us  [shift(): lax.ppermute(block, axis, [(i - distance, i) for i in devices if i - dist...]
    ppermute x31 -> x46, starting transfers between devices: 36.5 us -> 52.3 us  [swap(): lax.ppermute(block, axis, [(i, i ^ mask) for i in range(lax.axis_size(axi...]
    pallas_call x12 -> x21, Pallas kernels: 69.2 us -> 53.6 us  [the longest x17 32.9 us: single(): pl.pallas_call(body, grid=(1,), out_shape=tuple(outs), in_specs=[smem()]...]
    slice x16 -> x0, local copies, waits for them, and re-layouts: 14.7 us -> none  [the longest x4 2.67 us: local(): pieces[i] = flat[place:place + size].reshape(filter_grads[i].shape)]
    reshape x20 -> x0, local copies, waits for them, and re-layouts: 13.4 us -> none  [the longest x10 8.63 us: local(): line = lambda v: v.reshape(1, -1)]
    ppermute x2 -> x8, waiting for transfers between devices: 1.21 us -> 14.1 us  [shift(): lax.ppermute(block, axis, [(i - distance, i) for i in devices if i - dist...]
  transfers between devices with their start and end apart: 35 -> 54, of which waited for: 11 -> 16; matrix products, arithmetic and copies ran while one was open for 22% -> 1% of each run, Pallas kernels for 14% -> 25%
where the time goes in v2:
time: 203 us; the launch traced here: 202 us
  starting transfers between devices  72.5 us (36%)
  waiting for transfers between devices  58 us (29%)
  Pallas kernels  53.6 us (26%)
  local copies, waits for them, and re-layouts  14.8 us (7%)
    ppermute x46, starting transfers between devices, swap(): lax.ppermute(block, axis, [(i, i ^ mask) for i in range(lax.axis_size(axi...  52.3 us
    ppermute x46, waiting for transfers between devices, swap(): lax.ppermute(block, axis, [(i, i ^ mask) for i in range(lax.axis_size(axi...  43.8 us
    pallas_call x17, Pallas kernels, single(): pl.pallas_call(body, grid=(1,), out_shape=tuple(outs), in_specs=[smem()]...  32.9 us
    ppermute x8, starting transfers between devices, shift(): lax.ppermute(block, axis, [(i - distance, i) for i in devices if i - dist...  20.2 us
    ppermute x8, waiting for transfers between devices, shift(): lax.ppermute(block, axis, [(i - distance, i) for i in devices if i - dist...  14.1 us
    unnamed x82, local copies, waits for them, and re-layouts  13.3 us
    pallas_call x1, Pallas kernels, local(): pl.pallas_call(partial(mlp_kernel, packed), grid=(fsteps,), out_shape=(sd...  10 us
    pallas_call x1, Pallas kernels, local(): pl.pallas_call(partial(conv_back_kernel, ndocs, length, nparts), grid=(st...  5.35 us
  transfers between devices with their start and end apart: 54, of which 16 were waited for; matrix products, arithmetic and copies ran while one was open for 1% of the time, Pallas kernels for 25%

profile of v2, /device:TPU:0, one launch (start us, length us, event | category | flops | bytes accessed | tf_op | source)
XLA Modules:
  0.0 201.9 jit_solution(14524608090034969527)
XLA Ops:
  1.5 2.3 %collective-permute-start = (bf16[16,768]{1,0:T(8,128)(2,1)S(1)}, bf16[16,768]{1,0:T(8,128)(2,1)S(1)}, u32[]{:S(2)}, u32[]{:S(2)}) collective-permute-start(bf16[16,768]{1,0:T(8,128)(2,1)S(1)} %slice_bitcast_fusion), channel_id=1, source_target_pairs={{0,1},{1,2},{2,3},{3,4},{4,5},{5,6},{6,7},{8,9},{9,10},{10,11},{11... | collective-permute-start | bytes 73736 | tf_op jit(solution)/shard_map/ppermute | solution.py:750
  4.7 2.0 copy-done
  12.0 1.8 front.1
  13.8 6.9 %collective-permute-start.1 = (bf16[128,768]{1,0:T(8,128)(2,1)S(1)}, bf16[128,768]{1,0:T(8,128)(2,1)S(1)}, u32[]{:S(2)}, u32[]{:S(2)}) collective-permute-start(bf16[128,768]{1,0:T(8,128)(2,1)S(1)} %get-tuple-element.94.refs_11_.refs_1_.carried), channel_id=1, source_target_pairs={{0,2},{1,3},{2,4},{3,5},{4,6},{5,7},{8,10},{9,11},{10,12},{11,13},... | collective-permute-start | bytes 589832 | tf_op jit(solution)/shard_map/ppermute | solution.py:750
  20.7 4.5 %collective-permute-start.2 = (bf16[128,768]{1,0:T(8,128)(2,1)S(1)}, bf16[128,768]{1,0:T(8,128)(2,1)S(1)}, u32[]{:S(2)}, u32[]{:S(2)}) collective-permute-start(bf16[128,768]{1,0:T(8,128)(2,1)S(1)} %get-tuple-element.94.refs_11_.refs_1_.carried), channel_id=1, source_target_pairs={{0,4},{1,5},{2,6},{3,7},{8,12},{9,13},{10,14},{11,15},{16,20},{17,... | collective-permute-start | bytes 589832 | tf_op jit(solution)/shard_map/ppermute | solution.py:750
  32.4 5.4 %filter.1 = (f32[8,256,768]{2,1,0:T(8,128)S(1)}, f32[1024,768]{1,0:T(8,128)S(1)}, f32[192,1024]{1,0:T(8,128)S(1)}, f32[192,1024]{1,0:T(8,128)S(1)}, f32[192,1024]{1,0:T(8,128)S(1)}) custom-call(s32[9]{0:T(128)S(1)} %concatenate.3.refs_0_.meta, f32[40,1024]{1,0:T(8,128)S(1)} %copy-done.8, bf16[33,64]{1,0:T(8,128)(2,1)S(1)} %copy-done.19, ...), custom_call_target="tpu_custom_call" | custom-call | bytes 24000000 | tf_op jit(solution)/shard_map/filter/pallas_call | solution.py:38
  40.9 2.6 %conv.1 = f32[128,768]{1,0:T(8,128)S(1)} custom-call(s32[9]{0:T(128)S(1)} %concatenate.3.refs_0_.meta, bf16[4,128,768]{2,1,0:T(8,128)(2,1)S(1)} %collect.2.refs_0_, bf16[4,128,768]{2,1,0:T(8,128)(2,1)S(1)} %collective-permute-done.4.refs_1_, f32[8,256,768]{2,1,0:T(8,128)S(1)} %get-tuple-element.95.refs_5_.refs_2_.refs_3_, bf16[256,256]{1,0:T(8,128)(2,1)S(1)} %copy-done.10, ...), custom_call_target="tpu_custom_call" | custom-call | bytes 9000000 | tf_op jit(solution)/shard_map/conv/pallas_call | solution.py:1047
  43.7 10.0 %mlp.1 = (bf16[128,768]{1,0:T(8,128)(2,1)}, f32[128,768]{1,0:T(8,128)S(1)}, f32[128,768]{1,0:T(8,128)S(1)}, bf16[128,768]{1,0:T(8,128)(2,1)S(1)}, f32[128,768]{1...) custom-call(s32[9]{0:T(128)S(1)} %concatenate.3.refs_0_.meta, ...), custom_call_target="tpu_custom_call" | custom-call | bytes 30000000 | tf_op jit(solution)/shard_map/mlp/pallas_call | solution.py:1072
  59.4 3.4 %collective-permute-done.5.refs_2_ = bf16[128,768]{1,0:T(8,128)(2,1)S(1)} collective-permute-done((bf16[128,768]{1,0:T(8,128)(2,1)S(1)}, bf16[128,768]{1,0:T(8,128)(2,1)S(1)}, u32[]{:S(2)}, u32[]{:S(2)}) %collective-permute-start.5) | collective-permute-done | bytes 196640 | tf_op jit(solution)/shard_map/ppermute | solution.py:750
  62.7 9.2 %collective-permute-done.6.refs_3_ = bf16[128,768]{1,0:T(8,128)(2,1)S(1)} collective-permute-done((bf16[128,768]{1,0:T(8,128)(2,1)S(1)}, bf16[128,768]{1,0:T(8,128)(2,1)S(1)}, u32[]{:S(2)}, u32[]{:S(2)}) %collective-permute-start.6) | collective-permute-done | bytes 196640 | tf_op jit(solution)/shard_map/ppermute | solution.py:750
  73.2 2.7 %taps_grad.1.refs_1_ = f32[8,128,768]{2,1,0:T(8,128)S(1)} custom-call(s32[9]{0:T(128)S(1)} %concatenate.3.refs_0_.meta, bf16[4,128,768]{2,1,0:T(8,128)(2,1)S(1)} %collect.2.refs_0_, bf16[4,128,768]{2,1,0:T(8,128)(2,1)S(1)} %collective-permute-done.4.refs_1_, f32[128,768]{1,0:T(8,128)S(1)} %get-tuple-element.100.refs_2_, bf16[256,256]{1,0:T(8,128)(2,1)S(1)} %copy-done.10, ...), custom_call_target="tpu_custom_call" | custom-call | bytes 12000000 | tf_op jit(solution)/shard_map/taps_grad/pallas_call | solution.py:1099
  76.0 4.3 %filter_back.1 = (f32[40,1024]{1,0:T(8,128)S(1)}, f32[40,1024]{1,0:T(8,128)S(1)}) custom-call(s32[9]{0:T(128)S(1)} %concatenate.3.refs_0_.meta, f32[8,128,768]{2,1,0:T(8,128)S(1)} %taps_grad.1.refs_1_, f32[1024,768]{1,0:T(8,128)S(1)} %get-tuple-element.101.refs_2_, f32[192,1024]{1,0:T(8,128)S(1)} %get-tuple-element.102.refs_3_, ...), custom_call_target="tpu_custom_call" | custom-call | bytes 15000000 | tf_op jit(solution)/shard_map/filter_back/pallas_call | solution.py:38
  83.5 2.5 %collective-permute-done.19 = f32[40,1024]{1,0:T(8,128)S(1)} collective-permute-done((f32[40,1024]{1,0:T(8,128)S(1)}, f32[40,1024]{1,0:T(8,128)S(1)}, u32[]{:S(2)}, u32[]{:S(2)}) %collective-permute-start.19) | collective-permute-done | bytes 163872 | tf_op jit(solution)/shard_map/ppermute | solution.py:754
  87.1 5.4 %conv_back.1 = (f32[128,768]{1,0:T(8,128)S(1)}, f32[128,768]{1,0:T(8,128)S(1)}, f32[3,8,768]{2,1,0:T(8,128)S(1)}) custom-call(s32[9]{0:T(128)S(1)} %concatenate.3.refs_0_.meta, bf16[4,128,768]{2,1,0:T(8,128)(2,1)S(1)} %collect.3.refs_0_, bf16[4,128,768]{2,1,0:T(8,128)(2,1)S(1)} %collective-permute-done.8.refs_1_, f32[128,768]{1,0:T(8,128)S(1)} %get-tuple-element.100.refs_2_, ...), custom_call_target="tpu_custom_call" | custom-call | bytes 12000000 | tf_op jit(solution)/shard_map/conv_back/pallas_call | solution.py:1128
  93.8 2.6 %down_out.1 = (bf16[4,96,1024]{2,1,0:T(8,128)(2,1)S(1)}, bf16[4,96,1024]{2,1,0:T(8,128)(2,1)}) custom-call(s32[9]{0:T(128)S(1)} %concatenate.3.refs_0_.meta, bf16[2688,128]{1,0:T(8,128)(2,1)S(1)} %get-tuple-element.111.refs_1_, bf16[2688,128]{1,0:T(8,128)(2,1)S(1)} %collective-permute-done.10.refs_2_, bf16[2688,128]{1,0:T(8,128)(2,1)S(1)} %collective-permute-done.11.refs_3_, ...), custom_call_target="tpu_custom_call" | custom-call | bytes 9000000 | tf_op jit(solution)/shard_map/down_out/pallas_call | solution.py:38
  97.9 2.0 up_grad.1
  99.9 2.7 %short_back.1 = (bf16[128,2304]{1,0:T(8,128)(2,1)S(1)}, f32[24,768]{1,0:T(8,128)S(1)}, bf16[1152,128]{1,0:T(8,128)(2,1)S(1)}, bf16[1152,128]{1,0:T(8,128)(2,1)S(1)}) custom-call(s32[9]{0:T(128)S(1)} %concatenate.3.refs_0_.meta, f32[128,768]{1,0:T(8,128)S(1)} %get-tuple-element.98.refs_9_.refs_1_, f32[128,768]{1,0:T(8,128)S(1)} %get-tuple-element.107.refs_2_, ...), custom_call_target="tpu_custom_call" | custom-call | bytes 9000000 | tf_op jit(solution)/shard_map/short_back/pallas_call | solution.py:38
  105.3 2.8 %tail.1 = (f32[128,768]{1,0:T(8,128)}, f32[24,768]{1,0:T(8,128)S(1)}) custom-call(s32[9]{0:T(128)S(1)} %concatenate.3.refs_0_.meta, bf16[128,2304]{1,0:T(8,128)(2,1)S(1)} %get-tuple-element.118.refs_1_, bf16[768,2304]{1,0:T(8,128)(2,1)S(1)} %copy-done.1, bf16[128,768]{1,0:T(8,128)(2,1)S(1)} %bitcast.17, bf16[768]{0:T(1024)(128)(2,1)S(1)} %copy-done.23, ...), custom_call_target="tpu_custom_call" | custom-call | bytes 7500000 | tf_op jit(solution)/shard_map/tail/pallas_call | solution.py:38
  109.8 10.6 %collective-permute-done.21 = f32[40,1024]{1,0:T(8,128)S(1)} collective-permute-done((f32[40,1024]{1,0:T(8,128)S(1)}, f32[40,1024]{1,0:T(8,128)S(1)}, u32[]{:S(2)}, u32[]{:S(2)}) %collective-permute-start.21) | collective-permute-done | bytes 163872 | tf_op jit(solution)/shard_map/ppermute | solution.py:754
  121.1 5.8 %collective-permute-done.22 = f32[40,1024]{1,0:T(8,128)S(1)} collective-permute-done((f32[40,1024]{1,0:T(8,128)S(1)}, f32[40,1024]{1,0:T(8,128)S(1)}, u32[]{:S(2)}, u32[]{:S(2)}) %collective-permute-start.22) | collective-permute-done | bytes 163872 | tf_op jit(solution)/shard_map/ppermute | solution.py:754
  128.3 4.6 %collective-permute-done.27 = f32[24,768]{1,0:T(8,128)S(1)} collective-permute-done((f32[24,768]{1,0:T(8,128)S(1)}, f32[24,768]{1,0:T(8,128)S(1)}, u32[]{:S(2)}, u32[]{:S(2)}) %collective-permute-start.27) | collective-permute-done | bytes 73760 | tf_op jit(solution)/shard_map/ppermute | solution.py:754
  138.8 2.3 %collective-permute-start.48 = (bf16[96,768]{1,0:T(8,128)(2,1)S(1)}, bf16[96,768]{1,0:T(8,128)(2,1)}, u32[]{:S(2)}, u32[]{:S(2)}) collective-permute-start(bf16[96,768]{1,0:T(8,128)(2,1)S(1)} %get-tuple-element.157), channel_id=1, source_target_pairs={{0,2},{1,3},{2,0},{3,1},{4,6},{5,7},{6,4},{7,5},{8,10},{9,11},{10,... | collective-permute-start | bytes 442376 | tf_op jit(solution)/shard_map/ppermute | solution.py:754
  141.4 2.4 %collective-permute-start.50 = (bf16[96,768]{1,0:T(8,128)(2,1)S(1)}, bf16[96,768]{1,0:T(8,128)(2,1)}, u32[]{:S(2)}, u32[]{:S(2)}) collective-permute-start(bf16[96,768]{1,0:T(8,128)(2,1)S(1)} %get-tuple-element.159), channel_id=1, source_target_pairs={{0,6},{1,7},{2,4},{3,5},{4,2},{5,3},{6,0},{7,1},{8,14},{9,15},{10,... | collective-permute-start | bytes 442376 | tf_op jit(solution)/shard_map/ppermute | solution.py:754
  145.3 2.1 %collective-permute-start.41 = (bf16[96,1024]{1,0:T(8,128)(2,1)S(1)}, bf16[96,1024]{1,0:T(8,128)(2,1)S(1)}, u32[]{:S(2)}, u32[]{:S(2)}) collective-permute-start(bf16[96,1024]{1,0:T(8,128)(2,1)S(1)} %get-tuple-element.148), channel_id=1, source_target_pairs={{0,2},{1,3},{2,0},{3,1},{4,6},{5,7},{6,4},{7,5},{8,10},{9,11},{10,... | collective-permute-start | bytes 589832 | tf_op jit(solution)/shard_map/ppermute | solution.py:754
  147.4 7.1 %collective-permute-done.49 = bf16[96,768]{1,0:T(8,128)(2,1)} collective-permute-done((bf16[96,768]{1,0:T(8,128)(2,1)S(1)}, bf16[96,768]{1,0:T(8,128)(2,1)}, u32[]{:S(2)}, u32[]{:S(2)}) %collective-permute-start.49) | collective-permute-done | bytes 147488 | tf_op jit(solution)/shard_map/ppermute | solution.py:754
  157.1 1.9 collective-permute-start.29
  159.7 11.1 %collective-permute-start.34 = (bf16[48,1152]{1,0:T(8,128)(2,1)S(1)}, bf16[48,1152]{1,0:T(8,128)(2,1)S(1)}, u32[]{:S(2)}, u32[]{:S(2)}) collective-permute-start(bf16[48,1152]{1,0:T(8,128)(2,1)S(1)} %get-tuple-element.131), channel_id=1, source_target_pairs={{0,2},{1,3},{2,0},{3,1},{4,6},{5,7},{6,4},{7,5},{8,10},{9,11},{10,... | collective-permute-start | bytes 331784 | tf_op jit(solution)/shard_map/ppermute | solution.py:754
  171.5 1.8 collective-permute-start.36
  175.4 6.1 %collective-permute-done.35 = bf16[48,1152]{1,0:T(8,128)(2,1)S(1)} collective-permute-done((bf16[48,1152]{1,0:T(8,128)(2,1)S(1)}, bf16[48,1152]{1,0:T(8,128)(2,1)S(1)}, u32[]{:S(2)}, u32[]{:S(2)}) %collective-permute-start.35) | collective-permute-done | bytes 110624 | tf_op jit(solution)/shard_map/ppermute | solution.py:754
  181.6 1.7 collective-permute-start.53
  190.4 2.7 %collective-permute-done.44.refs_2_ = bf16[96,1024]{1,0:T(8,128)(2,1)S(1)} collective-permute-done((bf16[96,1024]{1,0:T(8,128)(2,1)S(1)}, bf16[96,1024]{1,0:T(8,128)(2,1)S(1)}, u32[]{:S(2)}, u32[]{:S(2)}) %collective-permute-start.44) | collective-permute-done | bytes 196640 | tf_op jit(solution)/shard_map/ppermute | solution.py:754
  197.7 1.8 place_down_out.1
  (197 shorter events, 65.4 us)
Async XLA Ops:
  13.8 24.0 %collective-permute-start.1 = (bf16[128,768]{1,0:T(8,128)(2,1)S(1)}, bf16[128,768]{1,0:T(8,128)(2,1)S(1)}, u32[]{:S(2)}, u32[]{:S(2)}) collective-permute-start(bf16[128,768]{1,0:T(8,128)(2,1)S(1)} %get-tuple-element.94.refs_11_.refs_1_.carried), channel_id=1, source_target_pairs={{0,2},{1,3},{2,4},{3,5},{4,6},{5,7},{8,10},{9,11},{10,12},{11,13},... | collective-permute-start | bytes 589832 | tf_op jit(solution)/shard_map/ppermute | solution.py:750
  20.7 17.2 %collective-permute-start.2 = (bf16[128,768]{1,0:T(8,128)(2,1)S(1)}, bf16[128,768]{1,0:T(8,128)(2,1)S(1)}, u32[]{:S(2)}, u32[]{:S(2)}) collective-permute-start(bf16[128,768]{1,0:T(8,128)(2,1)S(1)} %get-tuple-element.94.refs_11_.refs_1_.carried), channel_id=1, source_target_pairs={{0,4},{1,5},{2,6},{3,7},{8,12},{9,13},{10,14},{11,15},{16,20},{17,... | collective-permute-start | bytes 589832 | tf_op jit(solution)/shard_map/ppermute | solution.py:750
  25.2 12.7 %collective-permute-start.3 = (bf16[128,768]{1,0:T(8,128)(2,1)S(1)}, bf16[128,768]{1,0:T(8,128)(2,1)S(1)}, u32[]{:S(2)}, u32[]{:S(2)}) collective-permute-start(bf16[128,768]{1,0:T(8,128)(2,1)S(1)} %get-tuple-element.94.refs_11_.refs_1_.carried), channel_id=1, source_target_pairs={{0,6},{1,7},{8,14},{9,15},{16,22},{17,23},{24,30},{25,31}} | collective-permute-start | bytes 589832 | tf_op jit(solution)/shard_map/ppermute | solution.py:750
  38.7 20.7 %collective-permute-start.14 = (bf16[1536,128]{1,0:T(8,128)(2,1)S(1)}, bf16[1536,128]{1,0:T(8,128)(2,1)S(1)}, u32[]{:S(2)}, u32[]{:S(2)}) collective-permute-start(bf16[1536,128]{1,0:T(8,128)(2,1)S(1)} %get-tuple-element.113.refs_5_), channel_id=1, source_target_pairs={{0,8},{8,0},{16,24},{24,16},{1,9},{9,1},{17,25},{25,17},{2,10},{10... | collective-permute-start | bytes 1179656 | tf_op jit(solution)/shard_map/ppermute | solution.py:754
  53.7 29.3 %collective-permute-start.11 = (bf16[2688,128]{1,0:T(8,128)(2,1)S(1)}, bf16[2688,128]{1,0:T(8,128)(2,1)S(1)}, u32[]{:S(2)}, u32[]{:S(2)}) collective-permute-start(bf16[2688,128]{1,0:T(8,128)(2,1)S(1)} %get-tuple-element.112), channel_id=1, source_target_pairs={{0,8},{8,0},{16,24},{24,16},{1,9},{9,1},{17,25},{25,17},{2,10},{10... | collective-permute-start | bytes 2064392 | tf_op jit(solution)/shard_map/ppermute | solution.py:754
  56.5 15.5 %collective-permute-start.6 = (bf16[128,768]{1,0:T(8,128)(2,1)S(1)}, bf16[128,768]{1,0:T(8,128)(2,1)S(1)}, u32[]{:S(2)}, u32[]{:S(2)}) collective-permute-start(bf16[128,768]{1,0:T(8,128)(2,1)S(1)} %get-tuple-element.99.refs_1_), channel_id=1, source_target_pairs={{4,0},{5,1},{6,2},{7,3},{12,8},{13,9},{14,10},{15,11},{20,16},{21,... | collective-permute-start | bytes 589832 | tf_op jit(solution)/shard_map/ppermute | solution.py:750
  57.8 28.3 %collective-permute-start.17 = (bf16[2304,128]{1,0:T(8,128)(2,1)}, bf16[2304,128]{1,0:T(8,128)(2,1)S(1)}, u32[]{:S(2)}, u32[]{:S(2)}) collective-permute-start(bf16[2304,128]{1,0:T(8,128)(2,1)} %get-tuple-element.116), channel_id=1, source_target_pairs={{0,16},{8,24},{16,0},{24,8},{1,17},{9,25},{17,1},{25,9},{2,18},{10... | collective-permute-start | bytes 1769480 | tf_op jit(solution)/shard_map/ppermute | solution.py:754
  59.4 23.1 %collective-permute-start.13 = (bf16[1536,128]{1,0:T(8,128)(2,1)S(1)}, bf16[1536,128]{1,0:T(8,128)(2,1)S(1)}, u32[]{:S(2)}, u32[]{:S(2)}) collective-permute-start(bf16[1536,128]{1,0:T(8,128)(2,1)S(1)} %get-tuple-element.113.refs_5_), channel_id=1, source_target_pairs={{0,1},{1,0},{2,3},{3,2},{4,5},{5,4},{6,7},{7,6},{8,9},{9,8},{10,11... | collective-permute-start | bytes 1179656 | tf_op jit(solution)/shard_map/ppermute | solution.py:754
  62.7 20.2 %collective-permute-start.15 = (bf16[1536,128]{1,0:T(8,128)(2,1)S(1)}, bf16[1536,128]{1,0:T(8,128)(2,1)S(1)}, u32[]{:S(2)}, u32[]{:S(2)}) collective-permute-start(bf16[1536,128]{1,0:T(8,128)(2,1)S(1)} %collective-permute-done.14.refs_7_), channel_id=1, source_target_pairs={{0,1},{1,0},{2,3},{3,2},{4,5},{5,4},{6,7},{7,6},{8,9},{9,8},{10,11... | collective-permute-start | bytes 1179656 | tf_op jit(solution)/shard_map/ppermute | solution.py:754
  85.9 12.0 %collective-permute-start.16 = (bf16[2304,128]{1,0:T(8,128)(2,1)S(1)}, bf16[2304,128]{1,0:T(8,128)(2,1)S(1)}, u32[]{:S(2)}, u32[]{:S(2)}) collective-permute-start(bf16[2304,128]{1,0:T(8,128)(2,1)S(1)} %get-tuple-element.115.refs_1_), channel_id=1, source_target_pairs={{0,1},{1,0},{2,3},{3,2},{4,5},{5,4},{6,7},{7,6},{8,9},{9,8},{10,11... | collective-permute-start | bytes 1769480 | tf_op jit(solution)/shard_map/ppermute | solution.py:754
  86.1 11.8 %collective-permute-start.18 = (bf16[2304,128]{1,0:T(8,128)(2,1)S(1)}, bf16[2304,128]{1,0:T(8,128)(2,1)S(1)}, u32[]{:S(2)}, u32[]{:S(2)}) collective-permute-start(bf16[2304,128]{1,0:T(8,128)(2,1)S(1)} %collective-permute-done.17.refs_3_), channel_id=1, source_target_pairs={{0,1},{1,0},{2,3},{3,2},{4,5},{5,4},{6,7},{7,6},{8,9},{9,8},{10,11... | collective-permute-start | bytes 1769480 | tf_op jit(solution)/shard_map/ppermute | solution.py:754
  86.5 18.2 %collective-permute-start.20 = (f32[40,1024]{1,0:T(8,128)S(1)}, f32[40,1024]{1,0:T(8,128)S(1)}, u32[]{:S(2)}, u32[]{:S(2)}) collective-permute-start(f32[40,1024]{1,0:T(8,128)S(1)} %add.65), channel_id=1, source_target_pairs={{0,8},{8,0},{16,24},{24,16},{1,9},{9,1},{17,25},{25,17},{2,10},{10... | collective-permute-start | bytes 491528 | tf_op jit(solution)/shard_map/ppermute | solution.py:754
  96.4 47.5 %collective-permute-start.40 = (bf16[4,96,1024]{2,1,0:T(8,128)(2,1)}, bf16[4,96,1024]{2,1,0:T(8,128)(2,1)}, u32[]{:S(2)}, u32[]{:S(2)}) collective-permute-start(bf16[4,96,1024]{2,1,0:T(8,128)(2,1)} %get-tuple-element.146), channel_id=1, source_target_pairs={{0,16},{8,24},{16,0},{24,8},{1,17},{9,25},{17,1},{25,9},{2,18},{10... | collective-permute-start | bytes 2359304 | tf_op jit(solution)/shard_map/ppermute | solution.py:754
  102.6 18.2 %collective-permute-start.31 = (bf16[1152,128]{1,0:T(8,128)(2,1)S(1)}, bf16[1152,128]{1,0:T(8,128)(2,1)S(1)}, u32[]{:S(2)}, u32[]{:S(2)}) collective-permute-start(bf16[1152,128]{1,0:T(8,128)(2,1)S(1)} %get-tuple-element.127), channel_id=1, source_target_pairs={{0,8},{8,0},{16,24},{24,16},{1,9},{9,1},{17,25},{25,17},{2,10},{10... | collective-permute-start | bytes 884744 | tf_op jit(solution)/shard_map/ppermute | solution.py:754
  104.2 33.9 %collective-permute-start.47 = (bf16[4,96,768]{2,1,0:T(8,128)(2,1)S(1)}, bf16[4,96,768]{2,1,0:T(8,128)(2,1)S(1)}, u32[]{:S(2)}, u32[]{:S(2)}) collective-permute-start(bf16[4,96,768]{2,1,0:T(8,128)(2,1)S(1)} %get-tuple-element.155), channel_id=1, source_target_pairs={{0,8},{8,0},{16,24},{24,16},{1,9},{9,1},{17,25},{25,17},{2,10},{10... | collective-permute-start | bytes 1769480 | tf_op jit(solution)/shard_map/ppermute | solution.py:754
  104.7 15.6 %collective-permute-start.21 = (f32[40,1024]{1,0:T(8,128)S(1)}, f32[40,1024]{1,0:T(8,128)S(1)}, u32[]{:S(2)}, u32[]{:S(2)}) collective-permute-start(f32[40,1024]{1,0:T(8,128)S(1)} %add.66), channel_id=1, source_target_pairs={{0,16},{8,24},{16,0},{24,8},{1,17},{9,25},{17,1},{25,9},{2,18},{10... | collective-permute-start | bytes 491528 | tf_op jit(solution)/shard_map/ppermute | solution.py:754
  120.5 13.2 %collective-permute-start.30 = (bf16[1152,128]{1,0:T(8,128)(2,1)S(1)}, bf16[1152,128]{1,0:T(8,128)(2,1)S(1)}, u32[]{:S(2)}, u32[]{:S(2)}) collective-permute-start(bf16[1152,128]{1,0:T(8,128)(2,1)S(1)} %get-tuple-element.126.refs_1_), channel_id=1, source_target_pairs={{0,1},{1,0},{2,3},{3,2},{4,5},{5,4},{6,7},{7,6},{8,9},{9,8},{10,11... | collective-permute-start | bytes 884744 | tf_op jit(solution)/shard_map/ppermute | solution.py:754
  120.8 14.4 %collective-permute-start.32 = (bf16[1152,128]{1,0:T(8,128)(2,1)S(1)}, bf16[1152,128]{1,0:T(8,128)(2,1)S(1)}, u32[]{:S(2)}, u32[]{:S(2)}) collective-permute-start(bf16[1152,128]{1,0:T(8,128)(2,1)S(1)} %collective-permute-done.31.refs_3_), channel_id=1, source_target_pairs={{0,1},{1,0},{2,3},{3,2},{4,5},{5,4},{6,7},{7,6},{8,9},{9,8},{10,11... | collective-permute-start | bytes 884744 | tf_op jit(solution)/shard_map/ppermute | solution.py:754
  136.5 20.6 %collective-permute-start.33 = (bf16[4,48,1152]{2,1,0:T(8,128)(2,1)S(1)}, bf16[4,48,1152]{2,1,0:T(8,128)(2,1)S(1)}, u32[]{:S(2)}, u32[]{:S(2)}) collective-permute-start(bf16[4,48,1152]{2,1,0:T(8,128)(2,1)S(1)} %get-tuple-element.129), channel_id=1, source_target_pairs={{0,16},{8,24},{16,0},{24,8},{1,17},{9,25},{17,1},{25,9},{2,18},{10... | collective-permute-start | bytes 1327112 | tf_op jit(solution)/shard_map/ppermute | solution.py:754
  141.4 13.1 %collective-permute-start.49 = (bf16[96,768]{1,0:T(8,128)(2,1)S(1)}, bf16[96,768]{1,0:T(8,128)(2,1)}, u32[]{:S(2)}, u32[]{:S(2)}) collective-permute-start(bf16[96,768]{1,0:T(8,128)(2,1)S(1)} %get-tuple-element.158), channel_id=1, source_target_pairs={{0,4},{1,5},{2,6},{3,7},{4,0},{5,1},{6,2},{7,3},{8,12},{9,13},{10,... | collective-permute-start | bytes 442376 | tf_op jit(solution)/shard_map/ppermute | solution.py:754
  141.4 13.1 %collective-permute-start.50 = (bf16[96,768]{1,0:T(8,128)(2,1)S(1)}, bf16[96,768]{1,0:T(8,128)(2,1)}, u32[]{:S(2)}, u32[]{:S(2)}) collective-permute-start(bf16[96,768]{1,0:T(8,128)(2,1)S(1)} %get-tuple-element.159), channel_id=1, source_target_pairs={{0,6},{1,7},{2,4},{3,5},{4,2},{5,3},{6,0},{7,1},{8,14},{9,15},{10,... | collective-permute-start | bytes 442376 | tf_op jit(solution)/shard_map/ppermute | solution.py:754
  143.9 29.5 %collective-permute-start.24 = (f32[40,1024]{1,0:T(8,128)S(1)}, f32[40,1024]{1,0:T(8,128)S(1)}, u32[]{:S(2)}, u32[]{:S(2)}) collective-permute-start(f32[40,1024]{1,0:T(8,128)S(1)} %add.69), channel_id=1, source_target_pairs={{0,1},{1,0},{2,3},{3,2},{4,5},{5,4},{6,7},{7,6},{8,9},{9,8},{10,11... | collective-permute-start | bytes 491528 | tf_op jit(solution)/shard_map/ppermute | solution.py:754
  145.3 14.4 %collective-permute-start.41 = (bf16[96,1024]{1,0:T(8,128)(2,1)S(1)}, bf16[96,1024]{1,0:T(8,128)(2,1)S(1)}, u32[]{:S(2)}, u32[]{:S(2)}) collective-permute-start(bf16[96,1024]{1,0:T(8,128)(2,1)S(1)} %get-tuple-element.148), channel_id=1, source_target_pairs={{0,2},{1,3},{2,0},{3,1},{4,6},{5,7},{6,4},{7,5},{8,10},{9,11},{10,... | collective-permute-start | bytes 589832 | tf_op jit(solution)/shard_map/ppermute | solution.py:754
  154.5 16.3 %collective-permute-start.42 = (bf16[96,1024]{1,0:T(8,128)(2,1)S(1)}, bf16[96,1024]{1,0:T(8,128)(2,1)S(1)}, u32[]{:S(2)}, u32[]{:S(2)}) collective-permute-start(bf16[96,1024]{1,0:T(8,128)(2,1)S(1)} %get-tuple-element.149), channel_id=1, source_target_pairs={{0,4},{1,5},{2,6},{3,7},{4,0},{5,1},{6,2},{7,3},{8,12},{9,13},{10,... | collective-permute-start | bytes 589832 | tf_op jit(solution)/shard_map/ppermute | solution.py:754
  154.5 17.0 %collective-permute-start.43 = (bf16[96,1024]{1,0:T(8,128)(2,1)S(1)}, bf16[96,1024]{1,0:T(8,128)(2,1)S(1)}, u32[]{:S(2)}, u32[]{:S(2)}) collective-permute-start(bf16[96,1024]{1,0:T(8,128)(2,1)S(1)} %get-tuple-element.150), channel_id=1, source_target_pairs={{0,6},{1,7},{2,4},{3,5},{4,2},{5,3},{6,0},{7,1},{8,14},{9,15},{10,... | collective-permute-start | bytes 589832 | tf_op jit(solution)/shard_map/ppermute | solution.py:754
  157.1 27.3 %collective-permute-start.29 = (f32[24,768]{1,0:T(8,128)S(1)}, f32[24,768]{1,0:T(8,128)S(1)}, u32[]{:S(2)}, u32[]{:S(2)}) collective-permute-start(f32[24,768]{1,0:T(8,128)S(1)} %add.73), channel_id=1, source_target_pairs={{0,16},{8,24},{16,0},{24,8},{1,17},{9,25},{17,1},{25,9},{2,18},{10... | collective-permute-start | bytes 221192 | tf_op jit(solution)/shard_map/ppermute | solution.py:754
  159.7 14.8 %collective-permute-start.34 = (bf16[48,1152]{1,0:T(8,128)(2,1)S(1)}, bf16[48,1152]{1,0:T(8,128)(2,1)S(1)}, u32[]{:S(2)}, u32[]{:S(2)}) collective-permute-start(bf16[48,1152]{1,0:T(8,128)(2,1)S(1)} %get-tuple-element.131), channel_id=1, source_target_pairs={{0,2},{1,3},{2,0},{3,1},{4,6},{5,7},{6,4},{7,5},{8,10},{9,11},{10,... | collective-permute-start | bytes 331784 | tf_op jit(solution)/shard_map/ppermute | solution.py:754
  173.4 11.8 %collective-permute-start.51 = (bf16[96,768]{1,0:T(8,128)(2,1)S(1)}, bf16[96,768]{1,0:T(8,128)(2,1)S(1)}, u32[]{:S(2)}, u32[]{:S(2)}) collective-permute-start(bf16[96,768]{1,0:T(8,128)(2,1)S(1)} %add_convert_fusion.1.refs_1_), channel_id=1, source_target_pairs={{0,8},{8,0},{16,24},{24,16},{1,9},{9,1},{17,25},{25,17},{2,10},{10... | collective-permute-start | bytes 442376 | tf_op jit(solution)/shard_map/ppermute | solution.py:754
  174.6 12.3 %collective-permute-start.52 = (bf16[96,768]{1,0:T(8,128)(2,1)S(1)}, bf16[96,768]{1,0:T(8,128)(2,1)S(1)}, u32[]{:S(2)}, u32[]{:S(2)}) collective-permute-start(bf16[96,768]{1,0:T(8,128)(2,1)S(1)} %add_convert_fusion.1.refs_1_), channel_id=1, source_target_pairs={{0,16},{8,24},{16,0},{24,8},{1,17},{9,25},{17,1},{25,9},{2,18},{10... | collective-permute-start | bytes 442376 | tf_op jit(solution)/shard_map/ppermute | solution.py:754
  184.4 13.3 %collective-permute-start.45 = (bf16[96,1024]{1,0:T(8,128)(2,1)S(1)}, bf16[96,1024]{1,0:T(8,128)(2,1)S(1)}, u32[]{:S(2)}, u32[]{:S(2)}) collective-permute-start(bf16[96,1024]{1,0:T(8,128)(2,1)S(1)} %add_convert_fusion.refs_1_), channel_id=1, source_target_pairs={{0,16},{8,24},{16,0},{24,8},{1,17},{9,25},{17,1},{25,9},{2,18},{10... | collective-permute-start | bytes 589832 | tf_op jit(solution)/shard_map/ppermute | solution.py:754
  185.2 12.5 %collective-permute-start.46 = (bf16[96,1024]{1,0:T(8,128)(2,1)S(1)}, bf16[96,1024]{1,0:T(8,128)(2,1)S(1)}, u32[]{:S(2)}, u32[]{:S(2)}) collective-permute-start(bf16[96,1024]{1,0:T(8,128)(2,1)S(1)} %add_convert_fusion.refs_1_), channel_id=1, source_target_pairs={{0,24},{8,16},{16,8},{24,0},{1,25},{9,17},{17,9},{25,1},{2,26},{10... | collective-permute-start | bytes 589832 | tf_op jit(solution)/shard_map/ppermute | solution.py:754
  186.9 12.6 %collective-permute-start.37 = (bf16[48,1152]{1,0:T(8,128)(2,1)S(1)}, bf16[48,1152]{1,0:T(8,128)(2,1)S(1)}, u32[]{:S(2)}, u32[]{:S(2)}) collective-permute-start(bf16[48,1152]{1,0:T(8,128)(2,1)S(1)} %add_convert_fusion.2.refs_1_), channel_id=1, source_target_pairs={{0,8},{8,0},{16,24},{24,16},{1,9},{9,1},{17,25},{25,17},{2,10},{10... | collective-permute-start | bytes 331784 | tf_op jit(solution)/shard_map/ppermute | solution.py:754
  (63 other events, 480.5 us)

commit v3 on v2

--- a/solution.py
+++ b/solution.py
@@ -16,38 +16,59 @@
 F32 = jnp.float32
 BF16 = jnp.bfloat16
 RIM = 16
+LATE_ROWS = tuple(range(15)) + (22, 23)
 VMEM_LIMIT = 26 * 1024 * 1024
 GELU_C = math.sqrt(2.0 / math.pi)
 GELU_A = 0.044715
 
 
-def params():
-    return pltpu.CompilerParams(vmem_limit_bytes=VMEM_LIMIT)
+def params(limit=VMEM_LIMIT):
+    return pltpu.CompilerParams(vmem_limit_bytes=limit)
 
 
 def cost(micros):
-    return pl.CostEstimate(flops=0, bytes_accessed=int(micros * 3.0e6), transcendentals=0)
-
-
-def single(kernel, name, micros, outs, scalars, arrays, after=(), scratch=()):
-    count, skip = 1 + len(arrays), len(after)
-
-    def body(*refs):
-        kernel(*refs[:count], *refs[count + skip :])
-
-    made = pl.pallas_call(
+    return pl.CostEstimate(flops=int(micros * 1.1e9), bytes_accessed=0, transcendentals=0)
+
+
+def single(kernel, name, micros, outs, scalars, arrays, after=(), scratch=(), fetch=(), limit=VMEM_LIMIT):
+    count, skip, nouts = len(arrays), len(after), len(outs)
+
+    def body(meta, *refs):
+        ins, made = list(refs[:count]), refs[count + skip : count + skip + nouts]
+        rest = list(refs[count + skip + nouts :])
+        if fetch:
+            sems, rest = rest[-1], rest[:-1]
+            held, rest = rest[: len(fetch)], rest[len(fetch) :]
+            copies = [
+                pltpu.make_async_copy(ins[p], dest, sems.at[i])
+                for i, (p, dest) in enumerate(zip(fetch, held))
+            ]
+            for copy in copies:
+                copy.start()
+            for copy in copies:
+                copy.wait()
+            for p, dest in zip(fetch, held):
+                ins[p] = dest
+        kernel(meta, *ins, *made, *rest)
+
+    own = [pltpu.VMEM(arrays[p].shape, arrays[p].dtype) for p in fetch]
+    sems = [pltpu.SemaphoreType.DMA((len(fetch),))] if fetch else []
+    return pl.pallas_call(
         body,
         grid=(1,),
         out_shape=tuple(outs),
-        in_specs=[smem()] + [whole(v.shape) for v in arrays]
+        in_specs=[smem()]
+        + [
+            pl.BlockSpec(memory_space=pltpu.HBM) if p in fetch else whole(v.shape)
+            for p, v in enumerate(arrays)
+        ]
         + [pl.BlockSpec(memory_space=pl.ANY)] * skip,
         out_specs=tuple(whole(v.shape) for v in outs),
-        scratch_shapes=list(scratch),
-        compiler_params=params(),
+        scratch_shapes=own + list(scratch) + sems,
+        compiler_params=params(limit),
         cost_estimate=cost(micros),
         name=name,
     )(scalars, *arrays, *after)
-    return made
 
 
 def smem():
@@ -189,6 +210,13 @@
 
 def part_of(ref, first, size):
     return ref[pl.ds(first, size)].astype(F32).reshape(1, -1)
+
+
+def write_side(out, first, source, count, rows, parity):
+    for z in range(count):
+        out[pl.ds(first + z * rows, rows), :] = source[
+            pl.ds(pl.multiple_of((2 * z + parity) * rows, 16), rows), :
+        ]
 
 
 def write_strips(out, first, source, count, rows, core):
@@ -257,24 +285,23 @@
     lax.fori_loop(0, blocks, step, 0)
 
 
-def fill(meta, parts, held, ahead):
-    own, sibling = parts
-    chips = own.shape[0]
-    for k in range(chips):
-        z = meta[2] + k if ahead else meta[2] - k
-
-        @pl.when((z >= 0) & (z < chips))
-        def _():
-            held[2 * z + meta[1]] = own[k]
-            held[2 * z + 1 - meta[1]] = sibling[k]
-
-
-def conv_kernel(ndocs, nparts, meta, *refs):
+def fill(meta, parts, first, held):
+    near, sibling = parts[:-1], parts[-1]
+    block, width = held.shape[1:]
+    for k, ref in enumerate(near):
+        z = meta[2] ^ k
+        held[2 * z + meta[1]] = ref[...]
+        for t in range(width // 128):
+            rows = pl.ds(first + (k * (width // 128) + t) * block, block)
+            held[2 * z + 1 - meta[1], :, t * 128 : (t + 1) * 128] = sibling[rows, :]
+
+
+def conv_kernel(ndocs, nparts, first, meta, *refs):
     parts, (lags, left2, inv3, out, acc), rest = refs[:nparts], refs[nparts : nparts + 5], refs[nparts + 5 :]
     signal = parts[0]
     if nparts > 1:
         (signal,) = rest
-        fill(meta, parts, signal, False)
+        fill(meta, parts, first, signal)
     block = signal.shape[1]
     me = meta[0]
     base = me * block
@@ -308,7 +335,7 @@
 def mlp_kernel(packed, meta, tokens, cot, conv, carried, gate_out, fbias, w_out, b_out, gain, shift,
                up, up_bias, down, down_bias, *refs):
     (output, gresid, glong, glong16, ggate, smalls), refs = refs[:6], refs[6:]
-    (e1, e1_send, e2, e2_send) = refs[:4]
+    (own, shared, e1_send, e2_send) = refs[:4]
     if packed:
         refs = refs[4:]
     else:
@@ -342,15 +369,15 @@
         gacc[...] = jnp.zeros_like(gacc)
         if packed:
             turned[...] = gated_t
-            for dest in (e1, e1_send):
-                for p in range(2):
-                    for z in range(chips):
-                        dest[pl.ds(p * slot + chips * half + z * share, share), :] = turned[
-                            pl.ds(pl.multiple_of((2 * z + (core ^ p)) * share, 16), share), :
-                        ]
+            later = chips * half
+            for dest, p, first in ((own, 0, later), (shared, 1, later), (e1_send, 0, later),
+                                   (e1_send, 1, slot + later)):
+                write_side(dest, first, turned, chips, share, core ^ p)
             turned[...] = normed.T.astype(BF16)
-            for dest in (e2, e2_send):
-                write_strips(dest, 0, turned, chips, share, core)
+            after1 = slot + width // 2
+            for dest, p, first in ((own, 0, slot), (shared, 1, after1), (e2_send, 0, 0),
+                                   (e2_send, 1, chips * share)):
+                write_side(dest, first, turned, chips, share, core ^ p)
         else:
             gatedt_out[...] = gated_t
             n2t_out[...] = normed.T.astype(BF16)
@@ -365,11 +392,11 @@
     )
     if packed:
         turned[...] = act.T.astype(BF16)
-        for p in range(2):
-            for dest, side in ((e1, x), (e1_send, 1 - x)):
-                dest[pl.ds(pl.multiple_of(p * slot + j * half, 16), half), :] = turned[
-                    pl.ds(pl.multiple_of((core ^ p) * big + side * half, 16), half), :
-                ]
+        for dest, p, side, first in ((own, 0, x, 0), (shared, 1, x, 0), (e1_send, 0, 1 - x, 0),
+                                     (e1_send, 1, 1 - x, slot)):
+            dest[pl.ds(pl.multiple_of(first + j * half, 16), half), :] = turned[
+                pl.ds(pl.multiple_of((core ^ p) * big + side * half, 16), half), :
+            ]
     else:
         actt[...] = act.T.astype(BF16)
     oacc[...] += dot(act.astype(BF16), down[...])
@@ -378,16 +405,17 @@
         rows_held[...] = gpre
         per = chips // 2
         for t in range(ff // 128):
-            place = pl.ds(pl.multiple_of(width + ((j % per) * (ff // 128) + t) * block, 16), block)
+            at = ((j % per) * (ff // 128) + t) * block
             tile = gpre[:, t * 128 : (t + 1) * 128]
 
             @pl.when(j // per == y)
             def _():
-                e2[place, :] = tile
+                first = slot + width // 2 + chips * share
+                shared[pl.ds(pl.multiple_of(first + at, 16), block), :] = tile
 
             @pl.when(j // per != y)
             def _():
-                e2_send[place, :] = tile
+                e2_send[pl.ds(pl.multiple_of(width + at, 16), block), :] = tile
     else:
         gpre_out[...] = gpre
     ubias_grad[:, pl.ds(pl.multiple_of(j * ff, 128), ff)] = jnp.sum(
@@ -409,8 +437,8 @@
         gm = gr.astype(BF16)
         if packed:
             rows_held[...] = gm
-            for dest, side in ((e1, x), (e1_send, 1 - x)):
-                write_tiles(dest, 2 * slot, rows_held, side * (width // 2), width // 256)
+            write_tiles(shared, slot, rows_held, x * (width // 2), width // 256)
+            write_tiles(e1_send, 2 * slot, rows_held, (1 - x) * (width // 2), width // 256)
         else:
             gmix_out[...] = gm
         gg = dot_t(gm, w_out[...])
@@ -435,14 +463,14 @@
             smalls[len(rows) + i : len(rows) + i + 1, :] = ubias_grad[:, i * lanes : (i + 1) * lanes]
 
 
-def conv_back_kernel(ndocs, length, nparts, meta, *refs):
+def conv_back_kernel(ndocs, length, nparts, first, meta, *refs):
     parts, refs = refs[:nparts], refs[nparts:]
     (own_grad, lags, invt2, leftt3, fbias, gate_in, values, ggate, short_gate, short_in,
      short_values, for_in, for_values, rim, acc) = refs[:15]
     grads = parts[0]
     if nparts > 1:
         grads = refs[15]
-        fill(meta, parts, grads, True)
+        fill(meta, parts, first, grads)
     block = grads.shape[1]
     me = meta[0]
     base = me * block
@@ -490,13 +518,13 @@
         rim[third] = jnp.concatenate(rows, axis=0)
 
 
-def taps_grad_kernel(ndocs, nparts, meta, *refs):
+def taps_grad_kernel(ndocs, nparts, first, meta, *refs):
     parts, refs = refs[:nparts], refs[nparts:]
     own_grad, left2, invt2, leftt3, out, win, gspec = refs[:7]
     signal = parts[0]
     if nparts > 1:
         signal = refs[7]
-        fill(meta, parts, signal, False)
+        fill(meta, parts, first, signal)
     blocks, block = signal.shape[0], signal.shape[1]
     me = meta[0]
     base = me * block
@@ -587,10 +615,15 @@
     mean_q = jnp.mean(q, axis=-1, keepdims=True)
     mean_qh = jnp.mean(q * hat, axis=-1, keepdims=True)
     out[...] = gresid[...] + (q - mean_q - hat * mean_qh) * rstd
-    smalls[...] = others[...]
-    count = smalls.shape[0]
-    smalls[count - 2 : count - 1, :] = jnp.sum(gn * hat, axis=0, keepdims=True)
-    smalls[count - 1 :, :] = jnp.sum(gn, axis=0, keepdims=True)
+    rows = [others[i : i + 1, :] for i in range(others.shape[0] - 2)]
+    rows += [jnp.sum(gn * hat, axis=0, keepdims=True), jnp.sum(gn, axis=0, keepdims=True)]
+    if smalls.shape[1] == others.shape[1]:
+        smalls[...] = jnp.concatenate(rows, axis=0)
+        return
+    smalls[...] = jnp.zeros_like(smalls)
+    half = others.shape[1] // 2
+    for k, (r, h) in enumerate((r, h) for r in LATE_ROWS for h in range(2)):
+        smalls[k // 3 : k // 3 + 1, k % 3 * half : (k % 3 + 1) * half] = rows[r][:, h * half : (h + 1) * half]
 
 
 def filter_taps(first, first_bias, second, second_bias, third, third_bias, last, sine_freq, length):
@@ -705,8 +738,11 @@
     wh, wl = high_low(weighted)
     ah, al = high_low(act[2 * fwidth :, :])
     packed[...] = jnp.zeros_like(packed)
-    packed[:fwidth, :width] = dot(ah, wh) + (dot(ah, wl) + dot(al, wh))
-    packed[fwidth : fwidth + others.shape[0], :] = others[...]
+    half = fwidth // 2
+    made = dot(ah, wh) + (dot(ah, wl) + dot(al, wh))
+    packed[:half, :width] = made[:half]
+    packed[:half, width : 2 * width] = made[half:]
+    packed[half : half + others.shape[0], 256 : 256 + others.shape[1]] = others[...]
     back = dot_t(last[...], wh) + dot_t(last[...], wl)
     ones = jnp.ones((8, length), BF16)
 
@@ -720,7 +756,7 @@
         return (dot_t(ones, high) + dot_t(ones, low))[:1]
 
     freq_total = jnp.zeros((1, fwidth), F32)
-    place = width
+    place = 2 * width
     for i, weight in ((2, third), (1, second), (0, first)):
         rows = slice(i * fwidth, (i + 1) * fwidth)
         step = back * slope[rows, :]
@@ -728,14 +764,20 @@
         step = step * scale
         below = act[(i - 1) * fwidth : i * fwidth, :] if i else table[...]
         made = wide_t(below, step)
-        packed[: made.shape[0], place : place + fwidth] = made
-        packed[fwidth + others.shape[0] + i : fwidth + others.shape[0] + i + 1, :fwidth] = sums(step)
-        place += fwidth
+        if i:
+            packed[:half, place : place + fwidth] = made[:half]
+            packed[:half, place + fwidth : place + 2 * fwidth] = made[half:]
+            place += 2 * fwidth
+        else:
+            for part in range(0, made.shape[0], 16):
+                lanes = slice(part // 16 * fwidth, part // 16 * fwidth + fwidth)
+                piece = made[part : part + 16]
+                packed[half : half + piece.shape[0], lanes] = piece
+        packed[half + 8 + i : half + 9 + i, 2 * fwidth : 3 * fwidth] = sums(step)
         if i:
             high, low = high_low(step)
             back = dot(weight[...], high) + dot(weight[...], low)
-    at = fwidth + others.shape[0] + 3
-    packed[at : at + 1, :fwidth] = freq_total
+    packed[half + 11 : half + 12, 2 * fwidth : 3 * fwidth] = freq_total
     half = packed.shape[0] // 2
     for side in range(2):
 
@@ -754,44 +796,42 @@
     return lax.ppermute(block, axis, [(i, i ^ mask) for i in range(lax.axis_size(axis))])
 
 
-def butterfly(values):
-    for axis in ("seq", "rows"):
-        mask = 1
-        while mask < lax.axis_size(axis):
-            values = values + swap(values, axis, mask)
-            mask *= 2
-    return values
-
-
-def collect_kernel(meta, *refs):
-    out = refs[-1]
-    for k, ref in enumerate(refs[:-1]):
-        out[k] = ref[...]
-
-
-def along_row(meta, block, blocks, ahead, after):
-    if blocks > 8:
-        return (lax.all_gather(block, "seq", axis=0, tiled=False),)
-    step = -2 if ahead else 2
-    near = [block] + [shift(block, "seq", step * k) for k in range(1, blocks // 2)]
-    (own,) = single(
-        collect_kernel, "collect", 0.5, [jax.ShapeDtypeStruct((len(near),) + block.shape, block.dtype)],
-        meta, near, after,
+def collect_kernel(spans, meta, *refs):
+    out, place = refs[-1], 0
+    for ref, span in zip(refs[:-1], spans):
+        if span is None:
+            write_tiles(out, place, ref, 0, ref.shape[1] // 128)
+            place += ref.shape[0] * (ref.shape[1] // 128)
+        else:
+            out[pl.ds(place, span[1] - span[0]), :] = ref[pl.ds(span[0], span[1] - span[0]), :]
+            place += span[1] - span[0]
+
+
+def collected(meta, pieces, after=()):
+    rows = sum(v.shape[0] * v.shape[1] // 128 if span is None else span[1] - span[0] for v, span in pieces)
+    (out,) = single(
+        partial(collect_kernel, [span for _, span in pieces]), "collect", 0.6,
+        [jax.ShapeDtypeStruct((rows, 128), BF16)], meta, [v for v, _ in pieces], after,
     )
-    return own, swap(own, "seq", 1)
-
-
-def joined_left(sources, first, slot, rows):
-    return jnp.concatenate(
-        [ref[pl.ds(first + (i % 2) * slot, rows), :] for i, ref in enumerate(sources)], axis=1
-    )
-
-
-def joined_right(sources, first, block, count):
+    return out
+
+
+def near_blocks(block, blocks):
+    got = {k: swap(block, "seq", 2 * k) for k in (2, 3, 1)}
+    return [block] + [got[k] for k in range(1, blocks // 2)]
+
+
+def joined_left(sources, rows):
+    return jnp.concatenate([ref[pl.ds(first, rows), :] for ref, first in sources], axis=1)
+
+
+def joined_right(sources, block, start, count):
     return jnp.concatenate(
         [
-            jnp.concatenate([ref[pl.ds(first + t * block, block), :] for t in range(count)], axis=1)
-            for ref in sources
+            jnp.concatenate(
+                [ref[pl.ds(first + t * block, block), :] for t in range(start, start + count)], axis=1
+            )
+            for ref, first in sources
         ],
         axis=0,
     )
@@ -807,20 +847,30 @@
         store(send)
 
 
-def down_out_kernel(chips, meta, *refs):
-    acts, early, (keep, send) = refs[:4], refs[4:8], refs[8:]
-    block = acts[0].shape[1]
+def early_sources(early, early_got, early_sib, width, columns):
+    half = width // 2
+    if columns:
+        return ((early, width), (early_sib, half), (early_got, width), (early_sib, 2 * width))
+    return ((early, 0), (early_sib, 0), (early_got, 0), (early_sib, half + width))
+
+
+def down_out_kernel(chips, meta, own, shared, shared_sib, got, got_sib, early, early_got, early_sib,
+                    keep, send):
+    block = own.shape[1]
     share = keep.shape[1]
-    width = early[0].shape[0] // 2
+    width = early.shape[0] // 2
     half = 2 * share
     slot = chips * (half + share)
     y, chip = meta[3] // 2, meta[2]
+    sources = (own, shared_sib, got, got_sib)
     made = dot(
-        joined_left(acts, 0, slot, chips * half), joined_right(early, width, block, width // 128)
+        joined_left([(v, 0) for v in sources], chips * half),
+        joined_right(early_sources(early, early_got, early_sib, width, True), block, 0, width // 128),
     ).astype(BF16)
+    right = ((shared, slot), (shared_sib, slot), (got, 2 * slot), (got_sib, slot))
     out = dot(
-        joined_left(acts, chips * half, slot, chips * share),
-        joined_right(acts, 2 * slot, block, width // 256),
+        joined_left([(v, chips * half) for v in sources], chips * share),
+        joined_right(right, block, 0, width // 256),
     ).astype(BF16)
     part = share // 2
     for side in range(2):
@@ -839,15 +889,17 @@
         pick(y == side, keep, send, store)
 
 
-def up_kernel(chips, meta, *refs):
-    acts, (keep, send) = refs[:4], refs[4:]
-    block = acts[0].shape[1]
+def up_kernel(chips, meta, own, shared, shared_sib, got, got_sib, keep, send):
+    block = own.shape[1]
     share, width = keep.shape[1:]
     x, chip = meta[3] % 2, meta[2]
-    left = joined_left(acts, 0, width // 2, width // 2)
+    rows = chips * share
+    slot = 3 * rows
+    first = slot + width // 2
+    left = joined_left(((own, slot), (shared_sib, first), (got, 0), (got_sib, first)), rows)
+    right = ((shared, first + rows), (shared_sib, first + rows), (got, 2 * rows), (got_sib, first + rows))
     for side in range(2):
-        right = joined_right(acts, width + side * width, block, width // 128)
-        made = dot(left, right).astype(BF16)
+        made = dot(left, joined_right(right, block, side * (width // 128), width // 128)).astype(BF16)
 
         def store(dest):
             for z in range(chips):
@@ -856,14 +908,15 @@
         pick(x == side, keep, send, store)
 
 
-def in_kernel(chips, meta, *refs):
-    acts, early, (keep, send) = refs[:4], refs[4:8], refs[8:]
-    block = acts[0].shape[1]
+def in_kernel(chips, meta, mine, got, sib, early, early_got, early_sib, keep, send):
+    block = mine.shape[1]
     part, cols = keep.shape[1:]
-    width = early[0].shape[0] // 2
+    width = early.shape[0] // 2
     y, chip = meta[3] // 2, meta[2]
+    right = ((mine, 0), (sib, 0), (got, 0), (sib, mine.shape[0]))
     made = dot(
-        joined_left(early, 0, width // 2, width // 2), joined_right(acts, 0, block, cols // 128)
+        joined_left(early_sources(early, early_got, early_sib, width, False), width // 2),
+        joined_right(right, block, 0, cols // 128),
     ).astype(BF16)
     for side in range(2):
 
@@ -875,94 +928,144 @@
         pick(y == side, keep, send, store)
 
 
-def merge_kernel(meta, keep, got, own, *sends):
-    own[...] = keep[0].astype(F32) + got[0].astype(F32)
-    for j, dest in enumerate(sends):
-        dest[...] = (keep[j + 1].astype(F32) + got[j + 1].astype(F32)).astype(BF16)
-
-
-def spread_out(meta, keep, send, mask):
-    chips, rows, cols = keep.shape
-    outs = [jax.ShapeDtypeStruct((rows, cols), F32)]
-    outs += [jax.ShapeDtypeStruct((rows, cols), BF16)] * (chips - 1)
-    own, *sends = single(merge_kernel, "merge", 1.0, outs, meta, [keep, swap(send, "rows", mask)])
-    for j, block in enumerate(sends):
-        own = own + swap(block, "seq", 2 * (j + 1)).astype(F32)
-    own = own.astype(BF16)
-    return [own] + [swap(own, "rows", j) for j in (1, 2, 3)]
-
-
-def unpack_kernel(taps_n, fwidth, feats, meta, first_half, second_half, late, *outs):
+def merge_kernel(pairs, meta, *refs):
+    ins, refs = refs[: 2 * pairs], refs[2 * pairs :]
+    rows = ins[0].shape[1]
+    chips = ins[0].shape[0]
+    extra, (own, *sends) = refs[:-chips], refs[-chips:]
+    first = 0
+    for p in range(pairs):
+        keep, got = ins[2 * p : 2 * p + 2]
+        cols = slice(first, first + keep.shape[2])
+        first += keep.shape[2]
+        own[:rows, cols] = keep[0].astype(F32) + got[0].astype(F32)
+        for j, dest in enumerate(sends):
+            dest[:rows, cols] = (keep[j + 1].astype(F32) + got[j + 1].astype(F32)).astype(BF16)
+    if extra:
+        value = (extra[0][...] + extra[1][...]).astype(BF16)
+        own[rows:, :] = value.astype(F32)
+        for dest in sends:
+            dest[rows:, :] = value
+
+
+def total_kernel(extras, meta, own, one, two, three, *refs):
+    rows = own.shape[0]
+    out = refs[-1]
+    out[:rows, :] = (
+        (own[...] + one[...].astype(F32)) + (two[...].astype(F32) + three[...].astype(F32))
+    ).astype(BF16)
+    if extras:
+        small = refs[0]
+        out[rows : rows + small.shape[0], :] = small[...].astype(BF16)
+        out[rows + small.shape[0] :, :] = jnp.zeros(
+            (out.shape[0] - rows - small.shape[0], out.shape[1]), BF16
+        )
+
+
+def spread_out(meta, pairs, with_merge=(), with_total=()):
+    chips, rows, _ = pairs[0].shape
+    cols = sum(v.shape[2] for v in pairs[::2])
+    rows += with_merge[0].shape[0] if with_merge else 0
+    sds = jax.ShapeDtypeStruct
+    own, *sends = single(
+        partial(merge_kernel, len(pairs) // 2), "merge", 1.0,
+        [sds((rows, cols), F32)] + [sds((rows, cols), BF16)] * (chips - 1), meta, (*pairs, *with_merge),
+    )
+    got = {j: swap(sends[j - 1], "seq", 2 * j) for j in (2, 3, 1)}
+    (total,) = single(
+        partial(total_kernel, len(with_total)), "total", 1.0,
+        [sds((rows + (32 if with_total else 0), cols), BF16)], meta,
+        [own, got[1], got[2], got[3], *with_total],
+    )
+    return [total] + [swap(total, "rows", j) for j in (1, 2, 3)]
+
+
+def small_kernel(rows, meta, *refs):
+    pieces, out = refs[:4], refs[4]
+    take = pl.ds(rows, 32)
+    a, b, c, d = (ref[take, :].astype(F32) for ref in pieces)
+    total = (a + b) + (c + d)
+    out[...] = total[: out.shape[0]]
+
+
+def unpack_kernel(taps_n, fwidth, feats, first_late, meta, small, other, *refs):
+    late_pieces, outs, packed, late = refs[:4], refs[4:-2], refs[-2], refs[-1]
+    half = small.shape[0]
+    even = meta[1] == 0
+    packed[:half, :] = jnp.where(even, small[...], other[...])
+    packed[half:, :] = jnp.where(even, other[...], small[...])
     (gain1, shift1, in_bias, short_weight, short_bias, f1, f1b, f2, f2b, f3, f3b, flast, freq,
      fbias, obias, gain2, shift2, ubias, dbias) = outs
     width = gain1.shape[0]
-    half = first_half.shape[0]
-
-    def rows(first, count):
-        if first >= half:
-            return second_half[first - half : first - half + count, :]
-        return first_half[first : first + count, :]
-
-    def flat(ref, piece, start=0):
-        ref[pl.ds(start, piece.shape[1])] = piece.reshape(-1)
-
-    for g in range(0, fwidth, 8):
-        eight = rows(g, 8)
-        flast[g : g + 8, :] = eight[:, :width]
-        f3[g : g + 8, :] = eight[:, width : width + fwidth]
-        f2[g : g + 8, :] = eight[:, width + fwidth : width + 2 * fwidth]
-        take = min(8, feats - g)
-        if take > 0:
-            f1[g : g + take, :] = eight[:take, width + 2 * fwidth : width + 3 * fwidth]
+    take = pl.ds(first_late, late_pieces[0].shape[0] - first_late)
+    a, b, c, d = (ref[take, :].astype(F32) for ref in late_pieces)
+    late[...] = (a + b) + (c + d)
+    part = fwidth // 2
+    flast[:part, :] = packed[:part, :width]
+    flast[part:, :] = packed[:part, width : 2 * width]
+    place = 2 * width
+    for ref in (f3, f2):
+        ref[:part, :] = packed[:part, place : place + fwidth]
+        ref[part:, :] = packed[:part, place + fwidth : place + 2 * fwidth]
+        place += 2 * fwidth
+    for first in range(0, feats, 16):
+        count = min(16, feats - first)
+        lanes = slice(first // 16 * fwidth, first // 16 * fwidth + fwidth)
+        f1[first : first + count, :] = packed[part : part + count, lanes]
+    for i, ref in enumerate((f1b, f2b, f3b, freq)):
+        ref[...] = packed[part + 8 + i : part + 9 + i, 2 * fwidth : 3 * fwidth].reshape(-1)
     for i, ref in enumerate((dbias, gain2, shift2, obias, fbias)):
-        flat(ref, rows(fwidth + i, 1)[:, :width])
-    ubias[...] = jnp.concatenate([rows(fwidth + 5 + i, 1) for i in range(3)], axis=1).reshape(-1)
-    for i, ref in enumerate((f1b, f2b, f3b, freq)):
-        flat(ref, rows(fwidth + 8 + i, 1)[:, :fwidth])
-    wide = lambda first: jnp.concatenate([late[first + i : first + i + 1, :] for i in range(3)], axis=1)
+        ref[...] = packed[part + i : part + i + 1, 256 : 256 + width].reshape(-1)
+    lanes = ubias.shape[0] // 3
+    ubias[...] = jnp.concatenate(
+        [packed[part + 5 + i : part + 6 + i, 256 : 256 + lanes] for i in range(3)], axis=1
+    ).reshape(-1)
+    side = late.shape[1] // 3
+
+    def row(r):
+        return [
+            late[k // 3 : k // 3 + 1, k % 3 * side : (k % 3 + 1) * side] for k in (2 * r, 2 * r + 1)
+        ]
+
+    def wide(first):
+        return jnp.concatenate(row(first) + row(first + 1) + row(first + 2), axis=1)
+
     in_bias[...] = wide(0).reshape(-1)
     for k in range(taps_n):
         short_weight[k : k + 1, :] = wide(3 + 3 * k)
     short_bias[...] = wide(3 + 3 * taps_n).reshape(-1)
-    count = late.shape[0]
-    flat(gain1, late[count - 2 : count - 1, :])
-    flat(shift1, late[count - 1 : count, :])
-
-
-def place_down_out_kernel(meta, *refs):
-    pieces, (down, out) = refs[:4], refs[4:]
+    count = 6 + 3 * taps_n
+    gain1[...] = jnp.concatenate(row(count), axis=1).reshape(-1)
+    shift1[...] = jnp.concatenate(row(count + 1), axis=1).reshape(-1)
+
+
+def place_early_kernel(meta, *refs):
+    pieces, (down, out, up) = refs[:4], refs[4:]
     row = meta[3]
-    share = pieces[0].shape[0]
-    width = out.shape[1]
+    share, width = out.shape
     part = share // 2
     for j, piece in enumerate(pieces):
         x, y = (row ^ j) % 2, (row ^ j) // 2
-        down[pl.ds(pl.multiple_of((2 * x + y) * share, 8), share), :] = piece[:, :width].astype(F32)
+        down[pl.ds(pl.multiple_of((2 * x + y) * share, 8), share), :] = piece[:share, :width].astype(F32)
         tiles = (
             piece[:part, width : width + 128],
-            piece[part:, width : width + 128],
-            piece[:part, width + 128 :],
+            piece[part:share, width : width + 128],
+            piece[:part, width + 128 : width + 256],
         )
         for t, tile in enumerate(tiles):
             cols = pl.ds(pl.multiple_of(x * (width // 2) + t * 128, 128), 128)
             out[pl.ds(pl.multiple_of(y * part, 8), part), cols] = tile.astype(F32)
-
-
-def place_up_kernel(meta, *refs):
-    pieces, up = refs[:4], refs[4]
-    width = pieces[0].shape[1]
-    for j, piece in enumerate(pieces):
-        x, y = (meta[3] ^ j) % 2, (meta[3] ^ j) // 2
-        up[:, pl.ds(pl.multiple_of((2 * y + x) * width, 128), width)] = piece[...].astype(F32)
+        cols = pl.ds(pl.multiple_of((2 * y + x) * width, 128), width)
+        up[:, cols] = piece[:share, width + 256 :].astype(F32)
 
 
 def place_in_kernel(meta, *refs):
     pieces, full = refs[:4], refs[4]
-    part, cols = pieces[0].shape
+    part, cols = full.shape[0] // 2, pieces[0].shape[1]
     for j, piece in enumerate(pieces):
         x, y = (meta[3] ^ j) % 2, (meta[3] ^ j) // 2
         full[pl.ds(pl.multiple_of(y * part, 8), part), pl.ds(pl.multiple_of(x * cols, 128), cols)] = (
-            piece[...].astype(F32)
+            piece[:part, :].astype(F32)
         )
 
 
@@ -1006,8 +1109,10 @@
          sds((block, 3 * width), F32), sds((block, width), BF16)],
         meta,
         [tok, rim, cot, norm1_gain, norm1_bias, in_weight, in_bias, short_weight, short_bias],
-        scratch=[pltpu.VMEM((width, block), BF16)],
+        scratch=[pltpu.VMEM((width, block), BF16)], limit=58 * 1024 * 1024,
     )
+
+    early_got = swap(early, "rows", 1) if packed else None
 
     by_chunk = lambda lead: pl.BlockSpec(lead + (chunk,), lambda i: (0,) * len(lead) + (i,))
     fwidth, feats = sine_freq.shape[0], filter_first.shape[0]
@@ -1039,13 +1144,24 @@
             name="lags",
         )(taps.reshape(blocks, block, width), tables["left3"])
 
-    signal = along_row(meta, carried, blocks, False, [lags])
-    nparts = len(signal)
-    part_specs = [by_chunk((v.shape[0], block)) for v in signal]
-    held = [pltpu.VMEM((blocks, block, chunk), BF16)] if nparts > 1 else []
+    if packed:
+        near = near_blocks(carried, blocks)
+        span = (width // 2, 2 * width)
+        early_sib = swap(
+            collected(
+                meta, [(early, span), (early_got, span)] + [(v, None) for v in near], [lags]
+            ), "seq", 1,
+        )
+        signal, signal_row = near + [early_sib], 3 * width
+        nparts = len(signal)
+        part_specs = [whole(v.shape) for v in signal]
+        held = [pltpu.VMEM((blocks, block, chunk), BF16)]
+    else:
+        signal, signal_row = [lax.all_gather(carried, "seq", axis=0, tiled=False)], 0
+        nparts, part_specs, held = 1, [by_chunk((blocks, block))], []
     spec_scratch = pltpu.VMEM((2 * block, chunk), F32)
     conv = pl.pallas_call(
-        partial(conv_kernel, ndocs, nparts),
+        partial(conv_kernel, ndocs, nparts, signal_row),
         grid=(steps,),
         out_shape=sds((block, width), F32),
         in_specs=[smem()] + part_specs + [by_chunk((blocks, 2 * block)),
@@ -1058,10 +1174,12 @@
     )(meta, *signal, lags, tables["left2"], tables["inv3"])
 
     if packed:
-        e1_rows = 2 * chips * 3 * share + width // 2
-        e2_rows = width + hidden // 2
-        extra = (sds((e1_rows, block), BF16),) * 2 + (sds((e2_rows, block), BF16),) * 2
-        extra_specs = (whole((e1_rows, block)),) * 2 + (whole((e2_rows, block)),) * 2
+        left1, right1, left2, right2 = chips * 3 * share, width // 2, width // 2, hidden // 2
+        row_counts = (
+            left1 + left2, left1 + right1 + left2 + right2, 2 * left1 + right1, 2 * left2 + right2
+        )
+        extra = tuple(sds((n, block), BF16) for n in row_counts)
+        extra_specs = tuple(whole((n, block)) for n in row_counts)
     else:
         extra = (sds((hidden, block), BF16), sds((block, hidden), BF16), sds((width, block), BF16),
                  sds((width, block), BF16), sds((block, width), BF16))
@@ -1097,7 +1215,7 @@
       norm2_bias, up_weight, up_bias, down_weight, down_bias)
 
     taps_grad = pl.pallas_call(
-        partial(taps_grad_kernel, ndocs, nparts),
+        partial(taps_grad_kernel, ndocs, nparts, signal_row),
         grid=(steps,),
         out_shape=sds((blocks, block, width), F32),
         in_specs=[smem()] + part_specs + [
@@ -1110,26 +1228,36 @@
         name="taps_grad",
     )(meta, *signal, glong, tables["left2"], tables["invt2"], tables["leftt3"])
     if packed:
-        half_rows = (fwidth + 16) // 2
+        own, shared, e1_send, e2_send = acts
+        got1, got2 = swap(e1_send, "rows", 1), swap(e2_send, "rows", 2)
+        near = near_blocks(glong16, blocks)
+        shared_sib = swap(shared, "seq", 1)
+        bundle = collected(
+            meta, [(got1, (left1, 2 * left1 + right1)), (got2, (left2, 2 * left2 + right2))]
+            + [(v, None) for v in near],
+        )
+        got_sib = swap(bundle, "seq", 1)
+        grads, grads_row = near + [got_sib], shared.shape[0]
+        grad_specs = [whole(v.shape) for v in grads]
+        half_rows, small_cols = (fwidth // 2 + 16) // 2, 2 * width + 4 * fwidth
         mine, send = single(
-            filter_back_kernel, "filter_back", 5.0, [sds((half_rows, lanes), F32)] * 2, meta,
+            filter_back_kernel, "filter_back", 5.0, [sds((half_rows, small_cols), F32)] * 2, meta,
             [taps_grad, window, *net, table, filter_first, filter_second, filter_third, filter_last,
              sine_freq, smalls_mlp],
-            scratch=[pltpu.VMEM((2 * half_rows, lanes), F32)],
-        )
-        wait_for = [mine]
+            after=[bundle], scratch=[pltpu.VMEM((2 * half_rows, small_cols), F32)],
+        )
     else:
+        grads, grads_row = [lax.all_gather(glong16, "seq", axis=0, tiled=False)], 0
+        grad_specs = part_specs
         filter_grads = taps_pull(taps_grad.reshape(length, width))
-        wait_for = []
-
-    grads = along_row(meta, glong16, blocks, True, wait_for)
+
     third = lambda n: pl.BlockSpec((block, chunk), lambda i: (0, n * steps + i))
     tap_third = lambda n: pl.BlockSpec((taps_n, chunk), lambda i: (0, n * steps + i))
     for_in, for_values, rim_out = pl.pallas_call(
-        partial(conv_back_kernel, ndocs, length, nparts),
+        partial(conv_back_kernel, ndocs, length, nparts, grads_row),
         grid=(steps,),
         out_shape=(sds((block, width), F32), sds((block, width), F32), sds((3, 8, width), F32)),
-        in_specs=[smem()] + part_specs + [
+        in_specs=[smem()] + grad_specs + [
             by_chunk((block,)), by_chunk((blocks, 2 * block)), whole(tables["invt2"].shape),
             whole(tables["leftt3"].shape), vec if steps == 1 else by_chunk((1,)), third(1), third(2),
             by_chunk((block,)), tap_third(0), tap_third(1), tap_third(2)],
@@ -1142,36 +1270,33 @@
       filter_bias if steps == 1 else filter_bias.reshape(1, -1),
       mixed, mixed, ggate, short_weight, short_weight, short_weight)
     rim_back = shift(rim_out, "seq", -1)
-
-    parts1 = parts2 = ()
+    tied = ()
     if packed:
-        def gathered(mine, send, mask):
-            got = swap(send, "rows", mask)
-            return mine, swap(mine, "seq", 1), got, swap(got, "seq", 1)
-
         def partials(kernel, name, piece, arrays, after=()):
             return single(
                 partial(kernel, chips), name, 3.0, [sds((chips,) + piece, BF16)] * 2, meta, arrays, after
             )
 
-        e1, e1_send, e2, e2_send = acts
-        early_all = gathered(early, early, 1)
-        e1_all = gathered(e1, e1_send, 1)
-        e2_all = gathered(e2, e2_send, 2)
-        parts2 = partials(up_kernel, "up_grad", (share, width), e2_all, [rim_out])
+        parts2 = partials(up_kernel, "up_grad", (share, width), (own, shared, shared_sib, got2, got_sib), [rim_out])
         parts1 = partials(
-            down_out_kernel, "down_out", (share, width + 256), (*e1_all, *early_all), [rim_out]
-        )
+            down_out_kernel, "down_out", (share, width + 256),
+            (own, shared, shared_sib, got1, got_sib, early, early_got, early_sib), [rim_out],
+        )
+        small = mine + swap(send, "seq", 1)
+        small = small + swap(small, "seq", 2)
+        small = small + swap(small, "seq", 4)
+        tied = (parts1[0], parts2[0])
+
 
     gproj, smalls_short, *late = single(
         partial(short_back_kernel, ndocs, packed), "short_back", 3.0,
         [sds((block, 3 * width), BF16), sds((24, width), F32)]
         + ([sds((3 * width // 2, block), BF16)] * 2 if packed else []),
-        meta, [ggate, for_in, for_values, rim_back, proj, short_weight],
-        after=[v[0] for v in (parts1, parts2) if v],
+        meta, [ggate, for_in, for_values, rim_back, proj, short_weight], tied,
     )
+    late_shape = (16, 3 * width // 2) if packed else (24, width)
     grad_tokens, smalls_late = single(
-        tail_kernel, "tail", 2.5, [sds((block, width), F32), sds((24, width), F32)],
+        tail_kernel, "tail", 2.5, [sds((block, width), F32), sds(late_shape, F32)],
         meta, [gproj, in_weight, tok, norm1_gain, gresid, smalls_short],
     )
 
@@ -1179,31 +1304,44 @@
         def placed(kernel, name, shapes, pieces):
             return single(kernel, name, 1.5, [sds(v, F32) for v in shapes], meta, pieces)
 
-        pieces1 = spread_out(meta, *parts1, 2)
-        pieces2 = spread_out(meta, *parts2, 1)
-        late_all = gathered(*late, 1)
-        parts3 = partials(in_kernel, "in_grad", (share // 2, 3 * width // 2), (*late_all, *early_all))
-        pieces3 = spread_out(meta, *parts3, 2)
-        grad_down, grad_out = placed(
-            place_down_out_kernel, "place_down_out", ((hidden // blocks, width), (share, width)), pieces1
-        )
-        (grad_up,) = placed(place_up_kernel, "place_up", ((share, hidden),), pieces2)
+        keep1, send1 = parts1
+        keep2, send2 = parts2
+        pieces = spread_out(
+            meta, [keep1, swap(send1, "rows", 2), keep2, swap(send2, "rows", 1)], (), (small,)
+        )
+        late, late_send = late
+        late_got = swap(late_send, "rows", 1)
+        late_sib = swap(
+            collected(
+                meta, [(late, (0, late.shape[0])), (late_got, (0, late.shape[0]))], [small]
+            ), "seq", 1
+        )
+        keep3, send3 = partials(
+            in_kernel, "in_grad", (share // 2, 3 * width // 2),
+            (late, late_got, late_sib, early, early_got, early_sib),
+        )
+        pieces3 = spread_out(
+            meta, [keep3, swap(send3, "rows", 2)], (smalls_late, swap(smalls_late, "seq", 1))
+        )
+        grad_down, grad_out, grad_up = placed(
+            place_early_kernel, "place_early",
+            ((hidden // blocks, width), (share, width), (share, hidden)), pieces,
+        )
         (grad_in,) = placed(place_in_kernel, "place_in", ((share, 3 * width),), pieces3)
 
-        small = mine + swap(send, "seq", 1)
-        for axis, mask in (("rows", 1), ("rows", 2), ("seq", 2), ("seq", 4)):
-            small = small + swap(small, axis, mask)
+        (small,) = single(
+            partial(small_kernel, share), "small", 0.5, [sds((half_rows, small_cols), F32)], meta, pieces
+        )
         other = swap(small, "seq", 1)
-        first_half = jnp.where(index % 2 == 0, small, other)
-        second_half = jnp.where(index % 2 == 0, other, small)
         shapes = [
             (width,), (width,), (3 * width,), (taps_n, 3 * width), (3 * width,), (feats, fwidth),
             (fwidth,), (fwidth, fwidth), (fwidth,), (fwidth, fwidth), (fwidth,), (fwidth, width),
             (fwidth,), (width,), (width,), (width,), (width,), (hidden,), (width,),
         ]
         smalls = single(
-            partial(unpack_kernel, taps_n, fwidth, feats), "unpack", 1.5, [sds(v, F32) for v in shapes],
-            meta, [first_half, second_half, butterfly(smalls_late)],
+            partial(unpack_kernel, taps_n, fwidth, feats, share // 2), "unpack", 1.5,
+            [sds(v, F32) for v in shapes], meta, [small, other, *pieces3],
+            scratch=[pltpu.VMEM((2 * half_rows, small_cols), F32), pltpu.VMEM(late_shape, F32)],
         )
     else:
         def summed(left, right):

time: 203 us -> 186 us (0.916)
  starting transfers between devices: 72.5 us -> 52 us
  waiting for transfers between devices: 58 us -> 69.9 us
  local copies, waits for them, and re-layouts: 14.8 us -> 5.36 us
  Pallas kernels: 53.6 us -> 56.5 us
    ppermute x46 -> x34, waiting for transfers between devices: 43.8 us -> 69.9 us  [swap(): lax.ppermute(block, axis, [(i, i ^ mask) for i in range(lax.axis_size(axi...]
    ppermute x8 -> x2, starting transfers between devices: 20.2 us -> 3.64 us  [shift(): lax.ppermute(block, axis, [(i - distance, i) for i in devices if i - dist...]
    ppermute x8 -> x2, waiting for transfers between devices: 14.1 us -> 0.01 us  [shift(): lax.ppermute(block, axis, [(i - distance, i) for i in devices if i - dist...]
    unnamed x82 -> x78, local copies, waits for them, and re-layouts: 13.3 us -> 3.36 us
    ppermute x46 -> x34, starting transfers between devices: 52.3 us -> 48.4 us  [swap(): lax.ppermute(block, axis, [(i, i ^ mask) for i in range(lax.axis_size(axi...]
    pallas_call x17 -> x19, Pallas kernels: 32.9 us -> 35.8 us  [single(): pl.pallas_call(body, grid=(1,), out_shape=tuple(outs), in_specs=[smem()]...]
  transfers between devices with their start and end apart: 54 -> 36, of which waited for: 16 -> 12; matrix products, arithmetic and copies ran while one was open for 1% -> 1% of each run, Pallas kernels for 25% -> 19%
where the time goes in v3:
time: 186 us; the launch traced here: 185 us
  waiting for transfers between devices  69.9 us (38%)
  Pallas kernels  56.5 us (30%)
  starting transfers between devices  52 us (28%)
  local copies, waits for them, and re-layouts  5.36 us (3%)
    ppermute x34, waiting for transfers between devices, swap(): lax.ppermute(block, axis, [(i, i ^ mask) for i in range(lax.axis_size(axi...  69.9 us
    ppermute x34, starting transfers between devices, swap(): lax.ppermute(block, axis, [(i, i ^ mask) for i in range(lax.axis_size(axi...  48.4 us
    pallas_call x19, Pallas kernels, single(): pl.pallas_call(body, grid=(1,), out_shape=tuple(outs), in_specs=[smem()]...  35.8 us
    pallas_call x1, Pallas kernels, local(): pl.pallas_call(partial(mlp_kernel, packed), grid=(fsteps,), out_shape=(sd...  9.9 us
    pallas_call x1, Pallas kernels, local(): pl.pallas_call(partial(conv_back_kernel, ndocs, length, nparts, grads_row...  5.36 us
  transfers between devices with their start and end apart: 36, of which 12 were waited for; matrix products, arithmetic and copies ran while one was open for 1% of the time, Pallas kernels for 19%

profile of v3, /device:TPU:0, one launch (start us, length us, event | category | flops | bytes accessed | tf_op | source)
XLA Modules:
  0.0 185.5 jit_solution(3328022229710316587)
XLA Ops:
  1.4 2.3 %collective-permute-start = (bf16[16,768]{1,0:T(8,128)(2,1)S(1)}, bf16[16,768]{1,0:T(8,128)(2,1)S(1)}, u32[]{:S(2)}, u32[]{:S(2)}) collective-permute-start(bf16[16,768]{1,0:T(8,128)(2,1)S(1)} %slice_bitcast_fusion), channel_id=1, source_target_pairs={{0,1},{1,2},{2,3},{3,4},{4,5},{5,6},{6,7},{8,9},{9,10},{10,11},{11... | collective-permute-start | bytes 73736 | tf_op jit(solution)/shard_map/ppermute | solution.py:792
  5.7 5.0 %front.1 = (f32[144,2304]{1,0:T(8,128)}, bf16[1536,128]{1,0:T(8,128)(2,1)}, f32[128,2304]{1,0:T(8,128)}, bf16[128,768]{1,0:T(8,128)(2,1)}) custom-call(s32[9]{0:T(128)} %concatenate.3.meta, bf16[128,768]{1,0:T(8,128)(2,1)} %bitcast.11, bf16[16,768]{1,0:T(8,128)(2,1)} %copy-done.34, bf16[128,768]{1,0:T(8,128)(2,1)} %bitcast.18, bf16[768]{0:T(1024)(128)(2,1)} %refs_3_.5, ...), custom_call_target="tpu_custom_call" | custom-call | flops 3300000000 | tf_op jit(solution)/shard_map/front/pallas_call | solution.py:56
  10.8 4.5 %collective-permute-start.1 = (bf16[128,768]{1,0:T(8,128)(2,1)}, bf16[128,768]{1,0:T(8,128)(2,1)S(1)}, u32[]{:S(2)}, u32[]{:S(2)}) collective-permute-start(bf16[128,768]{1,0:T(8,128)(2,1)} %get-tuple-element.91.refs_10_.refs_2_.refs_0_.carried), channel_id=1, source_target_pairs={{0,2},{1,3},{2,0},{3,1},{4,6},{5,7},{6,4},{7,5},{8,10},{9,11},{10,... | collective-permute-start | bytes 589832 | tf_op jit(solution)/shard_map/ppermute | solution.py:796
  15.3 2.6 %collective-permute-start.2 = (bf16[128,768]{1,0:T(8,128)(2,1)}, bf16[128,768]{1,0:T(8,128)(2,1)S(1)}, u32[]{:S(2)}, u32[]{:S(2)}) collective-permute-start(bf16[128,768]{1,0:T(8,128)(2,1)} %get-tuple-element.91.refs_10_.refs_2_.refs_0_.carried), channel_id=1, source_target_pairs={{0,4},{1,5},{2,6},{3,7},{4,0},{5,1},{6,2},{7,3},{8,12},{9,13},{10,... | collective-permute-start | bytes 589832 | tf_op jit(solution)/shard_map/ppermute | solution.py:796
  20.4 5.4 %filter.1 = (f32[8,256,768]{2,1,0:T(8,128)S(1)}, f32[1024,768]{1,0:T(8,128)S(1)}, f32[192,1024]{1,0:T(8,128)S(1)}, f32[192,1024]{1,0:T(8,128)S(1)}, f32[192,1024]{1,0:T(8,128)S(1)}) custom-call(s32[9]{0:T(128)S(1)} %copy-done.3, f32[40,1024]{1,0:T(8,128)S(1)} %copy-done.27, bf16[33,64]{1,0:T(8,128)(2,1)S(1)} %copy-done.12, bf16[64]{0:T(256)(128)(2,1)S(1)} %copy-done.20, ...), custom_call_target="tpu_custom_call" | custom-call | flops 8800000000 | tf_op jit(solution)/shard_map/filter/pallas_call | solution.py:56
  27.5 5.2 %collective-permute-done.2.refs_4_.refs_2_ = bf16[128,768]{1,0:T(8,128)(2,1)S(1)} collective-permute-done((bf16[128,768]{1,0:T(8,128)(2,1)}, bf16[128,768]{1,0:T(8,128)(2,1)S(1)}, u32[]{:S(2)}, u32[]{:S(2)}) %collective-permute-start.2) | collective-permute-done | bytes 196640 | tf_op jit(solution)/shard_map/ppermute | solution.py:796
  33.7 3.1 %collective-permute-done.5.refs_4_.refs_7_.refs_5_ = bf16[5376,128]{1,0:T(8,128)(2,1)S(1)} collective-permute-done((bf16[5376,128]{1,0:T(8,128)(2,1)S(1)}, bf16[5376,128]{1,0:T(8,128)(2,1)S(1)}, u32[]{:S(2)}, u32[]{:S(2)}) %collective-permute-start.5) | collective-permute-done | bytes 1376288 | tf_op jit(solution)/shard_map/ppermute | solution.py:796
  36.9 2.9 %conv.1 = f32[128,768]{1,0:T(8,128)S(1)} custom-call(s32[9]{0:T(128)S(1)} %copy-done.3, bf16[128,768]{1,0:T(8,128)(2,1)S(1)} %copy-done.1, bf16[128,768]{1,0:T(8,128)(2,1)S(1)} %collective-permute-done.1.refs_3_.refs_1_, bf16[128,768]{1,0:T(8,128)(2,1)S(1)} %collective-permute-done.2.refs_4_.refs_2_, ...), custom_call_target="tpu_custom_call" | custom-call | flops 3300000000 | tf_op jit(solution)/shard_map/conv/pallas_call | solution.py:1163
  40.0 9.9 %mlp.1 = (bf16[128,768]{1,0:T(8,128)(2,1)}, f32[128,768]{1,0:T(8,128)S(1)}, f32[128,768]{1,0:T(8,128)S(1)}, bf16[128,768]{1,0:T(8,128)(2,1)S(1)}, f32[128,768]{1...) custom-call(s32[9]{0:T(128)S(1)} %copy-done.3, ...), custom_call_target="tpu_custom_call" | custom-call | flops 11000000512 | tf_op jit(solution)/shard_map/mlp/pallas_call | solution.py:1190
  52.9 2.5 %collective-permute-start.6 = (bf16[128,768]{1,0:T(8,128)(2,1)S(1)}, bf16[128,768]{1,0:T(8,128)(2,1)S(1)}, u32[]{:S(2)}, u32[]{:S(2)}) collective-permute-start(bf16[128,768]{1,0:T(8,128)(2,1)S(1)} %get-tuple-element.97.refs_2_.refs_0_), channel_id=1, source_target_pairs={{0,2},{1,3},{2,0},{3,1},{4,6},{5,7},{6,4},{7,5},{8,10},{9,11},{10,... | collective-permute-start | bytes 589832 | tf_op jit(solution)/shard_map/ppermute | solution.py:796
  58.5 5.6 %collective-permute-done.6.refs_3_.refs_1_ = bf16[128,768]{1,0:T(8,128)(2,1)S(1)} collective-permute-done((bf16[128,768]{1,0:T(8,128)(2,1)S(1)}, bf16[128,768]{1,0:T(8,128)(2,1)S(1)}, u32[]{:S(2)}, u32[]{:S(2)}) %collective-permute-start.6) | collective-permute-done | bytes 196640 | tf_op jit(solution)/shard_map/ppermute | solution.py:796
  64.0 8.5 %collective-permute-done.7.refs_4_.refs_2_ = bf16[128,768]{1,0:T(8,128)(2,1)S(1)} collective-permute-done((bf16[128,768]{1,0:T(8,128)(2,1)S(1)}, bf16[128,768]{1,0:T(8,128)(2,1)S(1)}, u32[]{:S(2)}, u32[]{:S(2)}) %collective-permute-start.7) | collective-permute-done | bytes 196640 | tf_op jit(solution)/shard_map/ppermute | solution.py:796
  73.9 2.6 %taps_grad.1.refs_0_ = f32[8,128,768]{2,1,0:T(8,128)S(1)} custom-call(s32[9]{0:T(128)S(1)} %copy-done.3, bf16[128,768]{1,0:T(8,128)(2,1)S(1)} %copy-done.2, bf16[128,768]{1,0:T(8,128)(2,1)S(1)} %collective-permute-done.1.refs_3_.refs_1_, bf16[128,768]{1,0:T(8,128)(2,1)S(1)} %collective-permute-done.2.refs_4_.refs_2_, ...), custom_call_target="tpu_custom_call" | custom-call | flops 4400000000 | tf_op jit(solution)/shard_map/taps_grad/pallas_call | solution.py:1217
  76.5 4.3 %filter_back.1 = (f32[24,1792]{1,0:T(8,128)S(1)}, f32[24,1792]{1,0:T(8,128)S(1)}) custom-call(s32[9]{0:T(128)S(1)} %copy-done.3, f32[8,128,768]{2,1,0:T(8,128)S(1)} %taps_grad.1.refs_0_, f32[1024,768]{1,0:T(8,128)S(1)} %copy-done.32, f32[192,1024]{1,0:T(8,128)S(1)} %get-tuple-element.120.refs_2_, f32[192,1024]{1,0:T(8,128)S(1)} %get-tuple-element.121.refs_3_, ...), custom_call_target="tpu_custom_call" | custom-call | flops 5500000256 | tf_op jit(solution)/shard_map/filter_back/pallas_call | solution.py:56
  82.3 4.4 %collective-permute-start.20 = (f32[24,1792]{1,0:T(8,128)S(1)}, f32[24,1792]{1,0:T(8,128)S(1)}, u32[]{:S(2)}, u32[]{:S(2)}) collective-permute-start(f32[24,1792]{1,0:T(8,128)S(1)} %add.15), channel_id=1, source_target_pairs={{0,2},{1,3},{2,0},{3,1},{4,6},{5,7},{6,4},{7,5},{8,10},{9,11},{10,... | collective-permute-start | bytes 516104 | tf_op jit(solution)/shard_map/ppermute | solution.py:796
  86.7 5.4 %conv_back.1 = (f32[128,768]{1,0:T(8,128)S(1)}, f32[128,768]{1,0:T(8,128)S(1)}, f32[3,8,768]{2,1,0:T(8,128)S(1)}) custom-call(s32[9]{0:T(128)S(1)} %copy-done.3, bf16[128,768]{1,0:T(8,128)(2,1)S(1)} %get-tuple-element.97.refs_2_.refs_0_, bf16[128,768]{1,0:T(8,128)(2,1)S(1)} %collective-permute-done.6.refs_3_.refs_1_, ...), custom_call_target="tpu_custom_call" | custom-call | flops 4400000000 | tf_op jit(solution)/shard_map/conv_back/pallas_call | solution.py:1256
  95.1 2.0 %up_grad.1 = (bf16[4,96,768]{2,1,0:T(8,128)(2,1)S(1)}, bf16[4,96,768]{2,1,0:T(8,128)(2,1)S(1)}) custom-call(s32[9]{0:T(128)S(1)} %copy-done.3, bf16[1536,128]{1,0:T(8,128)(2,1)S(1)} %get-tuple-element.105.refs_0_, bf16[3456,128]{1,0:T(8,128)(2,1)S(1)} %get-tuple-element.106.refs_1_, bf16[3456,128]{1,0:T(8,128)(2,1)S(1)} %collective-permute-done.13.refs_2_, ...), custom_call_target="tpu_custom_call" | custom-call | flops 3300000000 | tf_op jit(solution)/shard_map/up_grad/pallas_call | solution.py:56
  97.1 2.7 %short_back.1 = (bf16[128,2304]{1,0:T(8,128)(2,1)S(1)}, f32[24,768]{1,0:T(8,128)S(1)}, bf16[1152,128]{1,0:T(8,128)(2,1)S(1)}, bf16[1152,128]{1,0:T(8,128)(2,1)S(1)}) custom-call(s32[9]{0:T(128)S(1)} %copy-done.3, f32[128,768]{1,0:T(8,128)S(1)} %get-tuple-element.96.refs_12_.refs_0_, f32[128,768]{1,0:T(8,128)S(1)} %get-tuple-element.101.refs_1_, ...), custom_call_target="tpu_custom_call" | custom-call | flops 3300000000 | tf_op jit(solution)/shard_map/short_back/pallas_call | solution.py:56
  104.1 7.2 %collective-permute-done.21 = f32[24,1792]{1,0:T(8,128)S(1)} collective-permute-done((f32[24,1792]{1,0:T(8,128)S(1)}, f32[24,1792]{1,0:T(8,128)S(1)}, u32[]{:S(2)}, u32[]{:S(2)}) %collective-permute-start.21) | collective-permute-done | bytes 172064 | tf_op jit(solution)/shard_map/ppermute | solution.py:796
  112.0 10.3 %collective-permute-done.15.refs_3_ = bf16[4,96,768]{2,1,0:T(8,128)(2,1)S(1)} collective-permute-done((bf16[4,96,768]{2,1,0:T(8,128)(2,1)S(1)}, bf16[4,96,768]{2,1,0:T(8,128)(2,1)S(1)}, u32[]{:S(2)}, u32[]{:S(2)}) %collective-permute-start.15) | collective-permute-done | bytes 589856 | tf_op jit(solution)/shard_map/ppermute | solution.py:796
  123.2 1.8 collective-permute-start.17
  125.0 2.6 %collective-permute-start.18 = (bf16[96,1792]{1,0:T(8,128)(2,1)S(1)}, bf16[96,1792]{1,0:T(8,128)(2,1)S(1)}, u32[]{:S(2)}, u32[]{:S(2)}) collective-permute-start(bf16[96,1792]{1,0:T(8,128)(2,1)S(1)} %get-tuple-element.118), channel_id=1, source_target_pairs={{0,6},{1,7},{2,4},{3,5},{4,2},{5,3},{6,0},{7,1},{8,14},{9,15},{10,... | collective-permute-start | bytes 1032200 | tf_op jit(solution)/shard_map/ppermute | solution.py:796
  129.5 2.7 %tail.1 = (f32[128,768]{1,0:T(8,128)}, f32[16,1152]{1,0:T(8,128)S(1)}) custom-call(s32[9]{0:T(128)S(1)} %copy-done.3, bf16[128,2304]{1,0:T(8,128)(2,1)S(1)} %get-tuple-element.109.refs_0_, bf16[768,2304]{1,0:T(8,128)(2,1)S(1)} %copy-done.5, bf16[128,768]{1,0:T(8,128)(2,1)S(1)} %bitcast.13, bf16[768]{0:T(1024)(128)(2,1)S(1)} %copy-done.19, ...), custom_call_target="tpu_custom_call" | custom-call | flops 2750000128 | tf_op jit(solution)/shard_map/tail/pallas_call | solution.py:56
  132.2 7.8 %collective-permute-done.16.refs_1_ = bf16[96,1792]{1,0:T(8,128)(2,1)S(1)} collective-permute-done((bf16[96,1792]{1,0:T(8,128)(2,1)S(1)}, bf16[96,1792]{1,0:T(8,128)(2,1)S(1)}, u32[]{:S(2)}, u32[]{:S(2)}) %collective-permute-start.16) | collective-permute-done | bytes 344096 | tf_op jit(solution)/shard_map/ppermute | solution.py:796
  140.1 9.8 %collective-permute-done.17.refs_2_ = bf16[96,1792]{1,0:T(8,128)(2,1)S(1)} collective-permute-done((bf16[96,1792]{1,0:T(8,128)(2,1)S(1)}, bf16[96,1792]{1,0:T(8,128)(2,1)S(1)}, u32[]{:S(2)}, u32[]{:S(2)}) %collective-permute-start.17) | collective-permute-done | bytes 344096 | tf_op jit(solution)/shard_map/ppermute | solution.py:796
  151.7 2.4 %collective-permute-start.24 = (bf16[128,1792]{1,0:T(8,128)(2,1)S(1)}, bf16[128,1792]{1,0:T(8,128)(2,1)S(1)}, u32[]{:S(2)}, u32[]{:S(2)}) collective-permute-start(bf16[128,1792]{1,0:T(8,128)(2,1)S(1)} %total.2.refs_0_), channel_id=1, source_target_pairs={{0,24},{8,16},{16,8},{24,0},{1,25},{9,17},{17,9},{25,1},{2,26},{10... | collective-permute-start | bytes 1376264 | tf_op jit(solution)/shard_map/ppermute | solution.py:796
  154.8 7.2 %collective-permute-start.30 = (bf16[64,1152]{1,0:T(8,128)(2,1)S(1)}, bf16[64,1152]{1,0:T(8,128)(2,1)S(1)}, u32[]{:S(2)}, u32[]{:S(2)}) collective-permute-start(bf16[64,1152]{1,0:T(8,128)(2,1)S(1)} %get-tuple-element.132), channel_id=1, source_target_pairs={{0,2},{1,3},{2,0},{3,1},{4,6},{5,7},{6,4},{7,5},{8,10},{9,11},{10,... | collective-permute-start | bytes 442376 | tf_op jit(solution)/shard_map/ppermute | solution.py:796
  162.6 3.7 %collective-permute-done.30.refs_1_ = bf16[64,1152]{1,0:T(8,128)(2,1)S(1)} collective-permute-done((bf16[64,1152]{1,0:T(8,128)(2,1)S(1)}, bf16[64,1152]{1,0:T(8,128)(2,1)S(1)}, u32[]{:S(2)}, u32[]{:S(2)}) %collective-permute-start.30) | collective-permute-done | bytes 147488 | tf_op jit(solution)/shard_map/ppermute | solution.py:796
  166.2 1.8 collective-permute-start.32
  168.0 6.4 %collective-permute-done.31.refs_2_ = bf16[64,1152]{1,0:T(8,128)(2,1)S(1)} collective-permute-done((bf16[64,1152]{1,0:T(8,128)(2,1)S(1)}, bf16[64,1152]{1,0:T(8,128)(2,1)S(1)}, u32[]{:S(2)}, u32[]{:S(2)}) %collective-permute-start.31) | collective-permute-done | bytes 147488 | tf_op jit(solution)/shard_map/ppermute | solution.py:796
  176.2 2.4 %collective-permute-start.35 = (bf16[64,1152]{1,0:T(8,128)(2,1)S(1)}, bf16[64,1152]{1,0:T(8,128)(2,1)S(1)}, u32[]{:S(2)}, u32[]{:S(2)}) collective-permute-start(bf16[64,1152]{1,0:T(8,128)(2,1)S(1)} %total.3.refs_2_.refs_0_), channel_id=1, source_target_pairs={{0,24},{8,16},{16,8},{24,0},{1,25},{9,17},{17,9},{25,1},{2,26},{10... | collective-permute-start | bytes 442376 | tf_op jit(solution)/shard_map/ppermute | solution.py:796
  179.3 2.2 %place_early.1 = (f32[384,768]{1,0:T(8,128)}, f32[96,768]{1,0:T(8,128)}, f32[96,3072]{1,0:T(8,128)}) custom-call(s32[9]{0:T(128)S(1)} %copy-done.3, bf16[128,1792]{1,0:T(8,128)(2,1)S(1)} %total.2.refs_0_, bf16[128,1792]{1,0:T(8,128)(2,1)S(1)} %collective-permute-done.22.refs_1_, bf16[128,1792]{1,0:T(8,128)(2,1)S(1)} %collective-permute-done.23.refs_2_, ...), custom_call_target="tpu_custom_call" | custom-call | flops 1650000000 | tf_op jit(solution)/shard_map/place_early/pallas_call | solution.py:56
  (148 shorter events, 36.5 us)
Async XLA Ops:
  10.8 16.7 %collective-permute-start.1 = (bf16[128,768]{1,0:T(8,128)(2,1)}, bf16[128,768]{1,0:T(8,128)(2,1)S(1)}, u32[]{:S(2)}, u32[]{:S(2)}) collective-permute-start(bf16[128,768]{1,0:T(8,128)(2,1)} %get-tuple-element.91.refs_10_.refs_2_.refs_0_.carried), channel_id=1, source_target_pairs={{0,2},{1,3},{2,0},{3,1},{4,6},{5,7},{6,4},{7,5},{8,10},{9,11},{10,... | collective-permute-start | bytes 589832 | tf_op jit(solution)/shard_map/ppermute | solution.py:796
  15.3 17.4 %collective-permute-start.2 = (bf16[128,768]{1,0:T(8,128)(2,1)}, bf16[128,768]{1,0:T(8,128)(2,1)S(1)}, u32[]{:S(2)}, u32[]{:S(2)}) collective-permute-start(bf16[128,768]{1,0:T(8,128)(2,1)} %get-tuple-element.91.refs_10_.refs_2_.refs_0_.carried), channel_id=1, source_target_pairs={{0,4},{1,5},{2,6},{3,7},{4,0},{5,1},{6,2},{7,3},{8,12},{9,13},{10,... | collective-permute-start | bytes 589832 | tf_op jit(solution)/shard_map/ppermute | solution.py:796
  17.9 14.8 %collective-permute-start.3 = (bf16[128,768]{1,0:T(8,128)(2,1)}, bf16[128,768]{1,0:T(8,128)(2,1)S(1)}, u32[]{:S(2)}, u32[]{:S(2)}) collective-permute-start(bf16[128,768]{1,0:T(8,128)(2,1)} %get-tuple-element.91.refs_10_.refs_2_.refs_0_.carried), channel_id=1, source_target_pairs={{0,6},{1,7},{2,4},{3,5},{4,2},{5,3},{6,0},{7,1},{8,14},{9,15},{10,... | collective-permute-start | bytes 589832 | tf_op jit(solution)/shard_map/ppermute | solution.py:796
  17.9 14.8 %collective-permute-start.4 = (bf16[1536,128]{1,0:T(8,128)(2,1)}, bf16[1536,128]{1,0:T(8,128)(2,1)S(1)}, u32[]{:S(2)}, u32[]{:S(2)}) collective-permute-start(bf16[1536,128]{1,0:T(8,128)(2,1)} %get-tuple-element.92.refs_0_.refs_5_.refs_3_), channel_id=1, source_target_pairs={{0,8},{8,0},{16,24},{24,16},{1,9},{9,1},{17,25},{25,17},{2,10},{10... | collective-permute-start | bytes 1179656 | tf_op jit(solution)/shard_map/ppermute | solution.py:796
  49.9 22.7 %collective-permute-start.9 = (bf16[2688,128]{1,0:T(8,128)(2,1)S(1)}, bf16[2688,128]{1,0:T(8,128)(2,1)S(1)}, u32[]{:S(2)}, u32[]{:S(2)}) collective-permute-start(bf16[2688,128]{1,0:T(8,128)(2,1)S(1)} %get-tuple-element.98), channel_id=1, source_target_pairs={{0,8},{8,0},{16,24},{24,16},{1,9},{9,1},{17,25},{25,17},{2,10},{10... | collective-permute-start | bytes 2064392 | tf_op jit(solution)/shard_map/ppermute | solution.py:796
  51.4 21.2 %collective-permute-start.10 = (bf16[2304,128]{1,0:T(8,128)(2,1)S(1)}, bf16[2304,128]{1,0:T(8,128)(2,1)S(1)}, u32[]{:S(2)}, u32[]{:S(2)}) collective-permute-start(bf16[2304,128]{1,0:T(8,128)(2,1)S(1)} %get-tuple-element.99), channel_id=1, source_target_pairs={{0,16},{8,24},{16,0},{24,8},{1,17},{9,25},{17,1},{25,9},{2,18},{10... | collective-permute-start | bytes 1769480 | tf_op jit(solution)/shard_map/ppermute | solution.py:796
  52.9 11.1 %collective-permute-start.6 = (bf16[128,768]{1,0:T(8,128)(2,1)S(1)}, bf16[128,768]{1,0:T(8,128)(2,1)S(1)}, u32[]{:S(2)}, u32[]{:S(2)}) collective-permute-start(bf16[128,768]{1,0:T(8,128)(2,1)S(1)} %get-tuple-element.97.refs_2_.refs_0_), channel_id=1, source_target_pairs={{0,2},{1,3},{2,0},{3,1},{4,6},{5,7},{6,4},{7,5},{8,10},{9,11},{10,... | collective-permute-start | bytes 589832 | tf_op jit(solution)/shard_map/ppermute | solution.py:796
  55.4 17.1 %collective-permute-start.7 = (bf16[128,768]{1,0:T(8,128)(2,1)S(1)}, bf16[128,768]{1,0:T(8,128)(2,1)S(1)}, u32[]{:S(2)}, u32[]{:S(2)}) collective-permute-start(bf16[128,768]{1,0:T(8,128)(2,1)S(1)} %get-tuple-element.97.refs_2_.refs_0_), channel_id=1, source_target_pairs={{0,4},{1,5},{2,6},{3,7},{4,0},{5,1},{6,2},{7,3},{8,12},{9,13},{10,... | collective-permute-start | bytes 589832 | tf_op jit(solution)/shard_map/ppermute | solution.py:796
  57.0 15.5 %collective-permute-start.8 = (bf16[128,768]{1,0:T(8,128)(2,1)S(1)}, bf16[128,768]{1,0:T(8,128)(2,1)S(1)}, u32[]{:S(2)}, u32[]{:S(2)}) collective-permute-start(bf16[128,768]{1,0:T(8,128)(2,1)S(1)} %get-tuple-element.97.refs_2_.refs_0_), channel_id=1, source_target_pairs={{0,6},{1,7},{2,4},{3,5},{4,2},{5,3},{6,0},{7,1},{8,14},{9,15},{10,... | collective-permute-start | bytes 589832 | tf_op jit(solution)/shard_map/ppermute | solution.py:796
  73.3 13.4 %collective-permute-start.11 = (bf16[6528,128]{1,0:T(8,128)(2,1)S(1)}, bf16[6528,128]{1,0:T(8,128)(2,1)S(1)}, u32[]{:S(2)}, u32[]{:S(2)}) collective-permute-start(bf16[6528,128]{1,0:T(8,128)(2,1)S(1)} %collect.4.refs_12_), channel_id=1, source_target_pairs={{0,1},{1,0},{2,3},{3,2},{4,5},{5,4},{6,7},{7,6},{8,9},{9,8},{10,11... | collective-permute-start | bytes 5013512 | tf_op jit(solution)/shard_map/ppermute | solution.py:796
  73.4 20.0 %collective-permute-start.13 = (bf16[3456,128]{1,0:T(8,128)(2,1)S(1)}, bf16[3456,128]{1,0:T(8,128)(2,1)S(1)}, u32[]{:S(2)}, u32[]{:S(2)}) collective-permute-start(bf16[3456,128]{1,0:T(8,128)(2,1)S(1)} %get-tuple-element.106.refs_1_), channel_id=1, source_target_pairs={{0,1},{1,0},{2,3},{3,2},{4,5},{5,4},{6,7},{7,6},{8,9},{9,8},{10,11... | collective-permute-start | bytes 2654216 | tf_op jit(solution)/shard_map/ppermute | solution.py:796
  82.3 18.6 %collective-permute-start.20 = (f32[24,1792]{1,0:T(8,128)S(1)}, f32[24,1792]{1,0:T(8,128)S(1)}, u32[]{:S(2)}, u32[]{:S(2)}) collective-permute-start(f32[24,1792]{1,0:T(8,128)S(1)} %add.15), channel_id=1, source_target_pairs={{0,2},{1,3},{2,0},{3,1},{4,6},{5,7},{6,4},{7,5},{8,10},{9,11},{10,... | collective-permute-start | bytes 516104 | tf_op jit(solution)/shard_map/ppermute | solution.py:796
  92.1 5.0 %collective-permute-start.12 = (f32[3,8,768]{2,1,0:T(8,128)S(1)}, f32[3,8,768]{2,1,0:T(8,128)S(1)}, u32[]{:S(2)}, u32[]{:S(2)}) collective-permute-start(f32[3,8,768]{2,1,0:T(8,128)S(1)} %get-tuple-element.103.refs_8_.refs_5_), channel_id=1, source_target_pairs={{1,0},{2,1},{3,2},{4,3},{5,4},{6,5},{7,6},{9,8},{10,9},{11,10},{12... | collective-permute-start | bytes 221192 | tf_op jit(solution)/shard_map/ppermute | solution.py:792
  99.8 11.4 %collective-permute-start.26 = (bf16[1152,128]{1,0:T(8,128)(2,1)S(1)}, bf16[1152,128]{1,0:T(8,128)(2,1)S(1)}, u32[]{:S(2)}, u32[]{:S(2)}) collective-permute-start(bf16[1152,128]{1,0:T(8,128)(2,1)S(1)} %get-tuple-element.127), channel_id=1, source_target_pairs={{0,8},{8,0},{16,24},{24,16},{1,9},{9,1},{17,25},{25,17},{2,10},{10... | collective-permute-start | bytes 884744 | tf_op jit(solution)/shard_map/ppermute | solution.py:796
  100.5 21.8 %collective-permute-start.14 = (bf16[4,96,1024]{2,1,0:T(8,128)(2,1)S(1)}, bf16[4,96,1024]{2,1,0:T(8,128)(2,1)S(1)}, u32[]{:S(2)}, u32[]{:S(2)}) collective-permute-start(bf16[4,96,1024]{2,1,0:T(8,128)(2,1)S(1)} %get-tuple-element.113), channel_id=1, source_target_pairs={{0,16},{8,24},{16,0},{24,8},{1,17},{9,25},{17,1},{25,9},{2,18},{10... | collective-permute-start | bytes 2359304 | tf_op jit(solution)/shard_map/ppermute | solution.py:796
  101.0 10.3 %collective-permute-start.21 = (f32[24,1792]{1,0:T(8,128)S(1)}, f32[24,1792]{1,0:T(8,128)S(1)}, u32[]{:S(2)}, u32[]{:S(2)}) collective-permute-start(f32[24,1792]{1,0:T(8,128)S(1)} %add.16), channel_id=1, source_target_pairs={{0,4},{1,5},{2,6},{3,7},{4,0},{5,1},{6,2},{7,3},{8,12},{9,13},{10,... | collective-permute-start | bytes 516104 | tf_op jit(solution)/shard_map/ppermute | solution.py:796
  102.6 19.7 %collective-permute-start.15 = (bf16[4,96,768]{2,1,0:T(8,128)(2,1)S(1)}, bf16[4,96,768]{2,1,0:T(8,128)(2,1)S(1)}, u32[]{:S(2)}, u32[]{:S(2)}) collective-permute-start(bf16[4,96,768]{2,1,0:T(8,128)(2,1)S(1)} %get-tuple-element.114), channel_id=1, source_target_pairs={{0,8},{8,0},{16,24},{24,16},{1,9},{9,1},{17,25},{25,17},{2,10},{10... | collective-permute-start | bytes 1769480 | tf_op jit(solution)/shard_map/ppermute | solution.py:796
  111.9 15.7 %collective-permute-start.27 = (bf16[2304,128]{1,0:T(8,128)(2,1)S(1)}, bf16[2304,128]{1,0:T(8,128)(2,1)S(1)}, u32[]{:S(2)}, u32[]{:S(2)}) collective-permute-start(bf16[2304,128]{1,0:T(8,128)(2,1)S(1)} %collect.5), channel_id=1, source_target_pairs={{0,1},{1,0},{2,3},{3,2},{4,5},{5,4},{6,7},{7,6},{8,9},{9,8},{10,11... | collective-permute-start | bytes 1769480 | tf_op jit(solution)/shard_map/ppermute | solution.py:796
  123.1 16.9 %collective-permute-start.16 = (bf16[96,1792]{1,0:T(8,128)(2,1)S(1)}, bf16[96,1792]{1,0:T(8,128)(2,1)S(1)}, u32[]{:S(2)}, u32[]{:S(2)}) collective-permute-start(bf16[96,1792]{1,0:T(8,128)(2,1)S(1)} %get-tuple-element.116), channel_id=1, source_target_pairs={{0,2},{1,3},{2,0},{3,1},{4,6},{5,7},{6,4},{7,5},{8,10},{9,11},{10,... | collective-permute-start | bytes 1032200 | tf_op jit(solution)/shard_map/ppermute | solution.py:796
  123.2 26.7 %collective-permute-start.17 = (bf16[96,1792]{1,0:T(8,128)(2,1)S(1)}, bf16[96,1792]{1,0:T(8,128)(2,1)S(1)}, u32[]{:S(2)}, u32[]{:S(2)}) collective-permute-start(bf16[96,1792]{1,0:T(8,128)(2,1)S(1)} %get-tuple-element.117), channel_id=1, source_target_pairs={{0,4},{1,5},{2,6},{3,7},{4,0},{5,1},{6,2},{7,3},{8,12},{9,13},{10,... | collective-permute-start | bytes 1032200 | tf_op jit(solution)/shard_map/ppermute | solution.py:796
  125.0 24.8 %collective-permute-start.18 = (bf16[96,1792]{1,0:T(8,128)(2,1)S(1)}, bf16[96,1792]{1,0:T(8,128)(2,1)S(1)}, u32[]{:S(2)}, u32[]{:S(2)}) collective-permute-start(bf16[96,1792]{1,0:T(8,128)(2,1)S(1)} %get-tuple-element.118), channel_id=1, source_target_pairs={{0,6},{1,7},{2,4},{3,5},{4,2},{5,3},{6,0},{7,1},{8,14},{9,15},{10,... | collective-permute-start | bytes 1032200 | tf_op jit(solution)/shard_map/ppermute | solution.py:796
  128.9 25.3 %collective-permute-start.28 = (bf16[4,48,1152]{2,1,0:T(8,128)(2,1)S(1)}, bf16[4,48,1152]{2,1,0:T(8,128)(2,1)S(1)}, u32[]{:S(2)}, u32[]{:S(2)}) collective-permute-start(bf16[4,48,1152]{2,1,0:T(8,128)(2,1)S(1)} %get-tuple-element.129), channel_id=1, source_target_pairs={{0,16},{8,24},{16,0},{24,8},{1,17},{9,25},{17,1},{25,9},{2,18},{10... | collective-permute-start | bytes 1327112 | tf_op jit(solution)/shard_map/ppermute | solution.py:796
  132.2 22.0 %collective-permute-start.29 = (f32[16,1152]{1,0:T(8,128)S(1)}, f32[16,1152]{1,0:T(8,128)S(1)}, u32[]{:S(2)}, u32[]{:S(2)}) collective-permute-start(f32[16,1152]{1,0:T(8,128)S(1)} %get-tuple-element.130.refs_2_), channel_id=1, source_target_pairs={{0,1},{1,0},{2,3},{3,2},{4,5},{5,4},{6,7},{7,6},{8,9},{9,8},{10,11... | collective-permute-start | bytes 221192 | tf_op jit(solution)/shard_map/ppermute | solution.py:796
  150.6 25.6 %collective-permute-start.22 = (bf16[128,1792]{1,0:T(8,128)(2,1)S(1)}, bf16[128,1792]{1,0:T(8,128)(2,1)S(1)}, u32[]{:S(2)}, u32[]{:S(2)}) collective-permute-start(bf16[128,1792]{1,0:T(8,128)(2,1)S(1)} %total.2.refs_0_), channel_id=1, source_target_pairs={{0,8},{8,0},{16,24},{24,16},{1,9},{9,1},{17,25},{25,17},{2,10},{10... | collective-permute-start | bytes 1376264 | tf_op jit(solution)/shard_map/ppermute | solution.py:796
  151.2 27.4 %collective-permute-start.23 = (bf16[128,1792]{1,0:T(8,128)(2,1)S(1)}, bf16[128,1792]{1,0:T(8,128)(2,1)S(1)}, u32[]{:S(2)}, u32[]{:S(2)}) collective-permute-start(bf16[128,1792]{1,0:T(8,128)(2,1)S(1)} %total.2.refs_0_), channel_id=1, source_target_pairs={{0,16},{8,24},{16,0},{24,8},{1,17},{9,25},{17,1},{25,9},{2,18},{10... | collective-permute-start | bytes 1376264 | tf_op jit(solution)/shard_map/ppermute | solution.py:796
  151.7 26.9 %collective-permute-start.24 = (bf16[128,1792]{1,0:T(8,128)(2,1)S(1)}, bf16[128,1792]{1,0:T(8,128)(2,1)S(1)}, u32[]{:S(2)}, u32[]{:S(2)}) collective-permute-start(bf16[128,1792]{1,0:T(8,128)(2,1)S(1)} %total.2.refs_0_), channel_id=1, source_target_pairs={{0,24},{8,16},{16,8},{24,0},{1,25},{9,17},{17,9},{25,1},{2,26},{10... | collective-permute-start | bytes 1376264 | tf_op jit(solution)/shard_map/ppermute | solution.py:796
  154.8 11.4 %collective-permute-start.30 = (bf16[64,1152]{1,0:T(8,128)(2,1)S(1)}, bf16[64,1152]{1,0:T(8,128)(2,1)S(1)}, u32[]{:S(2)}, u32[]{:S(2)}) collective-permute-start(bf16[64,1152]{1,0:T(8,128)(2,1)S(1)} %get-tuple-element.132), channel_id=1, source_target_pairs={{0,2},{1,3},{2,0},{3,1},{4,6},{5,7},{6,4},{7,5},{8,10},{9,11},{10,... | collective-permute-start | bytes 442376 | tf_op jit(solution)/shard_map/ppermute | solution.py:796
  162.0 12.4 %collective-permute-start.31 = (bf16[64,1152]{1,0:T(8,128)(2,1)S(1)}, bf16[64,1152]{1,0:T(8,128)(2,1)S(1)}, u32[]{:S(2)}, u32[]{:S(2)}) collective-permute-start(bf16[64,1152]{1,0:T(8,128)(2,1)S(1)} %get-tuple-element.133), channel_id=1, source_target_pairs={{0,4},{1,5},{2,6},{3,7},{4,0},{5,1},{6,2},{7,3},{8,12},{9,13},{10,... | collective-permute-start | bytes 442376 | tf_op jit(solution)/shard_map/ppermute | solution.py:796
  166.2 8.2 %collective-permute-start.32 = (bf16[64,1152]{1,0:T(8,128)(2,1)S(1)}, bf16[64,1152]{1,0:T(8,128)(2,1)S(1)}, u32[]{:S(2)}, u32[]{:S(2)}) collective-permute-start(bf16[64,1152]{1,0:T(8,128)(2,1)S(1)} %get-tuple-element.134), channel_id=1, source_target_pairs={{0,6},{1,7},{2,4},{3,5},{4,2},{5,3},{6,0},{7,1},{8,14},{9,15},{10,... | collective-permute-start | bytes 442376 | tf_op jit(solution)/shard_map/ppermute | solution.py:796
  175.0 6.4 %collective-permute-start.33 = (bf16[64,1152]{1,0:T(8,128)(2,1)S(1)}, bf16[64,1152]{1,0:T(8,128)(2,1)S(1)}, u32[]{:S(2)}, u32[]{:S(2)}) collective-permute-start(bf16[64,1152]{1,0:T(8,128)(2,1)S(1)} %total.3.refs_2_.refs_0_), channel_id=1, source_target_pairs={{0,8},{8,0},{16,24},{24,16},{1,9},{9,1},{17,25},{25,17},{2,10},{10... | collective-permute-start | bytes 442376 | tf_op jit(solution)/shard_map/ppermute | solution.py:796
  175.7 6.7 %collective-permute-start.34 = (bf16[64,1152]{1,0:T(8,128)(2,1)S(1)}, bf16[64,1152]{1,0:T(8,128)(2,1)S(1)}, u32[]{:S(2)}, u32[]{:S(2)}) collective-permute-start(bf16[64,1152]{1,0:T(8,128)(2,1)S(1)} %total.3.refs_2_.refs_0_), channel_id=1, source_target_pairs={{0,16},{8,24},{16,0},{24,8},{1,17},{9,25},{17,1},{25,9},{2,18},{10... | collective-permute-start | bytes 442376 | tf_op jit(solution)/shard_map/ppermute | solution.py:796
  176.2 6.2 %collective-permute-start.35 = (bf16[64,1152]{1,0:T(8,128)(2,1)S(1)}, bf16[64,1152]{1,0:T(8,128)(2,1)S(1)}, u32[]{:S(2)}, u32[]{:S(2)}) collective-permute-start(bf16[64,1152]{1,0:T(8,128)(2,1)S(1)} %total.3.refs_2_.refs_0_), channel_id=1, source_target_pairs={{0,24},{8,16},{16,8},{24,0},{1,25},{9,17},{17,9},{25,1},{2,26},{10... | collective-permute-start | bytes 442376 | tf_op jit(solution)/shard_map/ppermute | solution.py:796
  (43 other events, 352.6 us)

commit v4 on v3

--- a/solution.py
+++ b/solution.py
@@ -16,6 +16,8 @@
 F32 = jnp.float32
 BF16 = jnp.bfloat16
 RIM = 16
+OTHER_ROWS = 496
+SMALL_BLOCK = 80
 LATE_ROWS = tuple(range(15)) + (22, 23)
 VMEM_LIMIT = 26 * 1024 * 1024
 GELU_C = math.sqrt(2.0 / math.pi)
@@ -738,11 +740,16 @@
     wh, wl = high_low(weighted)
     ah, al = high_low(act[2 * fwidth :, :])
     packed[...] = jnp.zeros_like(packed)
-    half = fwidth // 2
     made = dot(ah, wh) + (dot(ah, wl) + dot(al, wh))
-    packed[:half, :width] = made[:half]
-    packed[:half, width : 2 * width] = made[half:]
-    packed[half : half + others.shape[0], 256 : 256 + others.shape[1]] = others[...]
+    place = 0
+    for t in range(width // 128):
+        packed[place : place + fwidth, :] = made[:, t * 128 : (t + 1) * 128]
+        place += fwidth
+    for i in range(others.shape[0]):
+        count = others.shape[1] // 128 if i >= 5 else width // 128
+        for t in range(count):
+            row = OTHER_ROWS + (i * 6 + t if i < 5 else 30 + (i - 5) * count + t)
+            packed[row : row + 1, :] = others[i : i + 1, t * 128 : (t + 1) * 128]
     back = dot_t(last[...], wh) + dot_t(last[...], wl)
     ones = jnp.ones((8, length), BF16)
 
@@ -756,7 +763,6 @@
         return (dot_t(ones, high) + dot_t(ones, low))[:1]
 
     freq_total = jnp.zeros((1, fwidth), F32)
-    place = 2 * width
     for i, weight in ((2, third), (1, second), (0, first)):
         rows = slice(i * fwidth, (i + 1) * fwidth)
         step = back * slope[rows, :]
@@ -764,27 +770,18 @@
         step = step * scale
         below = act[(i - 1) * fwidth : i * fwidth, :] if i else table[...]
         made = wide_t(below, step)
-        if i:
-            packed[:half, place : place + fwidth] = made[:half]
-            packed[:half, place + fwidth : place + 2 * fwidth] = made[half:]
-            place += 2 * fwidth
-        else:
-            for part in range(0, made.shape[0], 16):
-                lanes = slice(part // 16 * fwidth, part // 16 * fwidth + fwidth)
-                piece = made[part : part + 16]
-                packed[half : half + piece.shape[0], lanes] = piece
-        packed[half + 8 + i : half + 9 + i, 2 * fwidth : 3 * fwidth] = sums(step)
+        at, lanes = ((place + fwidth, 0), (place, fwidth), (place, 0))[i]
+        packed[at : at + made.shape[0], lanes : lanes + fwidth] = made
+        packed[place + fwidth + i : place + fwidth + i + 1, fwidth:] = sums(step)
         if i:
             high, low = high_low(step)
             back = dot(weight[...], high) + dot(weight[...], low)
-    packed[half + 11 : half + 12, 2 * fwidth : 3 * fwidth] = freq_total
-    half = packed.shape[0] // 2
-    for side in range(2):
-
-        def store(dest):
-            dest[...] = packed[side * half : (side + 1) * half, :]
-
-        pick(core == side, mine, send, store)
+    packed[place + fwidth + 3 : place + fwidth + 4, fwidth:] = freq_total
+    size = SMALL_BLOCK
+    for z in range(mine.shape[0] // size):
+        out = slice(z * size, (z + 1) * size)
+        mine[out, :] = packed[pl.ds(pl.multiple_of((2 * z + core) * size, 8), size), :]
+        send[out, :] = packed[pl.ds(pl.multiple_of((2 * z + 1 - core) * size, 8), size), :]
 
 
 def shift(block, axis, distance):
@@ -928,10 +925,9 @@
         pick(y == side, keep, send, store)
 
 
-def merge_kernel(pairs, meta, *refs):
+def merge_kernel(pairs, kind, meta, *refs):
     ins, refs = refs[: 2 * pairs], refs[2 * pairs :]
-    rows = ins[0].shape[1]
-    chips = ins[0].shape[0]
+    chips, rows = ins[0].shape[:2]
     extra, (own, *sends) = refs[:-chips], refs[-chips:]
     first = 0
     for p in range(pairs):
@@ -941,85 +937,142 @@
         own[:rows, cols] = keep[0].astype(F32) + got[0].astype(F32)
         for j, dest in enumerate(sends):
             dest[:rows, cols] = (keep[j + 1].astype(F32) + got[j + 1].astype(F32)).astype(BF16)
-    if extra:
+    if kind == "rows":
         value = (extra[0][...] + extra[1][...]).astype(BF16)
         own[rows:, :] = value.astype(F32)
         for dest in sends:
             dest[rows:, :] = value
-
-
-def total_kernel(extras, meta, own, one, two, three, *refs):
-    rows = own.shape[0]
-    out = refs[-1]
-    out[:rows, :] = (
+    if kind == "tiles":
+        size = SMALL_BLOCK
+        for j, dest in enumerate((own, *sends)):
+            take = pl.ds(pl.multiple_of((meta[2] ^ j) * size, 8), size)
+            value = extra[0][take, :] + extra[1][take, :]
+            dest[:size, first:] = value.astype(dest.dtype)
+            dest[size:, first:] = jnp.zeros((rows - size, dest.shape[1] - first), dest.dtype)
+
+
+def total_kernel(meta, own, one, two, three, out):
+    out[...] = (
         (own[...] + one[...].astype(F32)) + (two[...].astype(F32) + three[...].astype(F32))
     ).astype(BF16)
-    if extras:
-        small = refs[0]
-        out[rows : rows + small.shape[0], :] = small[...].astype(BF16)
-        out[rows + small.shape[0] :, :] = jnp.zeros(
-            (out.shape[0] - rows - small.shape[0], out.shape[1]), BF16
-        )
-
-
-def spread_out(meta, pairs, with_merge=(), with_total=()):
+
+
+def chip_sums(meta, pairs, kind, extra):
     chips, rows, _ = pairs[0].shape
     cols = sum(v.shape[2] for v in pairs[::2])
-    rows += with_merge[0].shape[0] if with_merge else 0
+    rows += extra[0].shape[0] if kind == "rows" else 0
+    cols += 128 if kind == "tiles" else 0
     sds = jax.ShapeDtypeStruct
-    own, *sends = single(
-        partial(merge_kernel, len(pairs) // 2), "merge", 1.0,
-        [sds((rows, cols), F32)] + [sds((rows, cols), BF16)] * (chips - 1), meta, (*pairs, *with_merge),
-    )
+    return single(
+        partial(merge_kernel, len(pairs) // 2, kind), "merge", 1.0,
+        [sds((rows, cols), F32)] + [sds((rows, cols), BF16)] * (chips - 1), meta, (*pairs, *extra),
+    )
+
+
+def spread_out(meta, sums, after=()):
+    own, *sends = sums
     got = {j: swap(sends[j - 1], "seq", 2 * j) for j in (2, 3, 1)}
     (total,) = single(
-        partial(total_kernel, len(with_total)), "total", 1.0,
-        [sds((rows + (32 if with_total else 0), cols), BF16)], meta,
-        [own, got[1], got[2], got[3], *with_total],
+        total_kernel, "total", 1.0, [jax.ShapeDtypeStruct(own.shape, BF16)], meta,
+        [own, got[1], got[2], got[3]], after,
     )
     return [total] + [swap(total, "rows", j) for j in (1, 2, 3)]
 
 
-def small_kernel(rows, meta, *refs):
+def merge_halves_kernel(meta, keep, got, left, right, keep_out, send_out):
+    rows = keep.shape[1]
+    for dest, order in ((keep_out, (0, 2)), (send_out, (1, 3))):
+        for i, j in enumerate(order):
+            dest[i, :rows, :] = (keep[j].astype(F32) + got[j].astype(F32)).astype(dest.dtype)
+            dest[i, rows:, :] = (left[...] + right[...]).astype(BF16).astype(dest.dtype)
+
+
+def halve_kernel(exact, meta, keep, got, own, send):
+    mine = keep[0] + got[0].astype(F32)
+    own[:exact, :] = mine[:exact]
+    own[exact:, :] = mine[exact:].astype(BF16).astype(F32)
+    send[...] = (keep[1] + got[1].astype(F32)).astype(BF16)
+
+
+def add_kernel(meta, own, got, out):
+    out[...] = (own[...] + got[...].astype(F32)).astype(BF16)
+
+
+def late_sums_of(meta, keep, got, left, right):
+    _, rows, cols = keep.shape
+    full = rows + left.shape[0]
+    sds = jax.ShapeDtypeStruct
+    kept, send = single(
+        merge_halves_kernel, "merge_late", 1.0, [sds((2, full, cols), F32), sds((2, full, cols), BF16)],
+        meta, [keep, got, left, right],
+    )
+    halves = single(
+        partial(halve_kernel, rows), "halve", 1.0, [sds((full, cols), F32), sds((full, cols), BF16)],
+        meta, [kept, swap(send, "seq", 2)],
+    )
+    return kept, halves
+
+
+def spread_late(meta, halves):
+    own, send = halves
+    (total,) = single(
+        add_kernel, "total_late", 1.0, [jax.ShapeDtypeStruct(own.shape, BF16)], meta,
+        [own, swap(send, "seq", 4)],
+    )
+    return [total] + [swap(total, "rows", j) for j in (1, 2, 3)]
+
+
+def small_kernel(meta, *refs):
     pieces, out = refs[:4], refs[4]
-    take = pl.ds(rows, 32)
-    a, b, c, d = (ref[take, :].astype(F32) for ref in pieces)
-    total = (a + b) + (c + d)
-    out[...] = total[: out.shape[0]]
+    lanes = pieces[0].shape[1] - 128
+    a, b, c, d = (ref[:, lanes:].astype(F32) for ref in pieces)
+    out[...] = ((a + b) + (c + d))[: out.shape[0]]
+
+
+def copy_kernel(meta, *refs):
+    half = len(refs) // 2
+    for source, dest in zip(refs[:half], refs[half:]):
+        dest[...] = source[...]
+
+
+def stack_kernel(meta, *refs):
+    for k, ref in enumerate(refs[:-1]):
+        refs[-1][k] = ref[...]
 
 
 def unpack_kernel(taps_n, fwidth, feats, first_late, meta, small, other, *refs):
     late_pieces, outs, packed, late = refs[:4], refs[4:-2], refs[-2], refs[-1]
-    half = small.shape[0]
-    even = meta[1] == 0
-    packed[:half, :] = jnp.where(even, small[...], other[...])
-    packed[half:, :] = jnp.where(even, other[...], small[...])
+    chips, size = small.shape[:2]
+    core = meta[1]
+    for k in range(chips):
+        z = meta[2] ^ k
+        packed[pl.ds(pl.multiple_of((2 * z + core) * size, 8), size), :] = small[k]
+        packed[pl.ds(pl.multiple_of((2 * z + 1 - core) * size, 8), size), :] = other[k]
     (gain1, shift1, in_bias, short_weight, short_bias, f1, f1b, f2, f2b, f3, f3b, flast, freq,
      fbias, obias, gain2, shift2, ubias, dbias) = outs
     width = gain1.shape[0]
     take = pl.ds(first_late, late_pieces[0].shape[0] - first_late)
     a, b, c, d = (ref[take, :].astype(F32) for ref in late_pieces)
     late[...] = (a + b) + (c + d)
-    part = fwidth // 2
-    flast[:part, :] = packed[:part, :width]
-    flast[part:, :] = packed[:part, width : 2 * width]
-    place = 2 * width
-    for ref in (f3, f2):
-        ref[:part, :] = packed[:part, place : place + fwidth]
-        ref[part:, :] = packed[:part, place + fwidth : place + 2 * fwidth]
-        place += 2 * fwidth
-    for first in range(0, feats, 16):
-        count = min(16, feats - first)
-        lanes = slice(first // 16 * fwidth, first // 16 * fwidth + fwidth)
-        f1[first : first + count, :] = packed[part : part + count, lanes]
+    place = 0
+    for t in range(width // 128):
+        flast[:, t * 128 : (t + 1) * 128] = packed[place : place + fwidth, :]
+        place += fwidth
+    f3[...] = packed[place : place + fwidth, :fwidth]
+    f2[...] = packed[place : place + fwidth, fwidth:]
+    place += fwidth
+    f1[...] = packed[place : place + feats, :fwidth]
     for i, ref in enumerate((f1b, f2b, f3b, freq)):
-        ref[...] = packed[part + 8 + i : part + 9 + i, 2 * fwidth : 3 * fwidth].reshape(-1)
+        ref[...] = packed[place + i : place + i + 1, fwidth:].reshape(-1)
+
+    def line(first, count):
+        return jnp.concatenate(
+            [packed[OTHER_ROWS + first + t : OTHER_ROWS + first + t + 1, :] for t in range(count)], axis=1
+        ).reshape(-1)
+
     for i, ref in enumerate((dbias, gain2, shift2, obias, fbias)):
-        ref[...] = packed[part + i : part + i + 1, 256 : 256 + width].reshape(-1)
-    lanes = ubias.shape[0] // 3
-    ubias[...] = jnp.concatenate(
-        [packed[part + 5 + i : part + 6 + i, 256 : 256 + lanes] for i in range(3)], axis=1
-    ).reshape(-1)
+        ref[...] = line(6 * i, 6)
+    ubias[...] = line(30, ubias.shape[0] // 128)
     side = late.shape[1] // 3
 
     def row(r):
@@ -1056,7 +1109,7 @@
             cols = pl.ds(pl.multiple_of(x * (width // 2) + t * 128, 128), 128)
             out[pl.ds(pl.multiple_of(y * part, 8), part), cols] = tile.astype(F32)
         cols = pl.ds(pl.multiple_of((2 * y + x) * width, 128), width)
-        up[:, cols] = piece[:share, width + 256 :].astype(F32)
+        up[:, cols] = piece[:share, width + 256 : 2 * width + 256].astype(F32)
 
 
 def place_in_kernel(meta, *refs):
@@ -1232,35 +1285,41 @@
         got1, got2 = swap(e1_send, "rows", 1), swap(e2_send, "rows", 2)
         near = near_blocks(glong16, blocks)
         shared_sib = swap(shared, "seq", 1)
-        bundle = collected(
-            meta, [(got1, (left1, 2 * left1 + right1)), (got2, (left2, 2 * left2 + right2))]
-            + [(v, None) for v in near],
-        )
-        got_sib = swap(bundle, "seq", 1)
-        grads, grads_row = near + [got_sib], shared.shape[0]
+        near_all = collected(meta, [(v, None) for v in near])
+        grads, grads_row = near + [swap(near_all, "seq", 1)], 0
+        got_sib = swap(
+            collected(
+                meta, [(got1, (left1, 2 * left1 + right1)), (got2, (left2, 2 * left2 + right2))],
+                [near_all],
+            ), "seq", 1,
+        )
         grad_specs = [whole(v.shape) for v in grads]
-        half_rows, small_cols = (fwidth // 2 + 16) // 2, 2 * width + 4 * fwidth
+        half_rows, small_cols = chips * SMALL_BLOCK, 128
         mine, send = single(
             filter_back_kernel, "filter_back", 5.0, [sds((half_rows, small_cols), F32)] * 2, meta,
             [taps_grad, window, *net, table, filter_first, filter_second, filter_third, filter_last,
              sine_freq, smalls_mlp],
-            after=[bundle], scratch=[pltpu.VMEM((2 * half_rows, small_cols), F32)],
+            after=[near_all], scratch=[pltpu.VMEM((2 * half_rows, small_cols), F32)],
         )
     else:
         grads, grads_row = [lax.all_gather(glong16, "seq", axis=0, tiled=False)], 0
         grad_specs = part_specs
         filter_grads = taps_pull(taps_grad.reshape(length, width))
 
+    tied = ()
     third = lambda n: pl.BlockSpec((block, chunk), lambda i: (0, n * steps + i))
     tap_third = lambda n: pl.BlockSpec((taps_n, chunk), lambda i: (0, n * steps + i))
     for_in, for_values, rim_out = pl.pallas_call(
-        partial(conv_back_kernel, ndocs, length, nparts, grads_row),
+        lambda *refs: conv_back_kernel(
+            ndocs, length, nparts, grads_row, *refs[: nparts + 12], *refs[nparts + 12 + len(tied) :]
+        ),
         grid=(steps,),
         out_shape=(sds((block, width), F32), sds((block, width), F32), sds((3, 8, width), F32)),
         in_specs=[smem()] + grad_specs + [
             by_chunk((block,)), by_chunk((blocks, 2 * block)), whole(tables["invt2"].shape),
             whole(tables["leftt3"].shape), vec if steps == 1 else by_chunk((1,)), third(1), third(2),
-            by_chunk((block,)), tap_third(0), tap_third(1), tap_third(2)],
+            by_chunk((block,)), tap_third(0), tap_third(1), tap_third(2)]
+        + [pl.BlockSpec(memory_space=pl.ANY)] * len(tied),
         out_specs=(by_chunk((block,)), by_chunk((block,)), by_chunk((3, 8))),
         scratch_shapes=[spec_scratch] + held,
         compiler_params=params(),
@@ -1268,9 +1327,8 @@
         name="conv_back",
     )(meta, *grads, glong, lags, tables["invt2"], tables["leftt3"],
       filter_bias if steps == 1 else filter_bias.reshape(1, -1),
-      mixed, mixed, ggate, short_weight, short_weight, short_weight)
+      mixed, mixed, ggate, short_weight, short_weight, short_weight, *tied)
     rim_back = shift(rim_out, "seq", -1)
-    tied = ()
     if packed:
         def partials(kernel, name, piece, arrays, after=()):
             return single(
@@ -1282,12 +1340,14 @@
             down_out_kernel, "down_out", (share, width + 256),
             (own, shared, shared_sib, got1, got_sib, early, early_got, early_sib), [rim_out],
         )
-        small = mine + swap(send, "seq", 1)
-        small = small + swap(small, "seq", 2)
-        small = small + swap(small, "seq", 4)
         tied = (parts1[0], parts2[0])
-
-
+        keep1, send1 = parts1
+        keep2, send2 = parts2
+        pairs = [keep1, swap(send1, "rows", 2), keep2, swap(send2, "rows", 1)]
+        first_sums = chip_sums(meta, pairs, "tiles", (mine, swap(send, "seq", 1)))
+
+
+    tied = tied if packed else ()
     gproj, smalls_short, *late = single(
         partial(short_back_kernel, ndocs, packed), "short_back", 3.0,
         [sds((block, 3 * width), BF16), sds((24, width), F32)]
@@ -1304,25 +1364,22 @@
         def placed(kernel, name, shapes, pieces):
             return single(kernel, name, 1.5, [sds(v, F32) for v in shapes], meta, pieces)
 
-        keep1, send1 = parts1
-        keep2, send2 = parts2
-        pieces = spread_out(
-            meta, [keep1, swap(send1, "rows", 2), keep2, swap(send2, "rows", 1)], (), (small,)
-        )
         late, late_send = late
         late_got = swap(late_send, "rows", 1)
         late_sib = swap(
             collected(
-                meta, [(late, (0, late.shape[0])), (late_got, (0, late.shape[0]))], [small]
+                meta, [(late, (0, late.shape[0])), (late_got, (0, late.shape[0]))]
             ), "seq", 1
         )
         keep3, send3 = partials(
             in_kernel, "in_grad", (share // 2, 3 * width // 2),
-            (late, late_got, late_sib, early, early_got, early_sib),
-        )
-        pieces3 = spread_out(
-            meta, [keep3, swap(send3, "rows", 2)], (smalls_late, swap(smalls_late, "seq", 1))
-        )
+            (late, late_got, late_sib, early, early_got, early_sib), first_sums[:1],
+        )
+        kept3, halves3 = late_sums_of(
+            meta, keep3, swap(send3, "rows", 2), smalls_late, swap(smalls_late, "seq", 1)
+        )
+        pieces = spread_out(meta, first_sums, [kept3])
+        pieces3 = spread_late(meta, halves3)
         grad_down, grad_out, grad_up = placed(
             place_early_kernel, "place_early",
             ((hidden // blocks, width), (share, width), (share, hidden)), pieces,
@@ -1330,7 +1387,11 @@
         (grad_in,) = placed(place_in_kernel, "place_in", ((share, 3 * width),), pieces3)
 
         (small,) = single(
-            partial(small_kernel, share), "small", 0.5, [sds((half_rows, small_cols), F32)], meta, pieces
+            small_kernel, "small", 0.5, [sds((SMALL_BLOCK, 128), F32)], meta, pieces
+        )
+        near = [small] + [swap(small, "seq", 2 * k) for k in (1, 2, 3)]
+        (small,) = single(
+            stack_kernel, "stack", 0.5, [sds((chips, SMALL_BLOCK, 128), F32)], meta, near, [grad_up]
         )
         other = swap(small, "seq", 1)
         shapes = [

time: 186 us -> 183 us (0.984)
  waiting for transfers between devices: 69.9 us -> 62.3 us
  local copies, waits for them, and re-layouts: 5.36 us -> 7.53 us
    ppermute x34 -> x35, waiting for transfers between devices: 69.9 us -> 62.3 us  [swap(): lax.ppermute(block, axis, [(i, i ^ mask) for i in range(lax.axis_size(axi...]
    unnamed x78 -> x88, local copies, waits for them, and re-layouts: 3.36 us -> 5.53 us
    ppermute x34 -> x35, starting transfers between devices: 48.4 us -> 49.8 us  [swap(): lax.ppermute(block, axis, [(i, i ^ mask) for i in range(lax.axis_size(axi...]
    pallas_call x19 -> x22, Pallas kernels: 35.8 us -> 37.2 us  [single(): pl.pallas_call(body, grid=(1,), out_shape=tuple(outs), in_specs=[smem()]...]
  transfers between devices with their start and end apart: 36 -> 37, of which waited for: 12 -> 16; matrix products, arithmetic and copies ran while one was open for 1% -> 1% of each run, Pallas kernels for 19% -> 19%
where the time goes in v4:
time: 183 us
  waiting for transfers between devices  62.3 us (34%)
  Pallas kernels  58.2 us (32%)
  starting transfers between devices  53.5 us (29%)
  local copies, waits for them, and re-layouts  7.53 us (4%)
    ppermute x35, waiting for transfers between devices, swap(): lax.ppermute(block, axis, [(i, i ^ mask) for i in range(lax.axis_size(axi...  62.3 us
    ppermute x35, starting transfers between devices, swap(): lax.ppermute(block, axis, [(i, i ^ mask) for i in range(lax.axis_size(axi...  49.8 us
    pallas_call x22, Pallas kernels, single(): pl.pallas_call(body, grid=(1,), out_shape=tuple(outs), in_specs=[smem()]...  37.2 us
    pallas_call x1, Pallas kernels, local(): pl.pallas_call(partial(mlp_kernel, packed), grid=(fsteps,), out_shape=(sd...  9.89 us
    unnamed x88, local copies, waits for them, and re-layouts  5.53 us
    pallas_call x1, Pallas kernels, local(): pl.pallas_call(lambda *refs: conv_back_kernel(ndocs, length, nparts, grad...  5.4 us
  transfers between devices with their start and end apart: 37, of which 16 were waited for; matrix products, arithmetic and copies ran while one was open for 1% of the time, Pallas kernels for 19%

profile of v4, /device:TPU:0, one launch (start us, length us, event | category | flops | bytes accessed | tf_op | source)
XLA Modules:
  0.0 183.2 jit_solution(9172584545317599036)
XLA Ops:
  1.4 2.3 %collective-permute-start = (bf16[16,768]{1,0:T(8,128)(2,1)S(1)}, bf16[16,768]{1,0:T(8,128)(2,1)S(1)}, u32[]{:S(2)}, u32[]{:S(2)}) collective-permute-start(bf16[16,768]{1,0:T(8,128)(2,1)S(1)} %slice_bitcast_fusion), channel_id=1, source_target_pairs={{0,1},{1,2},{2,3},{3,4},{4,5},{5,6},{6,7},{8,9},{9,10},{10,11},{11... | collective-permute-start | bytes 73736 | tf_op jit(solution)/shard_map/ppermute | solution.py:789
  5.7 5.1 %front.1 = (f32[144,2304]{1,0:T(8,128)}, bf16[1536,128]{1,0:T(8,128)(2,1)}, f32[128,2304]{1,0:T(8,128)}, bf16[128,768]{1,0:T(8,128)(2,1)}) custom-call(s32[9]{0:T(128)} %concatenate.3.meta.refs_0_, bf16[128,768]{1,0:T(8,128)(2,1)} %bitcast.11, bf16[16,768]{1,0:T(8,128)(2,1)} %copy-done.39, bf16[128,768]{1,0:T(8,128)(2,1)} %bitcast.18, ...), custom_call_target="tpu_custom_call" | custom-call | flops 3300000000 | tf_op jit(solution)/shard_map/front/pallas_call | solution.py:58
  10.8 6.6 %collective-permute-start.3 = (bf16[128,768]{1,0:T(8,128)(2,1)}, bf16[128,768]{1,0:T(8,128)(2,1)S(1)}, u32[]{:S(2)}, u32[]{:S(2)}) collective-permute-start(bf16[128,768]{1,0:T(8,128)(2,1)} %get-tuple-element.91.refs_10_.refs_2_.refs_0_.carried), channel_id=1, source_target_pairs={{0,6},{1,7},{2,4},{3,5},{4,2},{5,3},{6,0},{7,1},{8,14},{9,15},{10,... | collective-permute-start | bytes 589832 | tf_op jit(solution)/shard_map/ppermute | solution.py:793
  20.5 5.4 %filter.1 = (f32[8,256,768]{2,1,0:T(8,128)S(1)}, f32[1024,768]{1,0:T(8,128)S(1)}, f32[192,1024]{1,0:T(8,128)S(1)}, f32[192,1024]{1,0:T(8,128)S(1)}, f32[192,1024]{1,0:T(8,128)S(1)}) custom-call(s32[9]{0:T(128)S(1)} %copy-done.3, f32[40,1024]{1,0:T(8,128)S(1)} %copy-done.28, bf16[33,64]{1,0:T(8,128)(2,1)S(1)} %copy-done.12, bf16[64]{0:T(256)(128)(2,1)S(1)} %copy-done.20, ...), custom_call_target="tpu_custom_call" | custom-call | flops 8800000000 | tf_op jit(solution)/shard_map/filter/pallas_call | solution.py:58
  25.9 1.6 copy-done.32
  28.4 5.8 %collective-permute-done.2.refs_4_.refs_2_ = bf16[128,768]{1,0:T(8,128)(2,1)S(1)} collective-permute-done((bf16[128,768]{1,0:T(8,128)(2,1)}, bf16[128,768]{1,0:T(8,128)(2,1)S(1)}, u32[]{:S(2)}, u32[]{:S(2)}) %collective-permute-start.2) | collective-permute-done | bytes 196640 | tf_op jit(solution)/shard_map/ppermute | solution.py:793
  35.2 3.1 %collective-permute-done.5.refs_4_.refs_7_.refs_5_ = bf16[5376,128]{1,0:T(8,128)(2,1)S(1)} collective-permute-done((bf16[5376,128]{1,0:T(8,128)(2,1)S(1)}, bf16[5376,128]{1,0:T(8,128)(2,1)S(1)}, u32[]{:S(2)}, u32[]{:S(2)}) %collective-permute-start.5) | collective-permute-done | bytes 1376288 | tf_op jit(solution)/shard_map/ppermute | solution.py:793
  38.3 2.9 %conv.1 = f32[128,768]{1,0:T(8,128)S(1)} custom-call(s32[9]{0:T(128)S(1)} %copy-done.3, bf16[128,768]{1,0:T(8,128)(2,1)S(1)} %copy-done.1, bf16[128,768]{1,0:T(8,128)(2,1)S(1)} %collective-permute-done.1.refs_3_.refs_1_, bf16[128,768]{1,0:T(8,128)(2,1)S(1)} %collective-permute-done.2.refs_4_.refs_2_, ...), custom_call_target="tpu_custom_call" | custom-call | flops 3300000000 | tf_op jit(solution)/shard_map/conv/pallas_call | solution.py:1216
  41.4 9.9 %mlp.1 = (bf16[128,768]{1,0:T(8,128)(2,1)}, f32[128,768]{1,0:T(8,128)S(1)}, f32[128,768]{1,0:T(8,128)S(1)}, bf16[128,768]{1,0:T(8,128)(2,1)S(1)}, f32[128,768]{1...) custom-call(s32[9]{0:T(128)S(1)} %copy-done.3, ...), custom_call_target="tpu_custom_call" | custom-call | flops 11000000512 | tf_op jit(solution)/shard_map/mlp/pallas_call | solution.py:1243
  54.3 3.0 %collective-permute-start.8 = (bf16[128,768]{1,0:T(8,128)(2,1)S(1)}, bf16[128,768]{1,0:T(8,128)(2,1)S(1)}, u32[]{:S(2)}, u32[]{:S(2)}) collective-permute-start(bf16[128,768]{1,0:T(8,128)(2,1)S(1)} %get-tuple-element.97.refs_0_.refs_1_), channel_id=1, source_target_pairs={{0,6},{1,7},{2,4},{3,5},{4,2},{5,3},{6,0},{7,1},{8,14},{9,15},{10,... | collective-permute-start | bytes 589832 | tf_op jit(solution)/shard_map/ppermute | solution.py:793
  58.7 5.3 %collective-permute-done.8.refs_3_.refs_4_ = bf16[128,768]{1,0:T(8,128)(2,1)S(1)} collective-permute-done((bf16[128,768]{1,0:T(8,128)(2,1)S(1)}, bf16[128,768]{1,0:T(8,128)(2,1)S(1)}, u32[]{:S(2)}, u32[]{:S(2)}) %collective-permute-start.8) | collective-permute-done | bytes 196640 | tf_op jit(solution)/shard_map/ppermute | solution.py:793
  64.1 8.1 %collective-permute-done.7.refs_2_.refs_3_ = bf16[128,768]{1,0:T(8,128)(2,1)S(1)} collective-permute-done((bf16[128,768]{1,0:T(8,128)(2,1)S(1)}, bf16[128,768]{1,0:T(8,128)(2,1)S(1)}, u32[]{:S(2)}, u32[]{:S(2)}) %collective-permute-start.7) | collective-permute-done | bytes 196640 | tf_op jit(solution)/shard_map/ppermute | solution.py:793
  75.2 5.4 %conv_back.1 = (f32[128,768]{1,0:T(8,128)S(1)}, f32[128,768]{1,0:T(8,128)S(1)}, f32[3,8,768]{2,1,0:T(8,128)S(1)}) custom-call(s32[9]{0:T(128)S(1)} %copy-done.3, bf16[128,768]{1,0:T(8,128)(2,1)S(1)} %get-tuple-element.97.refs_0_.refs_1_, bf16[128,768]{1,0:T(8,128)(2,1)S(1)} %collective-permute-done.6.refs_1_.refs_2_, ...), custom_call_target="tpu_custom_call" | custom-call | flops 4400000000 | tf_op jit(solution)/shard_map/conv_back/pallas_call | solution.py:1312
  82.0 1.8 up_grad.1
  83.8 1.7 down_out.1
  85.5 2.7 %short_back.1 = (bf16[128,2304]{1,0:T(8,128)(2,1)S(1)}, f32[24,768]{1,0:T(8,128)S(1)}, bf16[1152,128]{1,0:T(8,128)(2,1)S(1)}, bf16[1152,128]{1,0:T(8,128)(2,1)S(1)}) custom-call(s32[9]{0:T(128)S(1)} %copy-done.3, f32[128,768]{1,0:T(8,128)S(1)} %get-tuple-element.96.refs_13_.refs_0_, f32[128,768]{1,0:T(8,128)S(1)} %get-tuple-element.99.refs_1_, ...), custom_call_target="tpu_custom_call" | custom-call | flops 3300000000 | tf_op jit(solution)/shard_map/short_back/pallas_call | solution.py:58
  89.3 2.8 %taps_grad.1.refs_0_ = f32[8,128,768]{2,1,0:T(8,128)S(1)} custom-call(s32[9]{0:T(128)S(1)} %copy-done.3, bf16[128,768]{1,0:T(8,128)(2,1)S(1)} %copy-done.2, bf16[128,768]{1,0:T(8,128)(2,1)S(1)} %collective-permute-done.1.refs_3_.refs_1_, bf16[128,768]{1,0:T(8,128)(2,1)S(1)} %collective-permute-done.2.refs_4_.refs_2_, ...), custom_call_target="tpu_custom_call" | custom-call | flops 4400000000 | tf_op jit(solution)/shard_map/taps_grad/pallas_call | solution.py:1270
  93.7 4.3 %collective-permute-done.21.refs_1_ = bf16[1152,128]{1,0:T(8,128)(2,1)S(1)} collective-permute-done((bf16[1152,128]{1,0:T(8,128)(2,1)S(1)}, bf16[1152,128]{1,0:T(8,128)(2,1)S(1)}, u32[]{:S(2)}, u32[]{:S(2)}) %collective-permute-start.21) | collective-permute-done | bytes 294944 | tf_op jit(solution)/shard_map/ppermute | solution.py:793
  99.1 4.4 %filter_back.1 = (f32[320,128]{1,0:T(8,128)S(1)}, f32[320,128]{1,0:T(8,128)S(1)}) custom-call(s32[9]{0:T(128)S(1)} %copy-done.3, f32[8,128,768]{2,1,0:T(8,128)S(1)} %taps_grad.1.refs_0_, f32[1024,768]{1,0:T(8,128)S(1)} %copy-done.33, f32[192,1024]{1,0:T(8,128)S(1)} %get-tuple-element.116.refs_2_, f32[192,1024]{1,0:T(8,128)S(1)} %copy-done.36, ...), custom_call_target="tpu_custom_call" | custom-call | flops 5500000256 | tf_op jit(solution)/shard_map/filter_back/pallas_call | solution.py:58
  104.9 5.7 %collective-permute-done.16.refs_3_ = bf16[4,96,768]{2,1,0:T(8,128)(2,1)S(1)} collective-permute-done((bf16[4,96,768]{2,1,0:T(8,128)(2,1)S(1)}, bf16[4,96,768]{2,1,0:T(8,128)(2,1)S(1)}, u32[]{:S(2)}, u32[]{:S(2)}) %collective-permute-start.16) | collective-permute-done | bytes 589856 | tf_op jit(solution)/shard_map/ppermute | solution.py:793
  113.4 1.9 %collective-permute-start.19 = (bf16[96,1920]{1,0:T(8,128)(2,1)S(1)}, bf16[96,1920]{1,0:T(8,128)(2,1)S(1)}, u32[]{:S(2)}, u32[]{:S(2)}) collective-permute-start(bf16[96,1920]{1,0:T(8,128)(2,1)S(1)} %get-tuple-element.124), channel_id=1, source_target_pairs={{0,4},{1,5},{2,6},{3,7},{4,0},{5,1},{6,2},{7,3},{8,12},{9,13},{10,... | collective-permute-start | bytes 1105928 | tf_op jit(solution)/shard_map/ppermute | solution.py:793
  115.3 2.5 %collective-permute-start.20 = (bf16[96,1920]{1,0:T(8,128)(2,1)S(1)}, bf16[96,1920]{1,0:T(8,128)(2,1)S(1)}, u32[]{:S(2)}, u32[]{:S(2)}) collective-permute-start(bf16[96,1920]{1,0:T(8,128)(2,1)S(1)} %get-tuple-element.125), channel_id=1, source_target_pairs={{0,6},{1,7},{2,4},{3,5},{4,2},{5,3},{6,0},{7,1},{8,14},{9,15},{10,... | collective-permute-start | bytes 1105928 | tf_op jit(solution)/shard_map/ppermute | solution.py:793
  117.8 2.7 %tail.1 = (f32[128,768]{1,0:T(8,128)}, f32[16,1152]{1,0:T(8,128)S(1)}) custom-call(s32[9]{0:T(128)S(1)} %copy-done.3, bf16[128,2304]{1,0:T(8,128)(2,1)S(1)} %get-tuple-element.109.refs_0_, bf16[768,2304]{1,0:T(8,128)(2,1)S(1)} %copy-done.5, bf16[128,768]{1,0:T(8,128)(2,1)S(1)} %bitcast.13, bf16[768]{0:T(1024)(128)(2,1)S(1)} %copy-done.19, ...), custom_call_target="tpu_custom_call" | custom-call | flops 2750000128 | tf_op jit(solution)/shard_map/tail/pallas_call | solution.py:58
  121.8 3.3 %collective-permute-done.23.refs_1_ = bf16[4,48,1152]{2,1,0:T(8,128)(2,1)S(1)} collective-permute-done((bf16[4,48,1152]{2,1,0:T(8,128)(2,1)S(1)}, bf16[4,48,1152]{2,1,0:T(8,128)(2,1)S(1)}, u32[]{:S(2)}, u32[]{:S(2)}) %collective-permute-start.23) | collective-permute-done | bytes 442400 | tf_op jit(solution)/shard_map/ppermute | solution.py:793
  125.8 6.4 %collective-permute-done.18.refs_1_ = bf16[96,1920]{1,0:T(8,128)(2,1)S(1)} collective-permute-done((bf16[96,1920]{1,0:T(8,128)(2,1)S(1)}, bf16[96,1920]{1,0:T(8,128)(2,1)S(1)}, u32[]{:S(2)}, u32[]{:S(2)}) %collective-permute-start.18) | collective-permute-done | bytes 368672 | tf_op jit(solution)/shard_map/ppermute | solution.py:793
  132.2 9.5 %collective-permute-done.19.refs_2_ = bf16[96,1920]{1,0:T(8,128)(2,1)S(1)} collective-permute-done((bf16[96,1920]{1,0:T(8,128)(2,1)S(1)}, bf16[96,1920]{1,0:T(8,128)(2,1)S(1)}, u32[]{:S(2)}, u32[]{:S(2)}) %collective-permute-start.19) | collective-permute-done | bytes 368672 | tf_op jit(solution)/shard_map/ppermute | solution.py:793
  142.4 1.6 collective-permute-start.27
  146.5 7.4 %collective-permute-start.33 = (bf16[64,1152]{1,0:T(8,128)(2,1)S(1)}, bf16[64,1152]{1,0:T(8,128)(2,1)S(1)}, u32[]{:S(2)}, u32[]{:S(2)}) collective-permute-start(bf16[64,1152]{1,0:T(8,128)(2,1)S(1)} %get-tuple-element.135), channel_id=1, source_target_pairs={{0,4},{1,5},{2,6},{3,7},{4,0},{5,1},{6,2},{7,3},{8,12},{9,13},{10,... | collective-permute-start | bytes 442376 | tf_op jit(solution)/shard_map/ppermute | solution.py:793
  154.9 4.2 %collective-permute-done.26.refs_2_ = bf16[96,1920]{1,0:T(8,128)(2,1)S(1)} collective-permute-done((bf16[96,1920]{1,0:T(8,128)(2,1)S(1)}, bf16[96,1920]{1,0:T(8,128)(2,1)S(1)}, u32[]{:S(2)}, u32[]{:S(2)}) %collective-permute-start.26) | collective-permute-done | bytes 368672 | tf_op jit(solution)/shard_map/ppermute | solution.py:793
  161.8 8.5 %collective-permute-start.29 = (f32[80,128]{1,0:T(8,128)S(1)}, f32[80,128]{1,0:T(8,128)S(1)}, u32[]{:S(2)}, u32[]{:S(2)}) collective-permute-start(f32[80,128]{1,0:T(8,128)S(1)} %small.1.refs_0_), channel_id=1, source_target_pairs={{0,4},{1,5},{2,6},{3,7},{4,0},{5,1},{6,2},{7,3},{8,12},{9,13},{10,... | collective-permute-start | bytes 122888 | tf_op jit(solution)/shard_map/ppermute | solution.py:793
  174.4 2.2 %place_early.1 = (f32[384,768]{1,0:T(8,128)}, f32[96,768]{1,0:T(8,128)}, f32[96,3072]{1,0:T(8,128)}) custom-call(s32[9]{0:T(128)S(1)} %copy-done.3, bf16[96,1920]{1,0:T(8,128)(2,1)S(1)} %total.1.refs_0_, bf16[96,1920]{1,0:T(8,128)(2,1)S(1)} %collective-permute-done.25.refs_1_, bf16[96,1920]{1,0:T(8,128)(2,1)S(1)} %collective-permute-done.26.refs_2_, ...), custom_call_target="tpu_custom_call" | custom-call | flops 1650000000 | tf_op jit(solution)/shard_map/place_early/pallas_call | solution.py:58
  178.5 1.6 collective-permute-done.35.refs_4_.refs_2_
  (160 shorter events, 42.0 us)
Async XLA Ops:
  1.4 3.6 %collective-permute-start = (bf16[16,768]{1,0:T(8,128)(2,1)S(1)}, bf16[16,768]{1,0:T(8,128)(2,1)S(1)}, u32[]{:S(2)}, u32[]{:S(2)}) collective-permute-start(bf16[16,768]{1,0:T(8,128)(2,1)S(1)} %slice_bitcast_fusion), channel_id=1, source_target_pairs={{0,1},{1,2},{2,3},{3,4},{4,5},{5,6},{6,7},{8,9},{9,10},{10,11},{11... | collective-permute-start | bytes 73736 | tf_op jit(solution)/shard_map/ppermute | solution.py:789
  10.8 17.6 %collective-permute-start.3 = (bf16[128,768]{1,0:T(8,128)(2,1)}, bf16[128,768]{1,0:T(8,128)(2,1)S(1)}, u32[]{:S(2)}, u32[]{:S(2)}) collective-permute-start(bf16[128,768]{1,0:T(8,128)(2,1)} %get-tuple-element.91.refs_10_.refs_2_.refs_0_.carried), channel_id=1, source_target_pairs={{0,6},{1,7},{2,4},{3,5},{4,2},{5,3},{6,0},{7,1},{8,14},{9,15},{10,... | collective-permute-start | bytes 589832 | tf_op jit(solution)/shard_map/ppermute | solution.py:793
  17.4 16.8 %collective-permute-start.2 = (bf16[128,768]{1,0:T(8,128)(2,1)}, bf16[128,768]{1,0:T(8,128)(2,1)S(1)}, u32[]{:S(2)}, u32[]{:S(2)}) collective-permute-start(bf16[128,768]{1,0:T(8,128)(2,1)} %get-tuple-element.91.refs_10_.refs_2_.refs_0_.carried), channel_id=1, source_target_pairs={{0,4},{1,5},{2,6},{3,7},{4,0},{5,1},{6,2},{7,3},{8,12},{9,13},{10,... | collective-permute-start | bytes 589832 | tf_op jit(solution)/shard_map/ppermute | solution.py:793
  17.4 16.8 %collective-permute-start.1 = (bf16[128,768]{1,0:T(8,128)(2,1)}, bf16[128,768]{1,0:T(8,128)(2,1)S(1)}, u32[]{:S(2)}, u32[]{:S(2)}) collective-permute-start(bf16[128,768]{1,0:T(8,128)(2,1)} %get-tuple-element.91.refs_10_.refs_2_.refs_0_.carried), channel_id=1, source_target_pairs={{0,2},{1,3},{2,0},{3,1},{4,6},{5,7},{6,4},{7,5},{8,10},{9,11},{10,... | collective-permute-start | bytes 589832 | tf_op jit(solution)/shard_map/ppermute | solution.py:793
  18.0 16.2 %collective-permute-start.4 = (bf16[1536,128]{1,0:T(8,128)(2,1)}, bf16[1536,128]{1,0:T(8,128)(2,1)S(1)}, u32[]{:S(2)}, u32[]{:S(2)}) collective-permute-start(bf16[1536,128]{1,0:T(8,128)(2,1)} %get-tuple-element.92.refs_0_.refs_5_.refs_3_), channel_id=1, source_target_pairs={{0,8},{8,0},{16,24},{24,16},{1,9},{9,1},{17,25},{25,17},{2,10},{10... | collective-permute-start | bytes 1179656 | tf_op jit(solution)/shard_map/ppermute | solution.py:793
  51.3 22.1 %collective-permute-start.12 = (bf16[2688,128]{1,0:T(8,128)(2,1)S(1)}, bf16[2688,128]{1,0:T(8,128)(2,1)S(1)}, u32[]{:S(2)}, u32[]{:S(2)}) collective-permute-start(bf16[2688,128]{1,0:T(8,128)(2,1)S(1)} %get-tuple-element.105), channel_id=1, source_target_pairs={{0,8},{8,0},{16,24},{24,16},{1,9},{9,1},{17,25},{25,17},{2,10},{10... | collective-permute-start | bytes 2064392 | tf_op jit(solution)/shard_map/ppermute | solution.py:793
  52.8 20.6 %collective-permute-start.13 = (bf16[2304,128]{1,0:T(8,128)(2,1)S(1)}, bf16[2304,128]{1,0:T(8,128)(2,1)S(1)}, u32[]{:S(2)}, u32[]{:S(2)}) collective-permute-start(bf16[2304,128]{1,0:T(8,128)(2,1)S(1)} %get-tuple-element.106), channel_id=1, source_target_pairs={{0,16},{8,24},{16,0},{24,8},{1,17},{9,25},{17,1},{25,9},{2,18},{10... | collective-permute-start | bytes 1769480 | tf_op jit(solution)/shard_map/ppermute | solution.py:793
  54.3 9.7 %collective-permute-start.8 = (bf16[128,768]{1,0:T(8,128)(2,1)S(1)}, bf16[128,768]{1,0:T(8,128)(2,1)S(1)}, u32[]{:S(2)}, u32[]{:S(2)}) collective-permute-start(bf16[128,768]{1,0:T(8,128)(2,1)S(1)} %get-tuple-element.97.refs_0_.refs_1_), channel_id=1, source_target_pairs={{0,6},{1,7},{2,4},{3,5},{4,2},{5,3},{6,0},{7,1},{8,14},{9,15},{10,... | collective-permute-start | bytes 589832 | tf_op jit(solution)/shard_map/ppermute | solution.py:793
  57.4 14.8 %collective-permute-start.7 = (bf16[128,768]{1,0:T(8,128)(2,1)S(1)}, bf16[128,768]{1,0:T(8,128)(2,1)S(1)}, u32[]{:S(2)}, u32[]{:S(2)}) collective-permute-start(bf16[128,768]{1,0:T(8,128)(2,1)S(1)} %get-tuple-element.97.refs_0_.refs_1_), channel_id=1, source_target_pairs={{0,4},{1,5},{2,6},{3,7},{4,0},{5,1},{6,2},{7,3},{8,12},{9,13},{10,... | collective-permute-start | bytes 589832 | tf_op jit(solution)/shard_map/ppermute | solution.py:793
  57.4 14.8 %collective-permute-start.6 = (bf16[128,768]{1,0:T(8,128)(2,1)S(1)}, bf16[128,768]{1,0:T(8,128)(2,1)S(1)}, u32[]{:S(2)}, u32[]{:S(2)}) collective-permute-start(bf16[128,768]{1,0:T(8,128)(2,1)S(1)} %get-tuple-element.97.refs_0_.refs_1_), channel_id=1, source_target_pairs={{0,2},{1,3},{2,0},{3,1},{4,6},{5,7},{6,4},{7,5},{8,10},{9,11},{10,... | collective-permute-start | bytes 589832 | tf_op jit(solution)/shard_map/ppermute | solution.py:793
  73.1 8.9 %collective-permute-start.11 = (bf16[3456,128]{1,0:T(8,128)(2,1)S(1)}, bf16[3456,128]{1,0:T(8,128)(2,1)S(1)}, u32[]{:S(2)}, u32[]{:S(2)}) collective-permute-start(bf16[3456,128]{1,0:T(8,128)(2,1)S(1)} %get-tuple-element.104.refs_1_), channel_id=1, source_target_pairs={{0,1},{1,0},{2,3},{3,2},{4,5},{5,4},{6,7},{7,6},{8,9},{9,8},{10,11... | collective-permute-start | bytes 2654216 | tf_op jit(solution)/shard_map/ppermute | solution.py:793
  74.1 7.9 %collective-permute-start.14 = (bf16[3456,128]{1,0:T(8,128)(2,1)S(1)}, bf16[3456,128]{1,0:T(8,128)(2,1)S(1)}, u32[]{:S(2)}, u32[]{:S(2)}) collective-permute-start(bf16[3456,128]{1,0:T(8,128)(2,1)S(1)} %collect.6), channel_id=1, source_target_pairs={{0,1},{1,0},{2,3},{3,2},{4,5},{5,4},{6,7},{7,6},{8,9},{9,8},{10,11... | collective-permute-start | bytes 2654216 | tf_op jit(solution)/shard_map/ppermute | solution.py:793
  80.7 4.8 %collective-permute-start.10 = (f32[3,8,768]{2,1,0:T(8,128)S(1)}, f32[3,8,768]{2,1,0:T(8,128)S(1)}, u32[]{:S(2)}, u32[]{:S(2)}) collective-permute-start(f32[3,8,768]{2,1,0:T(8,128)S(1)} %get-tuple-element.101.refs_8_.refs_5_), channel_id=1, source_target_pairs={{1,0},{2,1},{3,2},{4,3},{5,4},{6,5},{7,6},{9,8},{10,9},{11,10},{12... | collective-permute-start | bytes 221192 | tf_op jit(solution)/shard_map/ppermute | solution.py:789
  88.2 9.8 %collective-permute-start.21 = (bf16[1152,128]{1,0:T(8,128)(2,1)S(1)}, bf16[1152,128]{1,0:T(8,128)(2,1)S(1)}, u32[]{:S(2)}, u32[]{:S(2)}) collective-permute-start(bf16[1152,128]{1,0:T(8,128)(2,1)S(1)} %get-tuple-element.127), channel_id=1, source_target_pairs={{0,8},{8,0},{16,24},{24,16},{1,9},{9,1},{17,25},{25,17},{2,10},{10... | collective-permute-start | bytes 884744 | tf_op jit(solution)/shard_map/ppermute | solution.py:793
  88.8 21.8 %collective-permute-start.15 = (bf16[4,96,1024]{2,1,0:T(8,128)(2,1)S(1)}, bf16[4,96,1024]{2,1,0:T(8,128)(2,1)S(1)}, u32[]{:S(2)}, u32[]{:S(2)}) collective-permute-start(bf16[4,96,1024]{2,1,0:T(8,128)(2,1)S(1)} %get-tuple-element.113), channel_id=1, source_target_pairs={{0,16},{8,24},{16,0},{24,8},{1,17},{9,25},{17,1},{25,9},{2,18},{10... | collective-permute-start | bytes 2359304 | tf_op jit(solution)/shard_map/ppermute | solution.py:793
  92.1 18.5 %collective-permute-start.16 = (bf16[4,96,768]{2,1,0:T(8,128)(2,1)S(1)}, bf16[4,96,768]{2,1,0:T(8,128)(2,1)S(1)}, u32[]{:S(2)}, u32[]{:S(2)}) collective-permute-start(bf16[4,96,768]{2,1,0:T(8,128)(2,1)S(1)} %get-tuple-element.114), channel_id=1, source_target_pairs={{0,8},{8,0},{16,24},{24,16},{1,9},{9,1},{17,25},{25,17},{2,10},{10... | collective-permute-start | bytes 1769480 | tf_op jit(solution)/shard_map/ppermute | solution.py:793
  98.6 12.9 %collective-permute-start.22 = (bf16[2304,128]{1,0:T(8,128)(2,1)S(1)}, bf16[2304,128]{1,0:T(8,128)(2,1)S(1)}, u32[]{:S(2)}, u32[]{:S(2)}) collective-permute-start(bf16[2304,128]{1,0:T(8,128)(2,1)S(1)} %collect.7), channel_id=1, source_target_pairs={{0,1},{1,0},{2,3},{3,2},{4,5},{5,4},{6,7},{7,6},{8,9},{9,8},{10,11... | collective-permute-start | bytes 1769480 | tf_op jit(solution)/shard_map/ppermute | solution.py:793
  112.8 12.3 %collective-permute-start.23 = (bf16[4,48,1152]{2,1,0:T(8,128)(2,1)S(1)}, bf16[4,48,1152]{2,1,0:T(8,128)(2,1)S(1)}, u32[]{:S(2)}, u32[]{:S(2)}) collective-permute-start(bf16[4,48,1152]{2,1,0:T(8,128)(2,1)S(1)} %get-tuple-element.129), channel_id=1, source_target_pairs={{0,16},{8,24},{16,0},{24,8},{1,17},{9,25},{17,1},{25,9},{2,18},{10... | collective-permute-start | bytes 1327112 | tf_op jit(solution)/shard_map/ppermute | solution.py:793
  113.4 18.8 %collective-permute-start.18 = (bf16[96,1920]{1,0:T(8,128)(2,1)S(1)}, bf16[96,1920]{1,0:T(8,128)(2,1)S(1)}, u32[]{:S(2)}, u32[]{:S(2)}) collective-permute-start(bf16[96,1920]{1,0:T(8,128)(2,1)S(1)} %get-tuple-element.123), channel_id=1, source_target_pairs={{0,2},{1,3},{2,0},{3,1},{4,6},{5,7},{6,4},{7,5},{8,10},{9,11},{10,... | collective-permute-start | bytes 1105928 | tf_op jit(solution)/shard_map/ppermute | solution.py:793
  113.4 28.2 %collective-permute-start.19 = (bf16[96,1920]{1,0:T(8,128)(2,1)S(1)}, bf16[96,1920]{1,0:T(8,128)(2,1)S(1)}, u32[]{:S(2)}, u32[]{:S(2)}) collective-permute-start(bf16[96,1920]{1,0:T(8,128)(2,1)S(1)} %get-tuple-element.124), channel_id=1, source_target_pairs={{0,4},{1,5},{2,6},{3,7},{4,0},{5,1},{6,2},{7,3},{8,12},{9,13},{10,... | collective-permute-start | bytes 1105928 | tf_op jit(solution)/shard_map/ppermute | solution.py:793
  115.3 26.4 %collective-permute-start.20 = (bf16[96,1920]{1,0:T(8,128)(2,1)S(1)}, bf16[96,1920]{1,0:T(8,128)(2,1)S(1)}, u32[]{:S(2)}, u32[]{:S(2)}) collective-permute-start(bf16[96,1920]{1,0:T(8,128)(2,1)S(1)} %get-tuple-element.125), channel_id=1, source_target_pairs={{0,6},{1,7},{2,4},{3,5},{4,2},{5,3},{6,0},{7,1},{8,14},{9,15},{10,... | collective-permute-start | bytes 1105928 | tf_op jit(solution)/shard_map/ppermute | solution.py:793
  125.7 20.2 %collective-permute-start.32 = (bf16[2,64,1152]{2,1,0:T(8,128)(2,1)S(1)}, bf16[2,64,1152]{2,1,0:T(8,128)(2,1)S(1)}, u32[]{:S(2)}, u32[]{:S(2)}) collective-permute-start(bf16[2,64,1152]{2,1,0:T(8,128)(2,1)S(1)} %get-tuple-element.133), channel_id=1, source_target_pairs={{0,2},{1,3},{2,0},{3,1},{4,6},{5,7},{6,4},{7,5},{8,10},{9,11},{10,... | collective-permute-start | bytes 884744 | tf_op jit(solution)/shard_map/ppermute | solution.py:793
  142.4 12.5 %collective-permute-start.27 = (bf16[96,1920]{1,0:T(8,128)(2,1)S(1)}, bf16[96,1920]{1,0:T(8,128)(2,1)S(1)}, u32[]{:S(2)}, u32[]{:S(2)}) collective-permute-start(bf16[96,1920]{1,0:T(8,128)(2,1)S(1)} %total.1.refs_0_), channel_id=1, source_target_pairs={{0,24},{8,16},{16,8},{24,0},{1,25},{9,17},{17,9},{25,1},{2,26},{10... | collective-permute-start | bytes 1105928 | tf_op jit(solution)/shard_map/ppermute | solution.py:793
  143.9 15.1 %collective-permute-start.26 = (bf16[96,1920]{1,0:T(8,128)(2,1)S(1)}, bf16[96,1920]{1,0:T(8,128)(2,1)S(1)}, u32[]{:S(2)}, u32[]{:S(2)}) collective-permute-start(bf16[96,1920]{1,0:T(8,128)(2,1)S(1)} %total.1.refs_0_), channel_id=1, source_target_pairs={{0,16},{8,24},{16,0},{24,8},{1,17},{9,25},{17,1},{25,9},{2,18},{10... | collective-permute-start | bytes 1105928 | tf_op jit(solution)/shard_map/ppermute | solution.py:793
  144.4 15.3 %collective-permute-start.25 = (bf16[96,1920]{1,0:T(8,128)(2,1)S(1)}, bf16[96,1920]{1,0:T(8,128)(2,1)S(1)}, u32[]{:S(2)}, u32[]{:S(2)}) collective-permute-start(bf16[96,1920]{1,0:T(8,128)(2,1)S(1)} %total.1.refs_0_), channel_id=1, source_target_pairs={{0,8},{8,0},{16,24},{24,16},{1,9},{9,1},{17,25},{25,17},{2,10},{10... | collective-permute-start | bytes 1105928 | tf_op jit(solution)/shard_map/ppermute | solution.py:793
  146.5 23.7 %collective-permute-start.33 = (bf16[64,1152]{1,0:T(8,128)(2,1)S(1)}, bf16[64,1152]{1,0:T(8,128)(2,1)S(1)}, u32[]{:S(2)}, u32[]{:S(2)}) collective-permute-start(bf16[64,1152]{1,0:T(8,128)(2,1)S(1)} %get-tuple-element.135), channel_id=1, source_target_pairs={{0,4},{1,5},{2,6},{3,7},{4,0},{5,1},{6,2},{7,3},{8,12},{9,13},{10,... | collective-permute-start | bytes 442376 | tf_op jit(solution)/shard_map/ppermute | solution.py:793
  160.3 12.7 %collective-permute-start.30 = (f32[80,128]{1,0:T(8,128)S(1)}, f32[80,128]{1,0:T(8,128)S(1)}, u32[]{:S(2)}, u32[]{:S(2)}) collective-permute-start(f32[80,128]{1,0:T(8,128)S(1)} %small.1.refs_0_), channel_id=1, source_target_pairs={{0,6},{1,7},{2,4},{3,5},{4,2},{5,3},{6,0},{7,1},{8,14},{9,15},{10,... | collective-permute-start | bytes 122888 | tf_op jit(solution)/shard_map/ppermute | solution.py:793
  161.8 14.8 %collective-permute-start.29 = (f32[80,128]{1,0:T(8,128)S(1)}, f32[80,128]{1,0:T(8,128)S(1)}, u32[]{:S(2)}, u32[]{:S(2)}) collective-permute-start(f32[80,128]{1,0:T(8,128)S(1)} %small.1.refs_0_), channel_id=1, source_target_pairs={{0,4},{1,5},{2,6},{3,7},{4,0},{5,1},{6,2},{7,3},{8,12},{9,13},{10,... | collective-permute-start | bytes 122888 | tf_op jit(solution)/shard_map/ppermute | solution.py:793
  170.3 6.4 %collective-permute-start.28 = (f32[80,128]{1,0:T(8,128)S(1)}, f32[80,128]{1,0:T(8,128)S(1)}, u32[]{:S(2)}, u32[]{:S(2)}) collective-permute-start(f32[80,128]{1,0:T(8,128)S(1)} %small.1.refs_0_), channel_id=1, source_target_pairs={{0,2},{1,3},{2,0},{3,1},{4,6},{5,7},{6,4},{7,5},{8,10},{9,11},{10,... | collective-permute-start | bytes 122888 | tf_op jit(solution)/shard_map/ppermute | solution.py:793
  170.9 7.7 %collective-permute-start.36 = (bf16[64,1152]{1,0:T(8,128)(2,1)S(1)}, bf16[64,1152]{1,0:T(8,128)(2,1)S(1)}, u32[]{:S(2)}, u32[]{:S(2)}) collective-permute-start(bf16[64,1152]{1,0:T(8,128)(2,1)S(1)} %total_late.1.refs_2_.refs_0_), channel_id=1, source_target_pairs={{0,24},{8,16},{16,8},{24,0},{1,25},{9,17},{17,9},{25,1},{2,26},{10... | collective-permute-start | bytes 442376 | tf_op jit(solution)/shard_map/ppermute | solution.py:793
  172.3 7.8 %collective-permute-start.35 = (bf16[64,1152]{1,0:T(8,128)(2,1)S(1)}, bf16[64,1152]{1,0:T(8,128)(2,1)S(1)}, u32[]{:S(2)}, u32[]{:S(2)}) collective-permute-start(bf16[64,1152]{1,0:T(8,128)(2,1)S(1)} %total_late.1.refs_2_.refs_0_), channel_id=1, source_target_pairs={{0,16},{8,24},{16,0},{24,8},{1,17},{9,25},{17,1},{25,9},{2,18},{10... | collective-permute-start | bytes 442376 | tf_op jit(solution)/shard_map/ppermute | solution.py:793
  173.0 7.1 %collective-permute-start.34 = (bf16[64,1152]{1,0:T(8,128)(2,1)S(1)}, bf16[64,1152]{1,0:T(8,128)(2,1)S(1)}, u32[]{:S(2)}, u32[]{:S(2)}) collective-permute-start(bf16[64,1152]{1,0:T(8,128)(2,1)S(1)} %total_late.1.refs_2_.refs_0_), channel_id=1, source_target_pairs={{0,8},{8,0},{16,24},{24,16},{1,9},{9,1},{17,25},{25,17},{2,10},{10... | collective-permute-start | bytes 442376 | tf_op jit(solution)/shard_map/ppermute | solution.py:793
  (49 other events, 340.6 us)

commit v5 on v4

--- a/solution.py
+++ b/solution.py
@@ -316,13 +316,17 @@
     spec = spectrum2(left2[...], masked(own, ids == first_doc))
     set_spec(acc, times(lags[0], spec))
 
-    def cross(s, carry):
-        position = s * block + lax.broadcasted_iota(jnp.int32, (block, 1), 0)
-        spec = spectrum2(left2[...], masked(signal[s], position >= start))
-        add_spec(acc, times(lags[me - s], spec))
+    def cross(pair, carry):
+        total = None
+        for s in (low_block + 2 * pair, low_block + 2 * pair + 1):
+            position = s * block + lax.broadcasted_iota(jnp.int32, (block, 1), 0)
+            spec = spectrum2(left2[...], masked(signal[s], (position >= start) & (position < base)))
+            made = times(lags[me - s], spec)
+            total = made if total is None else (total[0] + made[0], total[1] + made[1])
+        add_spec(acc, total)
         return carry
 
-    lax.fori_loop(low_block, me, cross, 0)
+    lax.fori_loop(0, (me - low_block + 1) // 2, cross, 0)
     out[...] = jnp.where(ids == first_doc, spectrum3(inv3[...], acc[...]), 0.0)
 
     def inner(d, carry):
@@ -484,13 +488,20 @@
     spec = spectrum2(invt2[...], masked(own, ids == last_doc))
     set_spec(acc, times_back(lags[0], spec))
 
-    def cross(t, carry):
-        _, far = doc_column(meta, ndocs, t * block, block)
-        spec = spectrum2(invt2[...], masked(grads[t], far == last_doc))
-        add_spec(acc, times_back(lags[t - me], spec))
+    def cross(pair, carry):
+        total = None
+        for t in (me + 1 + 2 * pair, me + 2 + 2 * pair):
+            place = jnp.minimum(t, grads.shape[0] - 1)
+            _, far = doc_column(meta, ndocs, place * block, block)
+            spec = spectrum2(
+                invt2[...], masked(grads[place], (far == last_doc) & (t <= last_block))
+            )
+            made = times_back(lags[place - me], spec)
+            total = made if total is None else (total[0] + made[0], total[1] + made[1])
+        add_spec(acc, total)
         return carry
 
-    lax.fori_loop(me + 1, last_block + 1, cross, 0)
+    lax.fori_loop(0, (last_block - me + 1) // 2, cross, 0)
     for_in[...] = jnp.where(ids == last_doc, spectrum3(leftt3[...], acc[...]), 0.0)
 
     def inner(d, carry):
@@ -1267,19 +1278,6 @@
     )(meta, tok, cot, conv, carried, mixed, filter_bias, out_weight, out_bias, norm2_gain,
       norm2_bias, up_weight, up_bias, down_weight, down_bias)
 
-    taps_grad = pl.pallas_call(
-        partial(taps_grad_kernel, ndocs, nparts, signal_row),
-        grid=(steps,),
-        out_shape=sds((blocks, block, width), F32),
-        in_specs=[smem()] + part_specs + [
-            by_chunk((block,)), whole(tables["left2"].shape), whole(tables["invt2"].shape),
-            whole(tables["leftt3"].shape)],
-        out_specs=by_chunk((blocks, block)),
-        scratch_shapes=[pltpu.VMEM((blocks + 1, 2 * block, chunk), F32), spec_scratch] + held,
-        compiler_params=params(),
-        cost_estimate=cost(4.0),
-        name="taps_grad",
-    )(meta, *signal, glong, tables["left2"], tables["invt2"], tables["leftt3"])
     if packed:
         own, shared, e1_send, e2_send = acts
         got1, got2 = swap(e1_send, "rows", 1), swap(e2_send, "rows", 2)
@@ -1294,17 +1292,9 @@
             ), "seq", 1,
         )
         grad_specs = [whole(v.shape) for v in grads]
-        half_rows, small_cols = chips * SMALL_BLOCK, 128
-        mine, send = single(
-            filter_back_kernel, "filter_back", 5.0, [sds((half_rows, small_cols), F32)] * 2, meta,
-            [taps_grad, window, *net, table, filter_first, filter_second, filter_third, filter_last,
-             sine_freq, smalls_mlp],
-            after=[near_all], scratch=[pltpu.VMEM((2 * half_rows, small_cols), F32)],
-        )
     else:
         grads, grads_row = [lax.all_gather(glong16, "seq", axis=0, tiled=False)], 0
         grad_specs = part_specs
-        filter_grads = taps_pull(taps_grad.reshape(length, width))
 
     tied = ()
     third = lambda n: pl.BlockSpec((block, chunk), lambda i: (0, n * steps + i))
@@ -1343,10 +1333,6 @@
         tied = (parts1[0], parts2[0])
         keep1, send1 = parts1
         keep2, send2 = parts2
-        pairs = [keep1, swap(send1, "rows", 2), keep2, swap(send2, "rows", 1)]
-        first_sums = chip_sums(meta, pairs, "tiles", (mine, swap(send, "seq", 1)))
-
-
     tied = tied if packed else ()
     gproj, smalls_short, *late = single(
         partial(short_back_kernel, ndocs, packed), "short_back", 3.0,
@@ -1354,6 +1340,41 @@
         + ([sds((3 * width // 2, block), BF16)] * 2 if packed else []),
         meta, [ggate, for_in, for_values, rim_back, proj, short_weight], tied,
     )
+    if packed:
+        late, late_send = late
+        late_got = swap(late_send, "rows", 1)
+        tied = (late_got,)
+    else:
+        tied = ()
+    taps_grad = pl.pallas_call(
+        lambda *refs: taps_grad_kernel(
+            ndocs, nparts, signal_row, *refs[: nparts + 5], *refs[nparts + 5 + len(tied) :]
+        ),
+        grid=(steps,),
+        out_shape=sds((blocks, block, width), F32),
+        in_specs=[smem()] + part_specs + [
+            by_chunk((block,)), whole(tables["left2"].shape), whole(tables["invt2"].shape),
+            whole(tables["leftt3"].shape)]
+        + [pl.BlockSpec(memory_space=pl.ANY)] * len(tied),
+        out_specs=by_chunk((blocks, block)),
+        scratch_shapes=[pltpu.VMEM((blocks + 1, 2 * block, chunk), F32), spec_scratch] + held,
+        compiler_params=params(),
+        cost_estimate=cost(4.0),
+        name="taps_grad",
+    )(meta, *signal, glong, tables["left2"], tables["invt2"], tables["leftt3"], *tied)
+    if packed:
+        half_rows, small_cols = chips * SMALL_BLOCK, 128
+        mine, send = single(
+            filter_back_kernel, "filter_back", 5.0, [sds((half_rows, small_cols), F32)] * 2, meta,
+            [taps_grad, window, *net, table, filter_first, filter_second, filter_third, filter_last,
+             sine_freq, smalls_mlp],
+            after=[near_all], scratch=[pltpu.VMEM((2 * half_rows, small_cols), F32)],
+        )
+        pairs = [keep1, swap(send1, "rows", 2), keep2, swap(send2, "rows", 1)]
+        first_sums = chip_sums(meta, pairs, "tiles", (mine, swap(send, "seq", 1)))
+    else:
+        filter_grads = taps_pull(taps_grad.reshape(length, width))
+
     late_shape = (16, 3 * width // 2) if packed else (24, width)
     grad_tokens, smalls_late = single(
         tail_kernel, "tail", 2.5, [sds((block, width), F32), sds(late_shape, F32)],
@@ -1364,8 +1385,6 @@
         def placed(kernel, name, shapes, pieces):
             return single(kernel, name, 1.5, [sds(v, F32) for v in shapes], meta, pieces)
 
-        late, late_send = late
-        late_got = swap(late_send, "rows", 1)
         late_sib = swap(
             collected(
                 meta, [(late, (0, late.shape[0])), (late_got, (0, late.shape[0]))]

time: 183 us -> 184 us (level)
  no operation moved by 1% of the time
where the time goes in v5:
time: 184 us; the launch traced here: 183 us
  waiting for transfers between devices  61.9 us (34%)
  Pallas kernels  58.3 us (32%)
  starting transfers between devices  54 us (29%)
  local copies, waits for them, and re-layouts  7.53 us (4%)
    ppermute x35, waiting for transfers between devices, swap(): lax.ppermute(block, axis, [(i, i ^ mask) for i in range(lax.axis_size(axi...  61.9 us
    ppermute x35, starting transfers between devices, swap(): lax.ppermute(block, axis, [(i, i ^ mask) for i in range(lax.axis_size(axi...  50.3 us
    pallas_call x22, Pallas kernels, single(): pl.pallas_call(body, grid=(1,), out_shape=tuple(outs), in_specs=[smem()]...  37.2 us
    pallas_call x1, Pallas kernels, local(): pl.pallas_call(partial(mlp_kernel, packed), grid=(fsteps,), out_shape=(sd...  9.91 us
    unnamed x88, local copies, waits for them, and re-layouts  5.53 us
    pallas_call x1, Pallas kernels, local(): pl.pallas_call(lambda *refs: conv_back_kernel(ndocs, length, nparts, grad...  5.4 us
  transfers between devices with their start and end apart: 37, of which 16 were waited for; matrix products, arithmetic and copies ran while one was open for 1% of the time, Pallas kernels for 19%

profile of v5, /device:TPU:0, one launch (start us, length us, event | category | flops | bytes accessed | tf_op | source)
XLA Modules:
  0.0 183.3 jit_solution(3889015670778154284)
XLA Ops:
  1.4 2.3 %collective-permute-start = (bf16[16,768]{1,0:T(8,128)(2,1)S(1)}, bf16[16,768]{1,0:T(8,128)(2,1)S(1)}, u32[]{:S(2)}, u32[]{:S(2)}) collective-permute-start(bf16[16,768]{1,0:T(8,128)(2,1)S(1)} %slice_bitcast_fusion), channel_id=1, source_target_pairs={{0,1},{1,2},{2,3},{3,4},{4,5},{5,6},{6,7},{8,9},{9,10},{10,11},{11... | collective-permute-start | bytes 73736 | tf_op jit(solution)/shard_map/ppermute | solution.py:800
  5.7 5.1 %front.1 = (f32[144,2304]{1,0:T(8,128)}, bf16[1536,128]{1,0:T(8,128)(2,1)}, f32[128,2304]{1,0:T(8,128)}, bf16[128,768]{1,0:T(8,128)(2,1)}) custom-call(s32[9]{0:T(128)} %concatenate.3.meta.refs_0_, bf16[128,768]{1,0:T(8,128)(2,1)} %bitcast.11, bf16[16,768]{1,0:T(8,128)(2,1)} %copy-done.39, bf16[128,768]{1,0:T(8,128)(2,1)} %bitcast.18, ...), custom_call_target="tpu_custom_call" | custom-call | flops 3300000000 | tf_op jit(solution)/shard_map/front/pallas_call | solution.py:58
  10.8 6.6 %collective-permute-start.3 = (bf16[128,768]{1,0:T(8,128)(2,1)}, bf16[128,768]{1,0:T(8,128)(2,1)S(1)}, u32[]{:S(2)}, u32[]{:S(2)}) collective-permute-start(bf16[128,768]{1,0:T(8,128)(2,1)} %get-tuple-element.91.refs_10_.refs_2_.refs_0_.carried.refs_1_), channel_id=1, source_target_pairs={{0,6},{1,7},{2,4},{3,5},{4,2},{5,3},{6,0},{7,1},{8,14},{9,15},{10,... | collective-permute-start | bytes 589832 | tf_op jit(solution)/shard_map/ppermute | solution.py:804
  20.5 5.4 %filter.1 = (f32[8,256,768]{2,1,0:T(8,128)S(1)}, f32[1024,768]{1,0:T(8,128)S(1)}, f32[192,1024]{1,0:T(8,128)S(1)}, f32[192,1024]{1,0:T(8,128)S(1)}, f32[192,1024]{1,0:T(8,128)S(1)}) custom-call(s32[9]{0:T(128)S(1)} %copy-done.3, f32[40,1024]{1,0:T(8,128)S(1)} %copy-done.28, bf16[33,64]{1,0:T(8,128)(2,1)S(1)} %copy-done.12, bf16[64]{0:T(256)(128)(2,1)S(1)} %copy-done.20, ...), custom_call_target="tpu_custom_call" | custom-call | flops 8800000000 | tf_op jit(solution)/shard_map/filter/pallas_call | solution.py:58
  25.9 1.6 copy-done.32
  28.4 5.8 %collective-permute-done.2.refs_4_.refs_2_.refs_3_ = bf16[128,768]{1,0:T(8,128)(2,1)S(1)} collective-permute-done((bf16[128,768]{1,0:T(8,128)(2,1)}, bf16[128,768]{1,0:T(8,128)(2,1)S(1)}, u32[]{:S(2)}, u32[]{:S(2)}) %collective-permute-start.2) | collective-permute-done | bytes 196640 | tf_op jit(solution)/shard_map/ppermute | solution.py:804
  35.2 3.1 %collective-permute-done.5.refs_4_.refs_7_.refs_5_ = bf16[5376,128]{1,0:T(8,128)(2,1)S(1)} collective-permute-done((bf16[5376,128]{1,0:T(8,128)(2,1)S(1)}, bf16[5376,128]{1,0:T(8,128)(2,1)S(1)}, u32[]{:S(2)}, u32[]{:S(2)}) %collective-permute-start.5) | collective-permute-done | bytes 1376288 | tf_op jit(solution)/shard_map/ppermute | solution.py:804
  38.3 2.9 %conv.1 = f32[128,768]{1,0:T(8,128)S(1)} custom-call(s32[9]{0:T(128)S(1)} %copy-done.3, bf16[128,768]{1,0:T(8,128)(2,1)S(1)} %copy-done.1, bf16[128,768]{1,0:T(8,128)(2,1)S(1)} %collective-permute-done.1.refs_3_.refs_1_.refs_2_, bf16[128,768]{1,0:T(8,128)(2,1)S(1)} %collective-permute-done.2.refs_4_.refs_2_.refs_3_, ...), custom_call_target="tpu_custom_call" | custom-call | flops 3300000000 | tf_op jit(solution)/shard_map/conv/pallas_call | solution.py:1227
  41.4 9.9 %mlp.1 = (bf16[128,768]{1,0:T(8,128)(2,1)}, f32[128,768]{1,0:T(8,128)S(1)}, f32[128,768]{1,0:T(8,128)S(1)}, bf16[128,768]{1,0:T(8,128)(2,1)S(1)}, f32[128,768]{1...) custom-call(s32[9]{0:T(128)S(1)} %copy-done.3, ...), custom_call_target="tpu_custom_call" | custom-call | flops 11000000512 | tf_op jit(solution)/shard_map/mlp/pallas_call | solution.py:1254
  54.3 2.8 %collective-permute-start.8 = (bf16[128,768]{1,0:T(8,128)(2,1)S(1)}, bf16[128,768]{1,0:T(8,128)(2,1)S(1)}, u32[]{:S(2)}, u32[]{:S(2)}) collective-permute-start(bf16[128,768]{1,0:T(8,128)(2,1)S(1)} %get-tuple-element.97.refs_0_.refs_1_), channel_id=1, source_target_pairs={{0,6},{1,7},{2,4},{3,5},{4,2},{5,3},{6,0},{7,1},{8,14},{9,15},{10,... | collective-permute-start | bytes 589832 | tf_op jit(solution)/shard_map/ppermute | solution.py:804
  58.7 5.3 %collective-permute-done.8.refs_3_.refs_4_ = bf16[128,768]{1,0:T(8,128)(2,1)S(1)} collective-permute-done((bf16[128,768]{1,0:T(8,128)(2,1)S(1)}, bf16[128,768]{1,0:T(8,128)(2,1)S(1)}, u32[]{:S(2)}, u32[]{:S(2)}) %collective-permute-start.8) | collective-permute-done | bytes 196640 | tf_op jit(solution)/shard_map/ppermute | solution.py:804
  64.1 8.3 %collective-permute-done.7.refs_2_.refs_3_ = bf16[128,768]{1,0:T(8,128)(2,1)S(1)} collective-permute-done((bf16[128,768]{1,0:T(8,128)(2,1)S(1)}, bf16[128,768]{1,0:T(8,128)(2,1)S(1)}, u32[]{:S(2)}, u32[]{:S(2)}) %collective-permute-start.7) | collective-permute-done | bytes 196640 | tf_op jit(solution)/shard_map/ppermute | solution.py:804
  75.4 5.4 %conv_back.1 = (f32[128,768]{1,0:T(8,128)S(1)}, f32[128,768]{1,0:T(8,128)S(1)}, f32[3,8,768]{2,1,0:T(8,128)S(1)}) custom-call(s32[9]{0:T(128)S(1)} %copy-done.3, bf16[128,768]{1,0:T(8,128)(2,1)S(1)} %get-tuple-element.97.refs_0_.refs_1_, bf16[128,768]{1,0:T(8,128)(2,1)S(1)} %collective-permute-done.6.refs_1_.refs_2_, ...), custom_call_target="tpu_custom_call" | custom-call | flops 4400000000 | tf_op jit(solution)/shard_map/conv_back/pallas_call | solution.py:1302
  82.1 1.8 up_grad.1
  83.9 1.7 down_out.1
  85.6 2.7 %short_back.1 = (bf16[128,2304]{1,0:T(8,128)(2,1)S(1)}, f32[24,768]{1,0:T(8,128)S(1)}, bf16[1152,128]{1,0:T(8,128)(2,1)S(1)}, bf16[1152,128]{1,0:T(8,128)(2,1)S(1)}) custom-call(s32[9]{0:T(128)S(1)} %copy-done.3, f32[128,768]{1,0:T(8,128)S(1)} %get-tuple-element.96.refs_13_.refs_0_, f32[128,768]{1,0:T(8,128)S(1)} %get-tuple-element.99.refs_1_, ...), custom_call_target="tpu_custom_call" | custom-call | flops 3300000000 | tf_op jit(solution)/shard_map/short_back/pallas_call | solution.py:58
  90.9 7.2 %collective-permute-done.17.refs_10_.refs_1_ = bf16[1152,128]{1,0:T(8,128)(2,1)S(1)} collective-permute-done((bf16[1152,128]{1,0:T(8,128)(2,1)S(1)}, bf16[1152,128]{1,0:T(8,128)(2,1)S(1)}, u32[]{:S(2)}, u32[]{:S(2)}) %collective-permute-start.17) | collective-permute-done | bytes 294944 | tf_op jit(solution)/shard_map/ppermute | solution.py:804
  99.2 2.8 %taps_grad.1.refs_0_ = f32[8,128,768]{2,1,0:T(8,128)S(1)} custom-call(s32[9]{0:T(128)S(1)} %copy-done.3, bf16[128,768]{1,0:T(8,128)(2,1)S(1)} %copy-done.2, bf16[128,768]{1,0:T(8,128)(2,1)S(1)} %collective-permute-done.1.refs_3_.refs_1_.refs_2_, bf16[128,768]{1,0:T(8,128)(2,1)S(1)} %collective-permute-done.2.refs_4_.refs_2_.refs_3_, ...), custom_call_target="tpu_custom_call" | custom-call | flops 4400000000 | tf_op jit(solution)/shard_map/taps_grad/pallas_call | solution.py:1349
  102.1 4.4 %filter_back.1 = (f32[320,128]{1,0:T(8,128)S(1)}, f32[320,128]{1,0:T(8,128)S(1)}) custom-call(s32[9]{0:T(128)S(1)} %copy-done.3, f32[8,128,768]{2,1,0:T(8,128)S(1)} %taps_grad.1.refs_0_, f32[1024,768]{1,0:T(8,128)S(1)} %copy-done.33, f32[192,1024]{1,0:T(8,128)S(1)} %get-tuple-element.117.refs_2_, f32[192,1024]{1,0:T(8,128)S(1)} %copy-done.36, ...), custom_call_target="tpu_custom_call" | custom-call | flops 5500000256 | tf_op jit(solution)/shard_map/filter_back/pallas_call | solution.py:58
  107.9 2.8 %collective-permute-done.16.refs_3_ = bf16[4,96,768]{2,1,0:T(8,128)(2,1)S(1)} collective-permute-done((bf16[4,96,768]{2,1,0:T(8,128)(2,1)S(1)}, bf16[4,96,768]{2,1,0:T(8,128)(2,1)S(1)}, u32[]{:S(2)}, u32[]{:S(2)}) %collective-permute-start.16) | collective-permute-done | bytes 589856 | tf_op jit(solution)/shard_map/ppermute | solution.py:804
  113.6 2.1 %collective-permute-start.20 = (bf16[96,1920]{1,0:T(8,128)(2,1)S(1)}, bf16[96,1920]{1,0:T(8,128)(2,1)S(1)}, u32[]{:S(2)}, u32[]{:S(2)}) collective-permute-start(bf16[96,1920]{1,0:T(8,128)(2,1)S(1)} %get-tuple-element.125), channel_id=1, source_target_pairs={{0,4},{1,5},{2,6},{3,7},{4,0},{5,1},{6,2},{7,3},{8,12},{9,13},{10,... | collective-permute-start | bytes 1105928 | tf_op jit(solution)/shard_map/ppermute | solution.py:804
  115.7 2.2 %collective-permute-start.21 = (bf16[96,1920]{1,0:T(8,128)(2,1)S(1)}, bf16[96,1920]{1,0:T(8,128)(2,1)S(1)}, u32[]{:S(2)}, u32[]{:S(2)}) collective-permute-start(bf16[96,1920]{1,0:T(8,128)(2,1)S(1)} %get-tuple-element.126), channel_id=1, source_target_pairs={{0,6},{1,7},{2,4},{3,5},{4,2},{5,3},{6,0},{7,1},{8,14},{9,15},{10,... | collective-permute-start | bytes 1105928 | tf_op jit(solution)/shard_map/ppermute | solution.py:804
  118.0 2.7 %tail.1 = (f32[128,768]{1,0:T(8,128)}, f32[16,1152]{1,0:T(8,128)S(1)}) custom-call(s32[9]{0:T(128)S(1)} %copy-done.3, bf16[128,2304]{1,0:T(8,128)(2,1)S(1)} %get-tuple-element.109.refs_0_, bf16[768,2304]{1,0:T(8,128)(2,1)S(1)} %copy-done.5, bf16[128,768]{1,0:T(8,128)(2,1)S(1)} %bitcast.13, bf16[768]{0:T(1024)(128)(2,1)S(1)} %copy-done.19, ...), custom_call_target="tpu_custom_call" | custom-call | flops 2750000128 | tf_op jit(solution)/shard_map/tail/pallas_call | solution.py:58
  122.0 3.3 %collective-permute-done.23.refs_1_ = bf16[4,48,1152]{2,1,0:T(8,128)(2,1)S(1)} collective-permute-done((bf16[4,48,1152]{2,1,0:T(8,128)(2,1)S(1)}, bf16[4,48,1152]{2,1,0:T(8,128)(2,1)S(1)}, u32[]{:S(2)}, u32[]{:S(2)}) %collective-permute-start.23) | collective-permute-done | bytes 442400 | tf_op jit(solution)/shard_map/ppermute | solution.py:804
  126.0 6.4 %collective-permute-done.19.refs_1_ = bf16[96,1920]{1,0:T(8,128)(2,1)S(1)} collective-permute-done((bf16[96,1920]{1,0:T(8,128)(2,1)S(1)}, bf16[96,1920]{1,0:T(8,128)(2,1)S(1)}, u32[]{:S(2)}, u32[]{:S(2)}) %collective-permute-start.19) | collective-permute-done | bytes 368672 | tf_op jit(solution)/shard_map/ppermute | solution.py:804
  132.3 9.5 %collective-permute-done.20.refs_2_ = bf16[96,1920]{1,0:T(8,128)(2,1)S(1)} collective-permute-done((bf16[96,1920]{1,0:T(8,128)(2,1)S(1)}, bf16[96,1920]{1,0:T(8,128)(2,1)S(1)}, u32[]{:S(2)}, u32[]{:S(2)}) %collective-permute-start.20) | collective-permute-done | bytes 368672 | tf_op jit(solution)/shard_map/ppermute | solution.py:804
  142.5 1.6 collective-permute-start.27
  146.7 7.8 %collective-permute-start.33 = (bf16[64,1152]{1,0:T(8,128)(2,1)S(1)}, bf16[64,1152]{1,0:T(8,128)(2,1)S(1)}, u32[]{:S(2)}, u32[]{:S(2)}) collective-permute-start(bf16[64,1152]{1,0:T(8,128)(2,1)S(1)} %get-tuple-element.135), channel_id=1, source_target_pairs={{0,4},{1,5},{2,6},{3,7},{4,0},{5,1},{6,2},{7,3},{8,12},{9,13},{10,... | collective-permute-start | bytes 442376 | tf_op jit(solution)/shard_map/ppermute | solution.py:804
  155.0 4.5 %collective-permute-done.26.refs_2_ = bf16[96,1920]{1,0:T(8,128)(2,1)S(1)} collective-permute-done((bf16[96,1920]{1,0:T(8,128)(2,1)S(1)}, bf16[96,1920]{1,0:T(8,128)(2,1)S(1)}, u32[]{:S(2)}, u32[]{:S(2)}) %collective-permute-start.26) | collective-permute-done | bytes 368672 | tf_op jit(solution)/shard_map/ppermute | solution.py:804
  160.1 1.8 collective-permute-start.30
  162.0 8.5 %collective-permute-start.29 = (f32[80,128]{1,0:T(8,128)S(1)}, f32[80,128]{1,0:T(8,128)S(1)}, u32[]{:S(2)}, u32[]{:S(2)}) collective-permute-start(f32[80,128]{1,0:T(8,128)S(1)} %small.1.refs_0_), channel_id=1, source_target_pairs={{0,4},{1,5},{2,6},{3,7},{4,0},{5,1},{6,2},{7,3},{8,12},{9,13},{10,... | collective-permute-start | bytes 122888 | tf_op jit(solution)/shard_map/ppermute | solution.py:804
  174.6 2.2 %place_early.1 = (f32[384,768]{1,0:T(8,128)}, f32[96,768]{1,0:T(8,128)}, f32[96,3072]{1,0:T(8,128)}) custom-call(s32[9]{0:T(128)S(1)} %copy-done.3, bf16[96,1920]{1,0:T(8,128)(2,1)S(1)} %total.1.refs_0_, bf16[96,1920]{1,0:T(8,128)(2,1)S(1)} %collective-permute-done.25.refs_1_, bf16[96,1920]{1,0:T(8,128)(2,1)S(1)} %collective-permute-done.26.refs_2_, ...), custom_call_target="tpu_custom_call" | custom-call | flops 1650000000 | tf_op jit(solution)/shard_map/place_early/pallas_call | solution.py:58
  (160 shorter events, 41.2 us)
Async XLA Ops:
  1.4 3.6 %collective-permute-start = (bf16[16,768]{1,0:T(8,128)(2,1)S(1)}, bf16[16,768]{1,0:T(8,128)(2,1)S(1)}, u32[]{:S(2)}, u32[]{:S(2)}) collective-permute-start(bf16[16,768]{1,0:T(8,128)(2,1)S(1)} %slice_bitcast_fusion), channel_id=1, source_target_pairs={{0,1},{1,2},{2,3},{3,4},{4,5},{5,6},{6,7},{8,9},{9,10},{10,11},{11... | collective-permute-start | bytes 73736 | tf_op jit(solution)/shard_map/ppermute | solution.py:800
  10.8 17.6 %collective-permute-start.3 = (bf16[128,768]{1,0:T(8,128)(2,1)}, bf16[128,768]{1,0:T(8,128)(2,1)S(1)}, u32[]{:S(2)}, u32[]{:S(2)}) collective-permute-start(bf16[128,768]{1,0:T(8,128)(2,1)} %get-tuple-element.91.refs_10_.refs_2_.refs_0_.carried.refs_1_), channel_id=1, source_target_pairs={{0,6},{1,7},{2,4},{3,5},{4,2},{5,3},{6,0},{7,1},{8,14},{9,15},{10,... | collective-permute-start | bytes 589832 | tf_op jit(solution)/shard_map/ppermute | solution.py:804
  17.4 16.8 %collective-permute-start.2 = (bf16[128,768]{1,0:T(8,128)(2,1)}, bf16[128,768]{1,0:T(8,128)(2,1)S(1)}, u32[]{:S(2)}, u32[]{:S(2)}) collective-permute-start(bf16[128,768]{1,0:T(8,128)(2,1)} %get-tuple-element.91.refs_10_.refs_2_.refs_0_.carried.refs_1_), channel_id=1, source_target_pairs={{0,4},{1,5},{2,6},{3,7},{4,0},{5,1},{6,2},{7,3},{8,12},{9,13},{10,... | collective-permute-start | bytes 589832 | tf_op jit(solution)/shard_map/ppermute | solution.py:804
  17.4 16.8 %collective-permute-start.1 = (bf16[128,768]{1,0:T(8,128)(2,1)}, bf16[128,768]{1,0:T(8,128)(2,1)S(1)}, u32[]{:S(2)}, u32[]{:S(2)}) collective-permute-start(bf16[128,768]{1,0:T(8,128)(2,1)} %get-tuple-element.91.refs_10_.refs_2_.refs_0_.carried.refs_1_), channel_id=1, source_target_pairs={{0,2},{1,3},{2,0},{3,1},{4,6},{5,7},{6,4},{7,5},{8,10},{9,11},{10,... | collective-permute-start | bytes 589832 | tf_op jit(solution)/shard_map/ppermute | solution.py:804
  18.0 16.2 %collective-permute-start.4 = (bf16[1536,128]{1,0:T(8,128)(2,1)}, bf16[1536,128]{1,0:T(8,128)(2,1)S(1)}, u32[]{:S(2)}, u32[]{:S(2)}) collective-permute-start(bf16[1536,128]{1,0:T(8,128)(2,1)} %get-tuple-element.92.refs_0_.refs_5_.refs_3_), channel_id=1, source_target_pairs={{0,8},{8,0},{16,24},{24,16},{1,9},{9,1},{17,25},{25,17},{2,10},{10... | collective-permute-start | bytes 1179656 | tf_op jit(solution)/shard_map/ppermute | solution.py:804
  51.4 22.3 %collective-permute-start.12 = (bf16[2688,128]{1,0:T(8,128)(2,1)S(1)}, bf16[2688,128]{1,0:T(8,128)(2,1)S(1)}, u32[]{:S(2)}, u32[]{:S(2)}) collective-permute-start(bf16[2688,128]{1,0:T(8,128)(2,1)S(1)} %get-tuple-element.105), channel_id=1, source_target_pairs={{0,8},{8,0},{16,24},{24,16},{1,9},{9,1},{17,25},{25,17},{2,10},{10... | collective-permute-start | bytes 2064392 | tf_op jit(solution)/shard_map/ppermute | solution.py:804
  52.8 20.8 %collective-permute-start.13 = (bf16[2304,128]{1,0:T(8,128)(2,1)S(1)}, bf16[2304,128]{1,0:T(8,128)(2,1)S(1)}, u32[]{:S(2)}, u32[]{:S(2)}) collective-permute-start(bf16[2304,128]{1,0:T(8,128)(2,1)S(1)} %get-tuple-element.106), channel_id=1, source_target_pairs={{0,16},{8,24},{16,0},{24,8},{1,17},{9,25},{17,1},{25,9},{2,18},{10... | collective-permute-start | bytes 1769480 | tf_op jit(solution)/shard_map/ppermute | solution.py:804
  54.3 9.7 %collective-permute-start.8 = (bf16[128,768]{1,0:T(8,128)(2,1)S(1)}, bf16[128,768]{1,0:T(8,128)(2,1)S(1)}, u32[]{:S(2)}, u32[]{:S(2)}) collective-permute-start(bf16[128,768]{1,0:T(8,128)(2,1)S(1)} %get-tuple-element.97.refs_0_.refs_1_), channel_id=1, source_target_pairs={{0,6},{1,7},{2,4},{3,5},{4,2},{5,3},{6,0},{7,1},{8,14},{9,15},{10,... | collective-permute-start | bytes 589832 | tf_op jit(solution)/shard_map/ppermute | solution.py:804
  57.2 15.2 %collective-permute-start.7 = (bf16[128,768]{1,0:T(8,128)(2,1)S(1)}, bf16[128,768]{1,0:T(8,128)(2,1)S(1)}, u32[]{:S(2)}, u32[]{:S(2)}) collective-permute-start(bf16[128,768]{1,0:T(8,128)(2,1)S(1)} %get-tuple-element.97.refs_0_.refs_1_), channel_id=1, source_target_pairs={{0,4},{1,5},{2,6},{3,7},{4,0},{5,1},{6,2},{7,3},{8,12},{9,13},{10,... | collective-permute-start | bytes 589832 | tf_op jit(solution)/shard_map/ppermute | solution.py:804
  57.2 15.2 %collective-permute-start.6 = (bf16[128,768]{1,0:T(8,128)(2,1)S(1)}, bf16[128,768]{1,0:T(8,128)(2,1)S(1)}, u32[]{:S(2)}, u32[]{:S(2)}) collective-permute-start(bf16[128,768]{1,0:T(8,128)(2,1)S(1)} %get-tuple-element.97.refs_0_.refs_1_), channel_id=1, source_target_pairs={{0,2},{1,3},{2,0},{3,1},{4,6},{5,7},{6,4},{7,5},{8,10},{9,11},{10,... | collective-permute-start | bytes 589832 | tf_op jit(solution)/shard_map/ppermute | solution.py:804
  73.2 8.9 %collective-permute-start.11 = (bf16[3456,128]{1,0:T(8,128)(2,1)S(1)}, bf16[3456,128]{1,0:T(8,128)(2,1)S(1)}, u32[]{:S(2)}, u32[]{:S(2)}) collective-permute-start(bf16[3456,128]{1,0:T(8,128)(2,1)S(1)} %get-tuple-element.104.refs_1_), channel_id=1, source_target_pairs={{0,1},{1,0},{2,3},{3,2},{4,5},{5,4},{6,7},{7,6},{8,9},{9,8},{10,11... | collective-permute-start | bytes 2654216 | tf_op jit(solution)/shard_map/ppermute | solution.py:804
  74.2 7.9 %collective-permute-start.14 = (bf16[3456,128]{1,0:T(8,128)(2,1)S(1)}, bf16[3456,128]{1,0:T(8,128)(2,1)S(1)}, u32[]{:S(2)}, u32[]{:S(2)}) collective-permute-start(bf16[3456,128]{1,0:T(8,128)(2,1)S(1)} %collect.6), channel_id=1, source_target_pairs={{0,1},{1,0},{2,3},{3,2},{4,5},{5,4},{6,7},{7,6},{8,9},{9,8},{10,11... | collective-permute-start | bytes 2654216 | tf_op jit(solution)/shard_map/ppermute | solution.py:804
  80.8 4.8 %collective-permute-start.10 = (f32[3,8,768]{2,1,0:T(8,128)S(1)}, f32[3,8,768]{2,1,0:T(8,128)S(1)}, u32[]{:S(2)}, u32[]{:S(2)}) collective-permute-start(f32[3,8,768]{2,1,0:T(8,128)S(1)} %get-tuple-element.101.refs_8_.refs_5_), channel_id=1, source_target_pairs={{1,0},{2,1},{3,2},{4,3},{5,4},{6,5},{7,6},{9,8},{10,9},{11,10},{12... | collective-permute-start | bytes 221192 | tf_op jit(solution)/shard_map/ppermute | solution.py:800
  88.3 9.8 %collective-permute-start.17 = (bf16[1152,128]{1,0:T(8,128)(2,1)S(1)}, bf16[1152,128]{1,0:T(8,128)(2,1)S(1)}, u32[]{:S(2)}, u32[]{:S(2)}) collective-permute-start(bf16[1152,128]{1,0:T(8,128)(2,1)S(1)} %get-tuple-element.115), channel_id=1, source_target_pairs={{0,8},{8,0},{16,24},{24,16},{1,9},{9,1},{17,25},{25,17},{2,10},{10... | collective-permute-start | bytes 884744 | tf_op jit(solution)/shard_map/ppermute | solution.py:804
  88.9 21.8 %collective-permute-start.16 = (bf16[4,96,768]{2,1,0:T(8,128)(2,1)S(1)}, bf16[4,96,768]{2,1,0:T(8,128)(2,1)S(1)}, u32[]{:S(2)}, u32[]{:S(2)}) collective-permute-start(bf16[4,96,768]{2,1,0:T(8,128)(2,1)S(1)} %get-tuple-element.114), channel_id=1, source_target_pairs={{0,8},{8,0},{16,24},{24,16},{1,9},{9,1},{17,25},{25,17},{2,10},{10... | collective-permute-start | bytes 1769480 | tf_op jit(solution)/shard_map/ppermute | solution.py:804
  90.4 20.3 %collective-permute-start.15 = (bf16[4,96,1024]{2,1,0:T(8,128)(2,1)S(1)}, bf16[4,96,1024]{2,1,0:T(8,128)(2,1)S(1)}, u32[]{:S(2)}, u32[]{:S(2)}) collective-permute-start(bf16[4,96,1024]{2,1,0:T(8,128)(2,1)S(1)} %get-tuple-element.113), channel_id=1, source_target_pairs={{0,16},{8,24},{16,0},{24,8},{1,17},{9,25},{17,1},{25,9},{2,18},{10... | collective-permute-start | bytes 2359304 | tf_op jit(solution)/shard_map/ppermute | solution.py:804
  98.7 12.9 %collective-permute-start.22 = (bf16[2304,128]{1,0:T(8,128)(2,1)S(1)}, bf16[2304,128]{1,0:T(8,128)(2,1)S(1)}, u32[]{:S(2)}, u32[]{:S(2)}) collective-permute-start(bf16[2304,128]{1,0:T(8,128)(2,1)S(1)} %collect.7), channel_id=1, source_target_pairs={{0,1},{1,0},{2,3},{3,2},{4,5},{5,4},{6,7},{7,6},{8,9},{9,8},{10,11... | collective-permute-start | bytes 1769480 | tf_op jit(solution)/shard_map/ppermute | solution.py:804
  113.0 12.3 %collective-permute-start.23 = (bf16[4,48,1152]{2,1,0:T(8,128)(2,1)S(1)}, bf16[4,48,1152]{2,1,0:T(8,128)(2,1)S(1)}, u32[]{:S(2)}, u32[]{:S(2)}) collective-permute-start(bf16[4,48,1152]{2,1,0:T(8,128)(2,1)S(1)} %get-tuple-element.129), channel_id=1, source_target_pairs={{0,16},{8,24},{16,0},{24,8},{1,17},{9,25},{17,1},{25,9},{2,18},{10... | collective-permute-start | bytes 1327112 | tf_op jit(solution)/shard_map/ppermute | solution.py:804
  113.6 18.8 %collective-permute-start.19 = (bf16[96,1920]{1,0:T(8,128)(2,1)S(1)}, bf16[96,1920]{1,0:T(8,128)(2,1)S(1)}, u32[]{:S(2)}, u32[]{:S(2)}) collective-permute-start(bf16[96,1920]{1,0:T(8,128)(2,1)S(1)} %get-tuple-element.124), channel_id=1, source_target_pairs={{0,2},{1,3},{2,0},{3,1},{4,6},{5,7},{6,4},{7,5},{8,10},{9,11},{10,... | collective-permute-start | bytes 1105928 | tf_op jit(solution)/shard_map/ppermute | solution.py:804
  113.6 28.2 %collective-permute-start.20 = (bf16[96,1920]{1,0:T(8,128)(2,1)S(1)}, bf16[96,1920]{1,0:T(8,128)(2,1)S(1)}, u32[]{:S(2)}, u32[]{:S(2)}) collective-permute-start(bf16[96,1920]{1,0:T(8,128)(2,1)S(1)} %get-tuple-element.125), channel_id=1, source_target_pairs={{0,4},{1,5},{2,6},{3,7},{4,0},{5,1},{6,2},{7,3},{8,12},{9,13},{10,... | collective-permute-start | bytes 1105928 | tf_op jit(solution)/shard_map/ppermute | solution.py:804
  115.7 26.1 %collective-permute-start.21 = (bf16[96,1920]{1,0:T(8,128)(2,1)S(1)}, bf16[96,1920]{1,0:T(8,128)(2,1)S(1)}, u32[]{:S(2)}, u32[]{:S(2)}) collective-permute-start(bf16[96,1920]{1,0:T(8,128)(2,1)S(1)} %get-tuple-element.126), channel_id=1, source_target_pairs={{0,6},{1,7},{2,4},{3,5},{4,2},{5,3},{6,0},{7,1},{8,14},{9,15},{10,... | collective-permute-start | bytes 1105928 | tf_op jit(solution)/shard_map/ppermute | solution.py:804
  125.9 20.2 %collective-permute-start.32 = (bf16[2,64,1152]{2,1,0:T(8,128)(2,1)S(1)}, bf16[2,64,1152]{2,1,0:T(8,128)(2,1)S(1)}, u32[]{:S(2)}, u32[]{:S(2)}) collective-permute-start(bf16[2,64,1152]{2,1,0:T(8,128)(2,1)S(1)} %get-tuple-element.133), channel_id=1, source_target_pairs={{0,2},{1,3},{2,0},{3,1},{4,6},{5,7},{6,4},{7,5},{8,10},{9,11},{10,... | collective-permute-start | bytes 884744 | tf_op jit(solution)/shard_map/ppermute | solution.py:804
  142.5 12.5 %collective-permute-start.27 = (bf16[96,1920]{1,0:T(8,128)(2,1)S(1)}, bf16[96,1920]{1,0:T(8,128)(2,1)S(1)}, u32[]{:S(2)}, u32[]{:S(2)}) collective-permute-start(bf16[96,1920]{1,0:T(8,128)(2,1)S(1)} %total.1.refs_0_), channel_id=1, source_target_pairs={{0,24},{8,16},{16,8},{24,0},{1,25},{9,17},{17,9},{25,1},{2,26},{10... | collective-permute-start | bytes 1105928 | tf_op jit(solution)/shard_map/ppermute | solution.py:804
  144.1 15.4 %collective-permute-start.26 = (bf16[96,1920]{1,0:T(8,128)(2,1)S(1)}, bf16[96,1920]{1,0:T(8,128)(2,1)S(1)}, u32[]{:S(2)}, u32[]{:S(2)}) collective-permute-start(bf16[96,1920]{1,0:T(8,128)(2,1)S(1)} %total.1.refs_0_), channel_id=1, source_target_pairs={{0,16},{8,24},{16,0},{24,8},{1,17},{9,25},{17,1},{25,9},{2,18},{10... | collective-permute-start | bytes 1105928 | tf_op jit(solution)/shard_map/ppermute | solution.py:804
  144.6 15.0 %collective-permute-start.25 = (bf16[96,1920]{1,0:T(8,128)(2,1)S(1)}, bf16[96,1920]{1,0:T(8,128)(2,1)S(1)}, u32[]{:S(2)}, u32[]{:S(2)}) collective-permute-start(bf16[96,1920]{1,0:T(8,128)(2,1)S(1)} %total.1.refs_0_), channel_id=1, source_target_pairs={{0,8},{8,0},{16,24},{24,16},{1,9},{9,1},{17,25},{25,17},{2,10},{10... | collective-permute-start | bytes 1105928 | tf_op jit(solution)/shard_map/ppermute | solution.py:804
  146.7 23.7 %collective-permute-start.33 = (bf16[64,1152]{1,0:T(8,128)(2,1)S(1)}, bf16[64,1152]{1,0:T(8,128)(2,1)S(1)}, u32[]{:S(2)}, u32[]{:S(2)}) collective-permute-start(bf16[64,1152]{1,0:T(8,128)(2,1)S(1)} %get-tuple-element.135), channel_id=1, source_target_pairs={{0,4},{1,5},{2,6},{3,7},{4,0},{5,1},{6,2},{7,3},{8,12},{9,13},{10,... | collective-permute-start | bytes 442376 | tf_op jit(solution)/shard_map/ppermute | solution.py:804
  160.1 12.9 %collective-permute-start.30 = (f32[80,128]{1,0:T(8,128)S(1)}, f32[80,128]{1,0:T(8,128)S(1)}, u32[]{:S(2)}, u32[]{:S(2)}) collective-permute-start(f32[80,128]{1,0:T(8,128)S(1)} %small.1.refs_0_), channel_id=1, source_target_pairs={{0,6},{1,7},{2,4},{3,5},{4,2},{5,3},{6,0},{7,1},{8,14},{9,15},{10,... | collective-permute-start | bytes 122888 | tf_op jit(solution)/shard_map/ppermute | solution.py:804
  162.0 14.8 %collective-permute-start.29 = (f32[80,128]{1,0:T(8,128)S(1)}, f32[80,128]{1,0:T(8,128)S(1)}, u32[]{:S(2)}, u32[]{:S(2)}) collective-permute-start(f32[80,128]{1,0:T(8,128)S(1)} %small.1.refs_0_), channel_id=1, source_target_pairs={{0,4},{1,5},{2,6},{3,7},{4,0},{5,1},{6,2},{7,3},{8,12},{9,13},{10,... | collective-permute-start | bytes 122888 | tf_op jit(solution)/shard_map/ppermute | solution.py:804
  170.4 6.4 %collective-permute-start.28 = (f32[80,128]{1,0:T(8,128)S(1)}, f32[80,128]{1,0:T(8,128)S(1)}, u32[]{:S(2)}, u32[]{:S(2)}) collective-permute-start(f32[80,128]{1,0:T(8,128)S(1)} %small.1.refs_0_), channel_id=1, source_target_pairs={{0,2},{1,3},{2,0},{3,1},{4,6},{5,7},{6,4},{7,5},{8,10},{9,11},{10,... | collective-permute-start | bytes 122888 | tf_op jit(solution)/shard_map/ppermute | solution.py:804
  171.0 7.7 %collective-permute-start.36 = (bf16[64,1152]{1,0:T(8,128)(2,1)S(1)}, bf16[64,1152]{1,0:T(8,128)(2,1)S(1)}, u32[]{:S(2)}, u32[]{:S(2)}) collective-permute-start(bf16[64,1152]{1,0:T(8,128)(2,1)S(1)} %total_late.1.refs_2_.refs_0_), channel_id=1, source_target_pairs={{0,24},{8,16},{16,8},{24,0},{1,25},{9,17},{17,9},{25,1},{2,26},{10... | collective-permute-start | bytes 442376 | tf_op jit(solution)/shard_map/ppermute | solution.py:804
  172.5 7.8 %collective-permute-start.35 = (bf16[64,1152]{1,0:T(8,128)(2,1)S(1)}, bf16[64,1152]{1,0:T(8,128)(2,1)S(1)}, u32[]{:S(2)}, u32[]{:S(2)}) collective-permute-start(bf16[64,1152]{1,0:T(8,128)(2,1)S(1)} %total_late.1.refs_2_.refs_0_), channel_id=1, source_target_pairs={{0,16},{8,24},{16,0},{24,8},{1,17},{9,25},{17,1},{25,9},{2,18},{10... | collective-permute-start | bytes 442376 | tf_op jit(solution)/shard_map/ppermute | solution.py:804
  173.1 7.2 %collective-permute-start.34 = (bf16[64,1152]{1,0:T(8,128)(2,1)S(1)}, bf16[64,1152]{1,0:T(8,128)(2,1)S(1)}, u32[]{:S(2)}, u32[]{:S(2)}) collective-permute-start(bf16[64,1152]{1,0:T(8,128)(2,1)S(1)} %total_late.1.refs_2_.refs_0_), channel_id=1, source_target_pairs={{0,8},{8,0},{16,24},{24,16},{1,9},{9,1},{17,25},{25,17},{2,10},{10... | collective-permute-start | bytes 442376 | tf_op jit(solution)/shard_map/ppermute | solution.py:804
  (49 other events, 327.0 us)
